TPU v7x, 1024 devices: a whole 4x8x16 slice. The times are simulated.
1024 devices in a mesh: ep: 64 (over y_lo, z), dp: 16 (over y_hi, x, core).
Axes of the slice: x: 4, y: 8 (y_hi: 2, y_lo: 4; y = y_hi * 4 + y_lo), z: 16, core: 2. Of those that a mesh axis runs over, the one named last changes fastest.
Arguments:
- tokens_first: bfloat16 [131072, 2048], P(('ep', 'dp')), may hold values from -6 to 6
- routes_first: int32 [131072, 1], P(('ep', 'dp')), may hold values from 0 to 63; in each aligned block of 128 rows (0 to 127, 128 to 255, ...) at most 4 rows name the same one
- gates_first: bfloat16 [131072, 1], P(('ep', 'dp')), may hold values from 0.099609375 to 0.5
- gate_up_weight: bfloat16 [64, 2048, 768], P('ep'), may hold values from -0.125 to 0.125
- down_weight: bfloat16 [64, 384, 2048], P('ep'), may hold values from -0.3125 to 0.3125
- saved_inputs: bfloat16 [64, 16, 256, 2048], P('ep', 'dp'), may hold values from -6 to 6
- upstream: bfloat16 [131072, 2048], P(('ep', 'dp')), may hold values from -0.3984375 to 0.3984375
- routes_second: int32 [131072, 1], P(('ep', 'dp')), may hold values from 0 to 63; in each aligned block of 128 rows (0 to 127, 128 to 255, ...) at most 4 rows name the same one
- gates_second: bfloat16 [131072, 1], P(('ep', 'dp')), may hold values from 0.099609375 to 0.5
Outputs:
- mixed_first: bfloat16 [131072, 2048], P(('ep', 'dp'))
- gate_grads: float32 [131072, 1], P(('ep', 'dp'))
- gate_up_grad: bfloat16 [64, 2048, 768], P('ep', 'dp')
- down_grad: bfloat16 [64, 384, 2048], P('ep', None, 'dp')
Inputs may be any that keep to these rules, and one draw needn't show every extreme that they name: `routes_first`: each row names 1 different experts; in the rows of one device no expert is named more than 4 times, a bound that some block reaches. `routes_second`: each row names 1 different experts; in the rows of one device no expert is named more than 4 times, a bound that some block reaches.
All inputs are finite; a program needn't handle non-finite values.
Results may differ from a plain program's by a relative error of at most 0.014.
Values may be sent and summed in bfloat16 or wider, within the bound.
No kernel may reach another device: no remote copies, remote signals or barrier semaphores. Data moves between devices by JAX's collectives and lax.ppermute only.
A program may use at most 64 MiB of HBM per device.

v0:
```python
import math

import jax
import jax.numpy as jnp
from jax import lax
from jax.sharding import PartitionSpec as P


def cut_along(x, dim, peers):
    before, after = (x.shape[:dim], x.shape[dim + 1 :])
    return jnp.moveaxis(x.reshape(*before, peers, -1, *after), dim, 0)


def cut_rows(length, count):
    unit = 8 if length >= 8 * count else 1
    return [length // unit * k // count * unit for k in range(1, count)]


def in_order(parts, dim):
    parts = jnp.moveaxis(parts, 0, dim)
    lengths = parts.shape
    return parts.reshape(*lengths[:dim], lengths[dim] * lengths[dim + 1], *lengths[dim + 2 :])


def cut_exchange(x, axis, pieces, split_dim, concat_dim):
    parts = cut_along(x, split_dim, lax.axis_size(axis))
    widest = max(range(1, max(2, parts.ndim - 1)), key=lambda d: parts.shape[d])
    outs = []
    for piece in jnp.split(parts, cut_rows(parts.shape[widest], pieces), axis=widest):
        if piece.size:
            outs.append(lax.all_to_all(piece, axis, split_axis=0, concat_axis=0, tiled=True))
    return in_order(jnp.concatenate(outs, axis=widest), concat_dim)


def in_one_piece(arrays, axis, split_dim, concat_dim, along):
    widths = [math.prod(a.shape[along:]) for a in arrays]
    both = jnp.concatenate(
        [a.reshape(*a.shape[:along], w) for a, w in zip(arrays, widths)], axis=along
    )
    whole = lax.all_to_all(both, axis, split_axis=split_dim, concat_axis=concat_dim, tiled=True)
    parts = jnp.split(whole, [sum(widths[:k]) for k in range(1, len(widths))], axis=along)
    return tuple((b.reshape(*whole.shape[:along], *a.shape[along:]) for a, b in zip(arrays, parts)))


def one_scatter(arrays, axis, dims):
    peers = lax.axis_size(axis)
    parts = [cut_along(a, dim, peers) for a, dim in zip(arrays, dims)]
    lines = jnp.concatenate([b.reshape(peers, -1) for b in parts], axis=1)
    span = max(16, -(-lines.shape[1] // 1024) * 8)
    lines = jnp.pad(lines, ((0, 0), (0, span * 128 - lines.shape[1]))).reshape(-1, 128)
    vector, at, outs = (lax.psum_scatter(lines, axis, tiled=True).reshape(-1), 0, [])
    for b in parts:
        part = b[0]
        outs.append(vector[at : at + part.size].reshape(part.shape))
        at += part.size
    return tuple(outs)


def slot_places(routing, experts, capacity):
    expert_ids = jnp.arange(experts, dtype=jnp.int32)
    onehot = (routing[:, :, None] == expert_ids).astype(jnp.int32)
    counts = jnp.sum(onehot, axis=1)
    before = jnp.cumsum(counts, axis=0) - counts
    slots = jnp.sum(onehot * before[:, None, :], axis=2)
    return routing * capacity + slots


def local(
    tokens_first,
    routes_first,
    gates_first,
    gate_up_weight,
    down_weight,
    saved_inputs,
    upstream,
    routes_second,
    gates_second,
):
    experts = lax.axis_size("ep")
    capacity = saved_inputs.shape[2] // experts
    places = experts * capacity
    model_width = tokens_first.shape[1]
    weight_gu = gate_up_weight[0]
    weight_down = down_weight[0]
    hidden_size = weight_down.shape[0]

    def expand(places_of):
        lookup = (places_of[:, :, None] == jnp.arange(places, dtype=jnp.int32)).astype(jnp.bfloat16)
        return (lookup, jnp.sum(lookup, axis=1))

    def dispatch(select, values):
        moved = lax.dot_general(
            select, values, (((0,), (0,)), ((), ())), preferred_element_type=jnp.float32
        )
        return moved.astype(jnp.bfloat16).reshape(experts, capacity, model_width)

    def project(inputs):
        return jnp.dot(inputs, weight_gu, preferred_element_type=jnp.float32)

    first_places = slot_places(routes_first, experts, capacity)
    first_lookup, first_select = expand(first_places)
    send_first = dispatch(first_select, tokens_first)
    second_places = slot_places(routes_second, experts, capacity)
    second_lookup, second_select = expand(second_places)
    send_grad = dispatch(second_select, upstream)
    send_gates = jnp.einsum(
        "tkp,tk->p",
        second_lookup.astype(jnp.float32),
        gates_second.astype(jnp.float32),
        precision=lax.Precision.HIGHEST,
    )
    send_gates = send_gates.astype(jnp.bfloat16).reshape(experts, capacity)
    received = lax.all_to_all(send_first, "ep", split_axis=0, concat_axis=0, tiled=True)
    sources = received.shape[0]
    items = received.shape[1]
    projected = project(received.reshape(sources * items, model_width))
    activated = (jax.nn.silu(projected[:, :hidden_size]) * projected[:, hidden_size:]).astype(
        jnp.bfloat16
    )
    outputs = jnp.dot(activated, weight_down, preferred_element_type=jnp.float32).astype(
        jnp.bfloat16
    )
    returned = cut_exchange(outputs.reshape(sources, items, model_width), "ep", 2, 0, 0)
    arrived_grad, arrived_gates = in_one_piece((send_grad, send_gates), "ep", 0, 0, 2)
    picked = returned.reshape(places, model_width)[first_places]
    mixed_first = jnp.sum(
        gates_first.astype(jnp.float32)[:, :, None] * picked.astype(jnp.float32), axis=1
    ).astype(jnp.bfloat16)
    saved_rows = saved_inputs[0, 0]
    projected_b = project(saved_rows)
    gate_part = projected_b[:, :hidden_size]
    up_part = projected_b[:, hidden_size:]
    squash = jax.nn.sigmoid(gate_part)
    swish = jax.nn.silu(gate_part)
    activated_b = (swish * up_part).astype(jnp.bfloat16)
    incoming = arrived_grad.reshape(places, model_width)
    gate_column = arrived_gates.reshape(places, 1).astype(jnp.float32)
    grad_hidden = lax.dot_general(
        incoming, weight_down, (((1,), (1,)), ((), ())), preferred_element_type=jnp.float32
    )
    slot_value = jnp.sum(grad_hidden * activated_b.astype(jnp.float32), axis=1)
    returned_value = lax.all_to_all(
        slot_value.reshape(experts, capacity), "ep", split_axis=0, concat_axis=0, tiled=True
    )
    gate_grads = returned_value.reshape(places)[second_places]
    grad_scaled = gate_column * grad_hidden
    grad_gate = grad_scaled * up_part * squash * (1.0 + gate_part * (1.0 - squash))
    grad_up = grad_scaled * swish
    grad_both = jnp.concatenate([grad_gate, grad_up], axis=1).astype(jnp.bfloat16)
    grad_rows = (gate_column * incoming.astype(jnp.float32)).astype(jnp.bfloat16)
    down_term = lax.dot_general(
        activated_b, grad_rows, (((0,), (0,)), ((), ())), preferred_element_type=jnp.float32
    )
    gate_up_term = lax.dot_general(
        saved_rows, grad_both, (((0,), (0,)), ((), ())), preferred_element_type=jnp.float32
    )
    gate_up_grad, down_grad = tuple(
        (
            part.astype(jnp.float32)
            for part in one_scatter(
                (gate_up_term[None].astype(jnp.bfloat16), down_term[None].astype(jnp.bfloat16)),
                "dp",
                (1, 2),
            )
        )
    )
    return (
        mixed_first,
        gate_grads,
        gate_up_grad.astype(jnp.bfloat16),
        down_grad.astype(jnp.bfloat16),
    )


def solution(mesh):
    return jax.shard_map(
        local,
        mesh=mesh,
        in_specs=(
            P(("ep", "dp"), None),
            P(("ep", "dp"), None),
            P(("ep", "dp"), None),
            P("ep", None, None),
            P("ep", None, None),
            P("ep", "dp", None, None),
            P(("ep", "dp"), None),
            P(("ep", "dp"), None),
            P(("ep", "dp"), None),
        ),
        out_specs=(
            P(("ep", "dp"), None),
            P(("ep", "dp"), None),
            P("ep", "dp", None),
            P("ep", None, "dp"),
        ),
        check_vma=False,
    )
```

profile of v0, /device:TPU:1, one launch (start us, length us, event | category | flops | bytes accessed | tf_op | source)
XLA Modules:
  0.0 294.8 jit_solution(4102644837034908801)
XLA Ops:
  7.2 0.0 copy-start
  7.2 0.0 copy-start.5
  7.2 3.5 %fusion.40 = s32[128]{0:T(128)S(1)} fusion(s32[128]{0:T(128)} %bitcast.76), kind=kOutput, calls=%fused_computation.73 | output fusion | flops 1097600 | bytes 1024 | tf_op jit(solution)/shard_map/jit(cumsum)/reduce_window_sum | solution.py:63
  10.7 0.7 fusion.33
  11.3 2.6 convolution_convert_fusion.2
  13.9 2.3 reshape.346
  16.2 0.0 copy-done.5
  16.2 0.2 fusion.21
  16.4 0.2 reshape_reshape.13
  16.7 0.0 copy-start.3
  16.7 2.8 pad_maximum_fusion.1
  19.5 23.6 %all-to-all-start.3 = ((bf16[64,4,2049]{2,1,0:T(4,128)(2,1)}), bf16[64,4,2049]{2,1,0:T(4,128)(2,1)}, u32[]{:S(2)}, u32[]{:S(2)}) async-start(bf16[64,4,2049]{2,1,0:T(4,128)(2,1)} %pad_maximum_fusion.1), calls=%async_computation.3 | async-start | bytes 2228224 | tf_op jit(solution)/shard_map/all_to_all | solution.py:40
  43.1 0.0 copy-done.3
  43.1 2.6 fusion.39
  45.8 2.6 convolution_convert_fusion.4
  48.4 2.2 reshape.344
  50.6 0.0 copy-done
  50.6 3.1 %fusion = f32[256,768]{1,0:T(8,128)} fusion(bf16[1,2048,768]{2,1,0:T(8,128)(2,1)S(1)} %copy-done, bf16[1,1,256,2048]{3,2,1,0:T(8,128)(2,1)} %param.14), kind=kOutput, calls=%fused_computation.4 | convolution fusion | flops 805306368 | bytes 4980736 | tf_op jit(solution)/shard_map/dot_general | solution.py:98
  53.7 42.2 %all-to-all-done.3 = bf16[64,4,2049]{2,1,0:T(4,128)(2,1)} async-done(((bf16[64,4,2049]{2,1,0:T(4,128)(2,1)}), bf16[64,4,2049]{2,1,0:T(4,128)(2,1)}, u32[]{:S(2)}, u32[]{:S(2)}) %all-to-all-start.3) | async-done | bytes 1049120 | tf_op jit(solution)/shard_map/all_to_all | solution.py:40
  95.9 11.1 %all-to-all-start = ((bf16[64,4,2048]{2,1,0:T(4,128)(2,1)}), bf16[64,4,2048]{2,1,0:T(4,128)(2,1)}, u32[]{:S(2)}, u32[]{:S(2)}) async-start(bf16[64,4,2048]{2,1,0:T(4,128)(2,1)} %reshape.344), calls=%async_computation | async-start | bytes 2097152 | tf_op jit(solution)/shard_map/all_to_all | solution.py:113
  107.0 0.0 reduce-scatter.2.cloned.1.call-start
  107.1 2.7 split.18
  109.7 2.2 reshape.348
  111.9 1.0 convert_reduce_fusion
  112.9 0.1 reshape.357
  113.0 0.0 copy-start.2
  113.0 2.9 multiply_convert_fusion.3
  115.9 0.0 copy-done.2
  115.9 2.7 fusion.4
  118.6 4.6 %copy.32 = bf16[2048,768]{1,0:T(8,128)(2,1)} copy(bf16[2048,768]{0,1:T(8,128)(2,1)} %fusion.4) | data formatting | bytes 6291456 | tf_op jit(solution)/shard_map/convert_element_type | solution.py:161
  123.3 4.0 %reshape_transpose_reshape.3 = bf16[16,98304]{1,0:T(8,128)(2,1)} reshape(bf16[2048,768]{1,0:T(8,128)(2,1)} %copy.32) | data formatting | bytes 6291456 | tf_op jit(solution)/shard_map/reshape;transpose;reshape | solution.py:48
  127.3 1.9 fusion.8
  129.2 0.4 copy.34
  129.6 0.4 copy.33
  130.1 1.0 copy.37
  131.1 0.9 copy-done.1
  131.9 8.4 %pad_maximum_fusion = bf16[16,147456]{1,0:T(8,128)(2,1)} fusion(bf16[16,49152]{1,0:T(8,128)(2,1)S(1)} %bitcast.72, bf16[16,98304]{1,0:T(8,128)(2,1)S(1)} %copy-done.1), kind=kLoop, calls=%fused_computation.2 | loop fusion | flops 9437184 | bytes 9437184 | tf_op jit(solution)/shard_map/concatenate | solution.py:48
  140.3 5.2 %reshape.352 = bf16[18432,128]{1,0:T(8,128)(2,1)} reshape(bf16[16,147456]{1,0:T(8,128)(2,1)} %pad_maximum_fusion) | data formatting | bytes 9437184 | tf_op jit(solution)/shard_map/reshape | solution.py:50
  145.5 0.0 reduce-scatter.2.cloned.1.call-update
  145.6 11.9 %all-to-all-done = bf16[64,4,2048]{2,1,0:T(4,128)(2,1)} async-done(((bf16[64,4,2048]{2,1,0:T(4,128)(2,1)}), bf16[64,4,2048]{2,1,0:T(4,128)(2,1)}, u32[]{:S(2)}, u32[]{:S(2)}) %all-to-all-start) | async-done | bytes 1048608 | tf_op jit(solution)/shard_map/all_to_all | solution.py:113
  157.4 2.2 reshape.345
  159.6 2.3 fusion.2
  161.9 1.7 convolution_convert_fusion.3
  163.7 2.3 reshape_reshape.10
  165.9 0.7 all_to_all.22
  166.7 10.5 %all-to-all-start.4 = ((f32[64,1,4]{2,1,0:T(1,128)}), f32[64,1,4]{2,1,0:T(1,128)S(1)}, u32[]{:S(2)}, u32[]{:S(2)}) async-start(f32[64,1,4]{2,1,0:T(1,128)} %bitcast.16), calls=%async_computation.4 | async-start | bytes 65536 | tf_op jit(solution)/shard_map/all_to_all | solution.py:142
  177.1 0.0 copy-start.6
  177.2 3.7 %fusion.38 = (bf16[64,1,2,2048]{3,2,1,0:T(2,128)(2,1)}, bf16[64,1,2,2048]{3,2,1,0:T(2,128)(2,1)}) fusion(bf16[64,1,4,2048]{3,2,1,0:T(4,128)(2,1)} %bitcast.75), kind=kLoop, calls=%fused_computation.71 | loop fusion | bytes 2097152 | tf_op jit(solution)/shard_map/split | solution.py:29
  180.9 9.8 %all-to-all-done.4 = f32[64,1,4]{2,1,0:T(1,128)S(1)} async-done(((f32[64,1,4]{2,1,0:T(1,128)}), f32[64,1,4]{2,1,0:T(1,128)S(1)}, u32[]{:S(2)}, u32[]{:S(2)}) %all-to-all-start.4) | async-done | bytes 1056 | tf_op jit(solution)/shard_map/all_to_all | solution.py:142
  190.6 34.3 %all_to_all.29 = bf16[64,1,2,2048]{3,2,1,0:T(2,128)(2,1)} all-to-all(bf16[64,1,2,2048]{3,2,1,0:T(2,128)(2,1)} %get-tuple-element.10), channel_id=1, replica_groups=mesh['ep'=64,'dp'=16] {'ep'}, dimensions={0} | all-to-all | bytes 1048576 | tf_op jit(solution)/shard_map/all_to_all | solution.py:31
  225.0 9.4 %all-to-all-start.2 = ((bf16[64,1,2,2048]{3,2,1,0:T(2,128)(2,1)}), bf16[64,1,2,2048]{3,2,1,0:T(2,128)(2,1)}, u32[]{:S(2)}, u32[]{:S(2)}) async-start(bf16[64,1,2,2048]{3,2,1,0:T(2,128)(2,1)} %get-tuple-element.11), calls=%async_computation.2 | async-start | bytes 1048576 | tf_op jit(solution)/shard_map/all_to_all | solution.py:31
  234.4 0.5 broadcast.194
  235.0 0.7 reduce.7
  235.7 0.1 reshape.349
  235.8 1.8 gather_fusion.1
  237.6 24.1 %all-to-all-done.2 = bf16[64,1,2,2048]{3,2,1,0:T(2,128)(2,1)} async-done(((bf16[64,1,2,2048]{3,2,1,0:T(2,128)(2,1)}), bf16[64,1,2,2048]{3,2,1,0:T(2,128)(2,1)}, u32[]{:S(2)}, u32[]{:S(2)}) %all-to-all-start.2) | async-done | bytes 524320 | tf_op jit(solution)/shard_map/all_to_all | solution.py:31
  261.7 3.3 %pad_maximum_fusion.2 = bf16[64,1,4,2048]{3,2,1,0:T(4,128)(2,1)} fusion(bf16[64,1,2,2048]{3,2,1,0:T(2,128)(2,1)} %all-to-all-done.2, bf16[64,1,2,2048]{3,2,1,0:T(2,128)(2,1)} %all_to_all.29), kind=kLoop, calls=%fused_computation.20 | loop fusion | flops 2097152 | bytes 2097152 | tf_op jit(solution)/shard_map/concatenate | solution.py:32
  265.0 2.2 reshape_reshape.11
  267.2 3.6 %gather_fusion = bf16[128,2048]{1,0:T(8,128)(2,1)} fusion(bf16[256,2048]{1,0:T(8,128)(2,1)} %reshape_reshape.11, s32[1024]{0:T(1024)S(1)} %pad_clamp_fusion.1), kind=kCustom, calls=%fused_computation | custom fusion | bytes 1049088 | tf_op jit(solution)/shard_map/gather | solution.py:125
  270.8 2.0 fusion.11
  272.8 11.8 %reduce-scatter.2.cloned.1.call-done = bf16[1152,128]{1,0:T(8,128)(2,1)} async-done(((bf16[18432,128]{1,0:T(8,128)(2,1)}), bf16[1152,128]{1,0:T(8,128)(2,1)}) %reduce-scatter.2.cloned.1.call-update) | async-done | bytes 294928 | tf_op jit(solution)/shard_map/reduce_scatter | solution.py:51
  284.6 0.9 slice.34
  285.6 0.9 reshape.353
  286.4 1.5 slice_bitcast_fusion
  (9 shorter events, 0.0 us)
Async XLA Ops:
  7.2 43.4 %copy-start = (bf16[1,2048,768]{2,1,0:T(8,128)(2,1)S(1)}, bf16[1,2048,768]{2,1,0:T(8,128)(2,1)}, u32[]{:S(2)}) copy-start(bf16[1,2048,768]{2,1,0:T(8,128)(2,1)} %param.12) | copy-start | bytes 9437188
  7.2 9.0 %copy-start.5 = (bf16[128,1]{0,1:T(2,128)(2,1)S(1)}, bf16[128,1]{0,1:T(2,128)(2,1)}, u32[]{:S(2)}) copy-start(bf16[128,1]{0,1:T(2,128)(2,1)} %param.17) | copy-start | bytes 772
  16.7 26.5 %copy-start.3 = (s32[128,1]{0,1:T(1,128)S(1)}, s32[128,1]{0,1:T(1,128)}, u32[]{:S(2)}) copy-start(s32[128,1]{0,1:T(1,128)} %param.10) | copy-start | bytes 1540
  19.5 76.4 %all-to-all-start.3 = ((bf16[64,4,2049]{2,1,0:T(4,128)(2,1)}), bf16[64,4,2049]{2,1,0:T(4,128)(2,1)}, u32[]{:S(2)}, u32[]{:S(2)}) async-start(bf16[64,4,2049]{2,1,0:T(4,128)(2,1)} %pad_maximum_fusion.1), calls=%async_computation.3 | async-start | bytes 2228224 | tf_op jit(solution)/shard_map/all_to_all | solution.py:40
  95.9 61.5 %all-to-all-start = ((bf16[64,4,2048]{2,1,0:T(4,128)(2,1)}), bf16[64,4,2048]{2,1,0:T(4,128)(2,1)}, u32[]{:S(2)}, u32[]{:S(2)}) async-start(bf16[64,4,2048]{2,1,0:T(4,128)(2,1)} %reshape.344), calls=%async_computation | async-start | bytes 2097152 | tf_op jit(solution)/shard_map/all_to_all | solution.py:113
  107.0 177.6 %reduce-scatter.2.cloned.1.call-start = ((), (), s32[]{:S(2)}) async-start(), calls=%async_computation.6 | async-start | bytes 5013504 | tf_op jit(solution)/shard_map/reduce_scatter | solution.py:51
  113.0 2.9 copy-start.2
  130.0 1.9 copy-start.1
  159.6 2.3 copy-start.4
  166.7 24.0 %all-to-all-start.4 = ((f32[64,1,4]{2,1,0:T(1,128)}), f32[64,1,4]{2,1,0:T(1,128)S(1)}, u32[]{:S(2)}, u32[]{:S(2)}) async-start(f32[64,1,4]{2,1,0:T(1,128)} %bitcast.16), calls=%async_computation.4 | async-start | bytes 65536 | tf_op jit(solution)/shard_map/all_to_all | solution.py:142
  177.1 57.3 %copy-start.6 = (bf16[128,1]{0,1:T(2,128)(2,1)S(1)}, bf16[128,1]{0,1:T(2,128)(2,1)}, u32[]{:S(2)}) copy-start(bf16[128,1]{0,1:T(2,128)(2,1)} %param.11) | copy-start | bytes 772
  225.0 36.7 %all-to-all-start.2 = ((bf16[64,1,2,2048]{3,2,1,0:T(2,128)(2,1)}), bf16[64,1,2,2048]{3,2,1,0:T(2,128)(2,1)}, u32[]{:S(2)}, u32[]{:S(2)}) async-start(bf16[64,1,2,2048]{3,2,1,0:T(2,128)(2,1)} %get-tuple-element.11), calls=%async_computation.2 | async-start | bytes 1048576 | tf_op jit(solution)/shard_map/all_to_all | solution.py:31
Sparse Core Ops, SparseCore 0:
  145.7 138.9 reduce-scatter.1
where the time goes:
time: 296 us; the launch traced here: 295 us
  waiting for transfers between devices  99.8 us (34%)
  starting transfers between devices  54.6 us (18%)
  local copies, waits for them, and re-layouts  46.7 us (16%)
  blocking collectives  34.3 us (12%)
  other arithmetic  25 us (8%)
  matrix products  20.1 us (7%)
  between operations  14.3 us (5%)
    all_to_all x1, waiting for transfers between devices, in_one_piece(): lax.all_to_all(both, axis, split_axis=split_dim, concat_axis=concat_dim,...  42.2 us
    all_to_all x1, blocking collectives, cut_exchange(): lax.all_to_all(piece, axis, split_axis=0, concat_axis=0, tiled=True)  34.3 us
    all_to_all x1, waiting for transfers between devices, cut_exchange(): lax.all_to_all(piece, axis, split_axis=0, concat_axis=0, tiled=True)  24.1 us
    all_to_all x1, starting transfers between devices, in_one_piece(): lax.all_to_all(both, axis, split_axis=split_dim, concat_axis=concat_dim,...  23.6 us
    all_to_all x1, waiting for transfers between devices, local(): lax.all_to_all(send_first, 'ep', split_axis=0, concat_axis=0, tiled=True)  11.9 us
    reduce_scatter x1, waiting for transfers between devices, one_scatter(): lax.psum_scatter(lines, axis, tiled=True).reshape(-1)  11.8 us
    all_to_all x1, starting transfers between devices, local(): lax.all_to_all(send_first, 'ep', split_axis=0, concat_axis=0, tiled=True)  11.1 us
    all_to_all x1, starting transfers between devices, local(): lax.all_to_all(slot_value.reshape(experts, capacity), 'ep', split_axis=0,...  10.5 us
  transfers between devices with their start and end apart: 5, of which 5 were waited for; matrix products, arithmetic and copies ran while one was open for 25% of the time, Pallas kernels for 0%

commit v1 on v0

v1 whole, which is shorter than its diff:
```python
import functools

import jax
import jax.numpy as jnp
from jax import lax
from jax.experimental import pallas as pl
from jax.experimental.pallas import tpu as pltpu
from jax.sharding import Mesh, PartitionSpec as P

BF16 = jnp.bfloat16
F32 = jnp.float32
I32 = jnp.int32
EP = ("yl", "z")
ALL = ("yl", "z", "yh", "x", "core")
CHUNK = 16


def iota(shape, dim):
    return lax.broadcasted_iota(I32, shape, dim)


def dot(a, b, ca=1, cb=0):
    return lax.dot_general(a, b, (((ca,), (cb,)), ((), ())), preferred_element_type=F32)


def slots_of(routes, experts):
    tokens = routes.shape[1]
    onehot = (iota((experts, tokens), 0) == routes).astype(F32)
    earlier = (iota((tokens, tokens), 0) < iota((tokens, tokens), 1)).astype(F32)
    before = dot(onehot.astype(BF16), earlier.astype(BF16))
    return onehot, jnp.sum(onehot * before, axis=0, keepdims=True).astype(I32)


def order_of(rows, cap, dim):
    j = iota((rows, rows), dim)
    pieces = CHUNK // cap
    per = rows // pieces
    return (j % CHUNK) // cap * per + j // CHUNK * cap + j % cap


def gather_order(rows, cap):
    return (iota((rows, rows), 0) == order_of(rows, cap, 1)).astype(F32).astype(BF16)


def scatter_order(rows, cap):
    return (iota((rows, rows), 1) == order_of(rows, cap, 0)).astype(F32).astype(BF16)


GROUP = 256


def from_chunks(chunks_ref, rows_ref, cap):
    width = chunks_ref.shape[1]
    pieces = CHUNK // cap
    per = GROUP // pieces
    order = gather_order(GROUP, cap)
    for g in range(chunks_ref.shape[0] // GROUP):
        part = dot(order, chunks_ref[g * GROUP : (g + 1) * GROUP, :]).astype(BF16)
        for q in range(pieces):
            rows_ref[g * per : (g + 1) * per, q * width : (q + 1) * width] = part[
                q * per : (q + 1) * per
            ]


def to_chunks(rows_ref, chunks_ref, cap):
    width = chunks_ref.shape[1]
    pieces = CHUNK // cap
    per = GROUP // pieces
    order = scatter_order(GROUP, cap)
    for g in range(chunks_ref.shape[0] // GROUP):
        part = jnp.concatenate(
            [
                rows_ref[g * per : (g + 1) * per, q * width : (q + 1) * width]
                for q in range(pieces)
            ],
            axis=0,
        )
        chunks_ref[g * GROUP : (g + 1) * GROUP, :] = dot(order, part).astype(BF16)


def send_rows(experts, cap, routes, weights, tokens_ref, chunks_ref):
    tokens = routes.shape[1]
    width = chunks_ref.shape[1]
    _, slots = slots_of(routes, experts)
    base = routes * CHUNK + slots
    for g in range(chunks_ref.shape[0] // GROUP):
        row = iota((GROUP, tokens), 0) + g * GROUP
        total = None
        for q in range(CHUNK // cap):
            select = jnp.where(row == base + q * cap, weights, 0.0).astype(BF16)
            term = dot(select, tokens_ref[:, q * width : (q + 1) * width])
            total = term if total is None else total + term
        chunks_ref[g * GROUP : (g + 1) * GROUP, :] = total.astype(BF16)
    return slots


def dispatch_second_kernel(experts, cap, routes_ref, gates_ref, tokens_ref, chunks_ref):
    send_rows(
        experts, cap, routes_ref[...], gates_ref[...].astype(F32), tokens_ref, chunks_ref
    )


def dispatch_first_kernel(
    experts, cap, routes_ref, gates_ref, tokens_ref, chunks_ref, mix_ref
):
    routes = routes_ref[...]
    slots = send_rows(
        experts, cap, routes, jnp.ones(routes.shape, F32), tokens_ref, chunks_ref
    )
    places = experts * cap
    hit = iota((places, routes.shape[1]), 0) == routes * cap + slots
    mix_ref[...] = jnp.where(hit, gates_ref[...].astype(F32), 0.0).T.astype(BF16)


def saved_kernel(x_ref, gu_ref, act_ref, gate_ref, up_ref):
    hid = act_ref.shape[1]
    both = dot(x_ref[...], gu_ref[...])
    gate, up = both[:, :hid], both[:, hid:]
    squash = jax.nn.sigmoid(gate)
    swish = gate * squash
    act_ref[...] = (swish * up).astype(BF16)
    gate_ref[...] = up * squash * (1.0 + gate * (1.0 - squash))
    up_ref[...] = swish


def backward_kernel(
    cap,
    at_ref,
    chunks_ref,
    down_ref,
    x_ref,
    act_ref,
    gate_ref,
    up_ref,
    keep_ref,
    send_ref,
    value_ref,
    rows_ref,
    both_ref,
):
    hid = act_ref.shape[1]
    block = keep_ref.shape[1]
    from_chunks(chunks_ref, rows_ref, cap)
    scaled = dot(rows_ref[...], down_ref[...], 1, 1)
    product = scaled * act_ref[...].astype(F32)
    folded = product[:, :128]
    for k in range(1, hid // 128):
        folded = folded + product[:, k * 128 : (k + 1) * 128]
    value_ref[...] = jnp.sum(folded.T, axis=0, keepdims=True)
    both_ref[:, :hid] = (scaled * gate_ref[...]).astype(BF16)
    both_ref[:, hid:] = (scaled * up_ref[...]).astype(BF16)
    y, x, core = at_ref[0], at_ref[1], at_ref[2]
    n_x = keep_ref.shape[0] // 2
    for out_ref, other in ((send_ref, 1), (keep_ref, 0)):
        for n in range(2 * n_x):
            to = ((y + n % 2) % 2 * n_x + (x + n // 2) % n_x) * 2 + (core + other) % 2
            columns = pl.ds(pl.multiple_of(to * block, block), block)
            out_ref[n, :, : 2 * hid] = dot(x_ref[:, columns], both_ref[...], 0, 0).astype(BF16)
            out_ref[n, :, 2 * hid :] = dot(rows_ref[:, columns], act_ref[...], 0, 0).astype(BF16)


def forward_kernel(cap, chunks_ref, gu_ref, down_ref, out_ref, rows_ref):
    hid = down_ref.shape[0]
    from_chunks(chunks_ref, rows_ref, cap)
    both = dot(rows_ref[...], gu_ref[...])
    act = (jax.nn.silu(both[:, :hid]) * both[:, hid:]).astype(BF16)
    rows_ref[...] = dot(act, down_ref[...]).astype(BF16)
    to_chunks(rows_ref, out_ref, cap)


def combine_kernel(cap, chunks_ref, mix_ref, out_ref, rows_ref):
    from_chunks(chunks_ref, rows_ref, cap)
    out_ref[...] = dot(mix_ref[...], rows_ref[...]).astype(BF16)


def gate_grad_kernel(cap, at_ref, values_ref, routes_ref, gates_ref, out_ref):
    values = values_ref[...]
    experts, places = values.shape
    onehot, slots = slots_of(routes_ref[...], experts)
    lane = iota((experts, places), 1)
    total = jnp.zeros(out_ref.shape, F32)
    for c in range(cap):
        mine = jnp.sum(
            jnp.where(lane == at_ref[0] * cap + c, values, 0.0), axis=1, keepdims=True
        )
        here = jnp.sum(onehot * mine, axis=0, keepdims=True)
        total = total + jnp.where(slots == c, here, 0.0)
    out_ref[...] = total / gates_ref[...].astype(F32)


def add_kernel(*refs):
    *terms, out_ref = refs
    total = terms[0][...].astype(F32)
    for term in terms[1:]:
        total = total + term[...].astype(F32)
    out_ref[...] = total.astype(BF16)


def finish_kernel(hid, a_ref, b_ref, gu_ref, down_ref):
    total = a_ref[...].astype(F32) + b_ref[...].astype(F32)
    gu_ref[...] = total[:, : 2 * hid].astype(BF16)
    down_ref[...] = total[:, 2 * hid :].T.astype(BF16)


VMEM = pl.BlockSpec(memory_space=pltpu.VMEM)
SMEM = pl.BlockSpec(memory_space=pltpu.SMEM)


def call(kernel, name, outs, args, scratch=(), scalars=0, flops=0, moved=0):
    shapes = [jax.ShapeDtypeStruct(*o) for o in outs]
    result = pl.pallas_call(
        kernel,
        name=name,
        out_shape=shapes,
        in_specs=[SMEM] * scalars + [VMEM] * (len(args) - scalars),
        out_specs=[VMEM] * len(outs),
        scratch_shapes=[pltpu.VMEM(*s) for s in scratch],
        compiler_params=pltpu.CompilerParams(vmem_limit_bytes=40 * 2**20),
        cost_estimate=pl.CostEstimate(flops=flops, bytes_accessed=moved, transcendentals=0),
    )(*args)
    return result[0] if len(outs) == 1 else result


def local(
    n_x,
    tokens_first,
    routes_first,
    gates_first,
    gate_up_weight,
    down_weight,
    saved_inputs,
    upstream,
    routes_second,
    gates_second,
):
    experts = lax.axis_size("yl") * lax.axis_size("z")
    places, model = saved_inputs.shape[2:]
    cap = places // experts
    tokens = tokens_first.shape[0]
    width = model * cap // CHUNK
    gu, down, x = gate_up_weight[0], down_weight[0], saved_inputs[0, 0]
    hid = down.shape[0]
    block = model // (4 * n_x)
    MB = 2**20

    def row(a):
        return a.reshape(1, tokens)

    def exchange(chunks):
        chunks = chunks.reshape(experts, CHUNK, width)
        moved = lax.all_to_all(chunks, EP, split_axis=0, concat_axis=0, tiled=True)
        return moved.reshape(experts * CHUNK, width)

    chunk_shape = ((experts * CHUNK, width), BF16)
    row_shape = ((places, model), BF16)
    here = jnp.stack(
        [lax.axis_index("yh"), lax.axis_index("x"), lax.axis_index("core")]
    ).astype(I32)
    home = lax.axis_index(EP).astype(I32).reshape(1)

    send_second = call(
        functools.partial(dispatch_second_kernel, experts, cap),
        "dispatch_second",
        [chunk_shape],
        (row(routes_second), row(gates_second), upstream),
        flops=2**29,
        moved=2 * MB,
    )
    got_second = exchange(send_second)
    send_first, mix = call(
        functools.partial(dispatch_first_kernel, experts, cap),
        "dispatch_first",
        [chunk_shape, ((tokens, places), BF16)],
        (row(routes_first), row(gates_first), tokens_first),
        flops=2**29,
        moved=2 * MB,
    )
    act, by_gate, by_up = call(
        saved_kernel,
        "saved",
        [((places, hid), BF16), ((places, hid), F32), ((places, hid), F32)],
        (x, gu),
        flops=2**30,
        moved=6 * MB,
    )
    got_first = exchange(send_first)

    half = ((2 * n_x, block, 3 * hid), BF16)
    keep, send, value = call(
        functools.partial(backward_kernel, cap),
        "backward",
        [half, half, ((1, places), F32)],
        (here, got_second, down, x, act, by_gate, by_up),
        scratch=(row_shape, ((places, 2 * hid), BF16)),
        scalars=1,
        flops=2**31,
        moved=12 * MB,
    )
    values = lax.all_gather(value.reshape(places), EP)
    other = lax.ppermute(send, "core", [(0, 1), (1, 0)])
    pair = ((2, block, 3 * hid), BF16)

    def add(*terms):
        return call(add_kernel, "add", [(terms[0].shape, BF16)], terms, moved=len(terms) * MB)

    def summed(k):
        return add(keep[2 * k : 2 * k + 2], other[2 * k : 2 * k + 2])

    terms = [summed(0)]
    for k in range(1, n_x):
        terms.append(
            lax.ppermute(summed(k), "x", [(i, (i + k) % n_x) for i in range(n_x)])
        )
    quarter = add(*terms)
    far = lax.ppermute(quarter[1], "yh", [(0, 1), (1, 0)])
    gate_up_grad, down_grad = call(
        functools.partial(finish_kernel, hid),
        "finish",
        [((block, 2 * hid), BF16), ((hid, block), BF16)],
        (quarter[0], far),
        moved=MB,
    )
    gate_grads = call(
        functools.partial(gate_grad_kernel, cap),
        "gate_grad",
        [((1, tokens), F32)],
        (home, values, row(routes_second), row(gates_second)),
        scalars=1,
        moved=MB // 8,
    )

    send_back = call(
        functools.partial(forward_kernel, cap),
        "forward",
        [chunk_shape],
        (got_first, gu, down),
        scratch=(row_shape,),
        flops=2**31,
        moved=7 * MB,
    )
    got_back = exchange(send_back)
    mixed_first = call(
        functools.partial(combine_kernel, cap),
        "combine",
        [((tokens, model), BF16)],
        (got_back, mix),
        scratch=(row_shape,),
        flops=2**29,
        moved=2 * MB,
    )
    return (
        mixed_first,
        gate_grads.reshape(tokens, 1),
        gate_up_grad[None],
        down_grad[None],
    )


def solution(mesh):
    n_ep, n_dp = mesh.devices.shape
    lows = 4
    n_x = n_dp // 4
    fine = Mesh(mesh.devices.reshape(lows, n_ep // lows, 2, n_x, 2), ALL)
    tokens = P(ALL, None)
    return jax.shard_map(
        functools.partial(local, n_x),
        mesh=fine,
        in_specs=(
            tokens,
            tokens,
            tokens,
            P(EP, None, None),
            P(EP, None, None),
            P(EP, ("yh", "x", "core"), None, None),
            tokens,
            tokens,
            tokens,
        ),
        out_specs=(
            tokens,
            tokens,
            P(EP, ("yh", "x", "core"), None),
            P(EP, None, ("yh", "x", "core")),
        ),
        check_vma=False,
    )
```

time: 296 us -> 353 us (1.19)
  the two profiles are of different devices: /device:TPU:1 before, /device:TPU:2 now
where the time goes in v1:
time: 353 us
  blocking collectives  151 us (43%)
  waiting for transfers between devices  115 us (33%)
  starting transfers between devices  55 us (16%)
  Pallas kernels  17.2 us (5%)
  local copies, waits for them, and re-layouts  14 us (4%)
    all_gather x1, blocking collectives, local(): values = lax.all_gather(value.reshape(places), EP)  151 us
    all_to_all x3, waiting for transfers between devices, exchange(): moved = lax.all_to_all(chunks, EP, split_axis=0, concat_axis=0, tiled=True)  92.6 us
    all_to_all x3, starting transfers between devices, exchange(): moved = lax.all_to_all(chunks, EP, split_axis=0, concat_axis=0, tiled=True)  37.6 us
    ppermute x3, waiting for transfers between devices, local(): lax.ppermute(summed(k), 'x', [(i, (i + k) % n_x) for i in range(n_x)])  22.1 us
    pallas_call x13, Pallas kernels, call(): pl.pallas_call(kernel, name=name, out_shape=shapes, in_specs=[SMEM] * sca...  17.2 us
    ppermute x3, starting transfers between devices, local(): lax.ppermute(summed(k), 'x', [(i, (i + k) % n_x) for i in range(n_x)])  10.5 us
    unnamed x33, local copies, waits for them, and re-layouts  10.4 us
  transfers between devices with their start and end apart: 8, of which 5 were waited for; matrix products, arithmetic and copies ran while one was open for 1% of the time, Pallas kernels for 4%

profile of v1, /device:TPU:2, one launch (start us, length us, event | category | flops | bytes accessed | tf_op | source)
XLA Modules:
  0.0 352.5 jit_solution(17251194128913378112)
XLA Ops:
  0.6 0.0 copy-start.14
  0.6 0.0 copy-start.15
  0.7 0.0 copy-start.6
  0.7 0.7 copy-done.6
  1.3 0.0 copy-start.8
  1.3 0.7 copy-done.8
  2.0 0.0 copy-start.12
  2.0 1.0 copy-done.12
  3.0 2.4 dispatch_second.1
  5.4 23.1 %all-to-all-start.2 = ((bf16[64,16,512]{2,1,0:T(8,128)(2,1)}), bf16[64,16,512]{2,1,0:T(8,128)(2,1)}, u32[]{:S(2)}, u32[]{:S(2)}) async-start(bf16[64,16,512]{2,1,0:T(8,128)(2,1)} %bitcast.14), calls=%async_computation.2 | async-start | bytes 2097152 | tf_op jit(solution)/shard_map/all_to_all | solution.py:251
  28.5 0.0 copy-start
  28.5 0.0 copy-done.14
  28.5 0.0 copy-done.15
  28.5 0.0 copy-start.13
  28.5 1.2 copy-done.13
  29.7 1.4 dispatch_first.1
  31.1 0.0 copy-start.3
  31.1 1.0 copy-done.3
  32.2 50.0 %all-to-all-done.2 = bf16[64,16,512]{2,1,0:T(8,128)(2,1)} async-done(((bf16[64,16,512]{2,1,0:T(8,128)(2,1)}), bf16[64,16,512]{2,1,0:T(8,128)(2,1)}, u32[]{:S(2)}, u32[]{:S(2)}) %all-to-all-start.2) | async-done | bytes 1048608 | tf_op jit(solution)/shard_map/all_to_all | solution.py:251
  82.2 7.5 %all-to-all-start = ((bf16[64,16,512]{2,1,0:T(8,128)(2,1)}), bf16[64,16,512]{2,1,0:T(8,128)(2,1)}, u32[]{:S(2)}, u32[]{:S(2)}) async-start(bf16[64,16,512]{2,1,0:T(8,128)(2,1)} %bitcast.32), calls=%async_computation | async-start | bytes 2097152 | tf_op jit(solution)/shard_map/all_to_all | solution.py:251
  89.6 0.0 copy-done
  89.6 0.0 copy-start.4
  89.7 1.2 copy-done.4
  90.9 0.0 copy-start.5
  90.9 0.0 copy-start.10
  90.9 1.0 saved.1
  91.9 0.1 pad_add_fusion.at_ref
  92.0 0.1 copy-done.5
  92.1 0.5 copy-done.10
  92.6 4.6 %backward.1 = (bf16[8,128,1152]{2,1,0:T(8,128)(2,1)S(1)}, bf16[8,128,1152]{2,1,0:T(8,128)(2,1)}, f32[1,256]{1,0:T(1,128)S(1)}) custom-call(s32[3]{0:T(128)S(1)} %pad_add_fusion.at_ref, bf16[1024,512]{1,0:T(8,128)(2,1)} %bitcast.15.chunks_ref, bf16[384,2048]{1,0:T(8,128)(2,1)S(1)} %bitcast.41, bf16[256,2048]{1,0:T(8,128)(2,1)S(1)} %bitcast.34, ...), custom_call_target="tpu_custom_call" | custom-call | flops 2147483648 | bytes 12582912 | tf_op jit(solution)/shard_map/backward/pallas_call | solution.py:211
  97.2 0.0 copy-start.1
  97.2 1.5 copy-done.1
  98.7 1.9 collective-permute-start
  100.6 42.6 %all-to-all-done = bf16[64,16,512]{2,1,0:T(8,128)(2,1)} async-done(((bf16[64,16,512]{2,1,0:T(8,128)(2,1)}), bf16[64,16,512]{2,1,0:T(8,128)(2,1)}, u32[]{:S(2)}, u32[]{:S(2)}) %all-to-all-start) | async-done | bytes 1048608 | tf_op jit(solution)/shard_map/all_to_all | solution.py:251
  143.2 1.4 copy-done.11
  144.6 4.0 %forward.1 = bf16[1024,512]{1,0:T(8,128)(2,1)S(1)} custom-call(bf16[1024,512]{1,0:T(8,128)(2,1)} %bitcast.3.chunks_ref, bf16[2048,768]{1,0:T(8,128)(2,1)S(1)} %bitcast.29, bf16[384,2048]{1,0:T(8,128)(2,1)S(1)} %bitcast.42), custom_call_target="tpu_custom_call" | custom-call | flops 2147483648 | bytes 7340032 | tf_op jit(solution)/shard_map/forward/pallas_call | solution.py:211
  148.6 0.0 copy-start.2
  148.6 1.0 copy-done.2
  149.7 7.1 %all-to-all-start.1 = ((bf16[64,16,512]{2,1,0:T(8,128)(2,1)}), bf16[64,16,512]{2,1,0:T(8,128)(2,1)S(1)}, u32[]{:S(2)}, u32[]{:S(2)}) async-start(bf16[64,16,512]{2,1,0:T(8,128)(2,1)} %bitcast.31), calls=%async_computation.1 | async-start | bytes 2097152 | tf_op jit(solution)/shard_map/all_to_all | solution.py:251
  156.8 1.8 fusion.1
  158.6 0.0 collective-permute-done
  158.6 1.8 fusion
  160.4 0.1 add.16
  160.5 2.4 collective-permute-start.3
  163.0 0.1 add.15
  163.1 4.3 %collective-permute-start.2 = (bf16[2,128,1152]{2,1,0:T(8,128)(2,1)S(1)}, bf16[2,128,1152]{2,1,0:T(8,128)(2,1)S(1)}, u32[]{:S(2)}, u32[]{:S(2)}) collective-permute-start(bf16[2,128,1152]{2,1,0:T(8,128)(2,1)S(1)} %add.15), channel_id=1, source_target_pairs={{0,4},{2,6},{4,0},{6,2},{1,5},{3,7},{5,1},{7,3},{8,12},{10,14},{12... | collective-permute-start | bytes 1769480 | tf_op jit(solution)/shard_map/ppermute | solution.py:312
  167.5 0.1 add.14
  167.6 3.7 %collective-permute-start.1 = (bf16[2,128,1152]{2,1,0:T(8,128)(2,1)S(1)}, bf16[2,128,1152]{2,1,0:T(8,128)(2,1)S(1)}, u32[]{:S(2)}, u32[]{:S(2)}) collective-permute-start(bf16[2,128,1152]{2,1,0:T(8,128)(2,1)S(1)} %add.14), channel_id=1, source_target_pairs={{0,2},{2,4},{4,6},{6,0},{1,3},{3,5},{5,7},{7,1},{8,10},{10,12},{12... | collective-permute-start | bytes 1769480 | tf_op jit(solution)/shard_map/ppermute | solution.py:312
  171.3 0.1 add.13.refs_0_
  171.5 0.0 copy-start.7
  171.5 0.0 copy-start.9
  171.5 6.3 %collective-permute-done.3.refs_3_ = bf16[2,128,1152]{2,1,0:T(8,128)(2,1)S(1)} collective-permute-done((bf16[2,128,1152]{2,1,0:T(8,128)(2,1)S(1)}, bf16[2,128,1152]{2,1,0:T(8,128)(2,1)S(1)}, u32[]{:S(2)}, u32[]{:S(2)}) %collective-permute-start.3) | collective-permute-done | bytes 589856 | tf_op jit(solution)/shard_map/ppermute | solution.py:312
  177.7 12.8 %collective-permute-done.2.refs_2_ = bf16[2,128,1152]{2,1,0:T(8,128)(2,1)S(1)} collective-permute-done((bf16[2,128,1152]{2,1,0:T(8,128)(2,1)S(1)}, bf16[2,128,1152]{2,1,0:T(8,128)(2,1)S(1)}, u32[]{:S(2)}, u32[]{:S(2)}) %collective-permute-start.2) | collective-permute-done | bytes 589856 | tf_op jit(solution)/shard_map/ppermute | solution.py:312
  190.6 3.0 collective-permute-done.1.refs_1_
  193.5 0.3 add.17
  193.9 5.0 %collective-permute-start.4 = (bf16[128,1152]{1,0:T(8,128)(2,1)S(1)}, bf16[128,1152]{1,0:T(8,128)(2,1)S(1)}, u32[]{:S(2)}, u32[]{:S(2)}) collective-permute-start(bf16[128,1152]{1,0:T(8,128)(2,1)S(1)} %get-tuple-element.32), channel_id=1, source_target_pairs={{0,8},{8,0},{1,9},{9,1},{2,10},{10,2},{3,11},{11,3},{4,12},{12,4},... | collective-permute-start | bytes 884744 | tf_op jit(solution)/shard_map/ppermute | solution.py:315
  198.9 150.6 %all-gather = f32[64,1,256]{2,1,0:T(1,128)S(1)} all-gather(f32[1,1,256]{2,1,0:T(1,128)S(1)} %bitcast.36), channel_id=1, replica_groups=mesh['yl'=4,'z'=16,'yh'=2,'x'=4,'core'=2] {'yl','z'}, dimensions={0}, use_global_device_ids=true | all-gather | bytes 66560 | tf_op jit(solution)/shard_map/all_gather | solution.py:299
  349.5 0.0 copy-done.7
  349.5 0.0 copy-done.9
  349.6 0.7 gate_grad.1
  350.2 0.0 collective-permute-done.4.b_ref
  350.2 0.8 finish.1
  351.0 0.0 all-to-all-done.1
  351.0 1.5 combine.1
  (3 shorter events, 0.1 us)
Async XLA Ops:
  0.6 27.9 %copy-start.14 = (s32[128,1]{0,1:T(1,128)S(1)}, s32[128,1]{0,1:T(1,128)}, u32[]{:S(2)}) copy-start(s32[128,1]{0,1:T(1,128)} %param.10) | copy-start | bytes 1540
  0.6 27.9 %copy-start.15 = (bf16[128,1]{0,1:T(2,128)(2,1)S(1)}, bf16[128,1]{0,1:T(2,128)(2,1)}, u32[]{:S(2)}) copy-start(bf16[128,1]{0,1:T(2,128)(2,1)} %param.11) | copy-start | bytes 772
  0.7 0.7 copy-start.6
  1.3 0.7 copy-start.8
  2.0 1.0 copy-start.12
  5.4 76.8 %all-to-all-start.2 = ((bf16[64,16,512]{2,1,0:T(8,128)(2,1)}), bf16[64,16,512]{2,1,0:T(8,128)(2,1)}, u32[]{:S(2)}, u32[]{:S(2)}) async-start(bf16[64,16,512]{2,1,0:T(8,128)(2,1)} %bitcast.14), calls=%async_computation.2 | async-start | bytes 2097152 | tf_op jit(solution)/shard_map/all_to_all | solution.py:251
  28.5 61.1 %copy-start = (bf16[1,2048,768]{2,1,0:T(8,128)(2,1)S(1)}, bf16[1,2048,768]{2,1,0:T(8,128)(2,1)}, u32[]{:S(2)}) copy-start(bf16[1,2048,768]{2,1,0:T(8,128)(2,1)} %param.12) | copy-start | bytes 9437188
  28.5 1.2 copy-start.13
  31.1 1.0 copy-start.3
  82.2 61.1 %all-to-all-start = ((bf16[64,16,512]{2,1,0:T(8,128)(2,1)}), bf16[64,16,512]{2,1,0:T(8,128)(2,1)}, u32[]{:S(2)}, u32[]{:S(2)}) async-start(bf16[64,16,512]{2,1,0:T(8,128)(2,1)} %bitcast.32), calls=%async_computation | async-start | bytes 2097152 | tf_op jit(solution)/shard_map/all_to_all | solution.py:251
  89.6 1.2 copy-start.4
  90.9 1.2 copy-start.5
  90.9 1.7 copy-start.10
  97.2 1.5 copy-start.1
  98.7 59.9 %collective-permute-start = (bf16[8,128,1152]{2,1,0:T(8,128)(2,1)}, bf16[8,128,1152]{2,1,0:T(8,128)(2,1)}, u32[]{:S(2)}, u32[]{:S(2)}) collective-permute-start(bf16[8,128,1152]{2,1,0:T(8,128)(2,1)} %get-tuple-element.21), channel_id=1, source_target_pairs={{0,1},{1,0},{2,3},{3,2},{4,5},{5,4},{6,7},{7,6},{8,9},{9,8},{10,11... | collective-permute-start | bytes 7077896 | tf_op jit(solution)/shard_map/ppermute | solution.py:300
  143.2 1.4 copy-start.11
  148.6 1.0 copy-start.2
  149.7 201.4 %all-to-all-start.1 = ((bf16[64,16,512]{2,1,0:T(8,128)(2,1)}), bf16[64,16,512]{2,1,0:T(8,128)(2,1)S(1)}, u32[]{:S(2)}, u32[]{:S(2)}) async-start(bf16[64,16,512]{2,1,0:T(8,128)(2,1)} %bitcast.31), calls=%async_computation.1 | async-start | bytes 2097152 | tf_op jit(solution)/shard_map/all_to_all | solution.py:251
  160.5 17.2 %collective-permute-start.3 = (bf16[2,128,1152]{2,1,0:T(8,128)(2,1)S(1)}, bf16[2,128,1152]{2,1,0:T(8,128)(2,1)S(1)}, u32[]{:S(2)}, u32[]{:S(2)}) collective-permute-start(bf16[2,128,1152]{2,1,0:T(8,128)(2,1)S(1)} %add.16), channel_id=1, source_target_pairs={{0,6},{2,0},{4,2},{6,4},{1,7},{3,1},{5,3},{7,5},{8,14},{10,8},{12,... | collective-permute-start | bytes 1769480 | tf_op jit(solution)/shard_map/ppermute | solution.py:312
  163.1 27.5 %collective-permute-start.2 = (bf16[2,128,1152]{2,1,0:T(8,128)(2,1)S(1)}, bf16[2,128,1152]{2,1,0:T(8,128)(2,1)S(1)}, u32[]{:S(2)}, u32[]{:S(2)}) collective-permute-start(bf16[2,128,1152]{2,1,0:T(8,128)(2,1)S(1)} %add.15), channel_id=1, source_target_pairs={{0,4},{2,6},{4,0},{6,2},{1,5},{3,7},{5,1},{7,3},{8,12},{10,14},{12... | collective-permute-start | bytes 1769480 | tf_op jit(solution)/shard_map/ppermute | solution.py:312
  167.6 25.9 %collective-permute-start.1 = (bf16[2,128,1152]{2,1,0:T(8,128)(2,1)S(1)}, bf16[2,128,1152]{2,1,0:T(8,128)(2,1)S(1)}, u32[]{:S(2)}, u32[]{:S(2)}) collective-permute-start(bf16[2,128,1152]{2,1,0:T(8,128)(2,1)S(1)} %add.14), channel_id=1, source_target_pairs={{0,2},{2,4},{4,6},{6,0},{1,3},{3,5},{5,7},{7,1},{8,10},{10,12},{12... | collective-permute-start | bytes 1769480 | tf_op jit(solution)/shard_map/ppermute | solution.py:312
  171.5 178.1 %copy-start.7 = (s32[128,1]{0,1:T(1,128)S(1)}, s32[128,1]{0,1:T(1,128)}, u32[]{:S(2)}) copy-start(s32[128,1]{0,1:T(1,128)} %param.16) | copy-start | bytes 1540
  171.5 178.1 %copy-start.9 = (bf16[128,1]{0,1:T(2,128)(2,1)S(1)}, bf16[128,1]{0,1:T(2,128)(2,1)}, u32[]{:S(2)}) copy-start(bf16[128,1]{0,1:T(2,128)(2,1)} %param.17) | copy-start | bytes 772
  193.9 156.4 %collective-permute-start.4 = (bf16[128,1152]{1,0:T(8,128)(2,1)S(1)}, bf16[128,1152]{1,0:T(8,128)(2,1)S(1)}, u32[]{:S(2)}, u32[]{:S(2)}) collective-permute-start(bf16[128,1152]{1,0:T(8,128)(2,1)S(1)} %get-tuple-element.32), channel_id=1, source_target_pairs={{0,8},{8,0},{1,9},{9,1},{2,10},{10,2},{3,11},{11,3},{4,12},{12,4},... | collective-permute-start | bytes 884744 | tf_op jit(solution)/shard_map/ppermute | solution.py:315

commit v2 on v1

--- a/solution.py
+++ b/solution.py
@@ -159,7 +159,8 @@
             out_ref[n, :, 2 * hid :] = dot(rows_ref[:, columns], act_ref[...], 0, 0).astype(BF16)
 
 
-def forward_kernel(cap, chunks_ref, gu_ref, down_ref, out_ref, rows_ref):
+def forward_kernel(cap, chunks_ref, gu_ref, down_ref, *refs):
+    out_ref, rows_ref = refs[-2:]
     hid = down_ref.shape[0]
     from_chunks(chunks_ref, rows_ref, cap)
     both = dot(rows_ref[...], gu_ref[...])
@@ -173,27 +174,43 @@
     out_ref[...] = dot(mix_ref[...], rows_ref[...]).astype(BF16)
 
 
-def gate_grad_kernel(cap, at_ref, values_ref, routes_ref, gates_ref, out_ref):
-    values = values_ref[...]
+def gate_grad_kernel(cap, digits, at_ref, *refs):
+    *value_refs, routes_ref, gates_ref, out_ref = refs
+    n_yl, n_high, n_low = digits
+    values = jnp.concatenate([ref[...] for ref in value_refs], axis=0)
     experts, places = values.shape
-    onehot, slots = slots_of(routes_ref[...], experts)
+    tokens = out_ref.shape[1]
+    routes = routes_ref[...]
+    _, slots = slots_of(routes, experts)
+    yl, high, low = at_ref[0], at_ref[1] // n_low, at_ref[1] % n_low
+    home = yl * (n_high * n_low) + at_ref[1]
+    far_yl = (yl + n_yl - routes // (n_high * n_low)) % n_yl
+    far_high = (high + n_high - routes // n_low % n_high) % n_high
+    far_low = (low + n_low - routes % n_low) % n_low
+    source = (far_low * n_high + far_high) * n_yl + far_yl
+    hit = (iota((experts, tokens), 0) == source).astype(F32)
     lane = iota((experts, places), 1)
     total = jnp.zeros(out_ref.shape, F32)
     for c in range(cap):
-        mine = jnp.sum(
-            jnp.where(lane == at_ref[0] * cap + c, values, 0.0), axis=1, keepdims=True
-        )
-        here = jnp.sum(onehot * mine, axis=0, keepdims=True)
+        mine = jnp.sum(jnp.where(lane == home * cap + c, values, 0.0), axis=1, keepdims=True)
+        here = jnp.sum(hit * mine, axis=0, keepdims=True)
         total = total + jnp.where(slots == c, here, 0.0)
     out_ref[...] = total / gates_ref[...].astype(F32)
 
 
-def add_kernel(*refs):
-    *terms, out_ref = refs
-    total = terms[0][...].astype(F32)
-    for term in terms[1:]:
-        total = total + term[...].astype(F32)
-    out_ref[...] = total.astype(BF16)
+def pair_kernel(a_ref, b_ref, *out_refs):
+    for k, out_ref in enumerate(out_refs):
+        total = a_ref[2 * k : 2 * k + 2].astype(F32) + b_ref[2 * k : 2 * k + 2].astype(F32)
+        out_ref[...] = total.astype(BF16)
+
+
+def sum_kernel(*refs):
+    *terms, near_ref, far_ref = refs
+    for k, out_ref in ((1, far_ref), (0, near_ref)):
+        total = terms[0][k].astype(F32)
+        for term in terms[1:]:
+            total = total + term[k].astype(F32)
+        out_ref[...] = total.astype(BF16)
 
 
 def finish_kernel(hid, a_ref, b_ref, gu_ref, down_ref):
@@ -204,20 +221,21 @@
 
 VMEM = pl.BlockSpec(memory_space=pltpu.VMEM)
 SMEM = pl.BlockSpec(memory_space=pltpu.SMEM)
-
-
-def call(kernel, name, outs, args, scratch=(), scalars=0, flops=0, moved=0):
+ANY = pl.BlockSpec(memory_space=pl.ANY)
+
+
+def call(kernel, name, outs, args, scratch=(), scalars=0, after=(), flops=0, moved=0):
     shapes = [jax.ShapeDtypeStruct(*o) for o in outs]
     result = pl.pallas_call(
         kernel,
         name=name,
         out_shape=shapes,
-        in_specs=[SMEM] * scalars + [VMEM] * (len(args) - scalars),
+        in_specs=[SMEM] * scalars + [VMEM] * (len(args) - scalars) + [ANY] * len(after),
         out_specs=[VMEM] * len(outs),
         scratch_shapes=[pltpu.VMEM(*s) for s in scratch],
-        compiler_params=pltpu.CompilerParams(vmem_limit_bytes=40 * 2**20),
+        compiler_params=pltpu.CompilerParams(vmem_limit_bytes=24 * 2**20),
         cost_estimate=pl.CostEstimate(flops=flops, bytes_accessed=moved, transcendentals=0),
-    )(*args)
+    )(*args, *after)
     return result[0] if len(outs) == 1 else result
 
 
@@ -256,7 +274,19 @@
     here = jnp.stack(
         [lax.axis_index("yh"), lax.axis_index("x"), lax.axis_index("core")]
     ).astype(I32)
-    home = lax.axis_index(EP).astype(I32).reshape(1)
+    home = jnp.stack([lax.axis_index("yl"), lax.axis_index("z")]).astype(I32)
+    n_yl, n_z = lax.axis_size("yl"), lax.axis_size("z")
+    n_high = min(4, n_z)
+    n_low = n_z // n_high
+
+    def shifted(a, axis, n, unit, k):
+        size = lax.axis_size(axis)
+        span = n * unit
+        pairs = [(i, i // span * span + (i + k * unit) % span) for i in range(size)]
+        return lax.ppermute(a, axis, pairs)
+
+    def spread(a, axis, n, unit):
+        return [a] + [shifted(a, axis, n, unit, k) for k in range(1, n)]
 
     send_second = call(
         functools.partial(dispatch_second_kernel, experts, cap),
@@ -296,35 +326,29 @@
         flops=2**31,
         moved=12 * MB,
     )
-    values = lax.all_gather(value.reshape(places), EP)
-    other = lax.ppermute(send, "core", [(0, 1), (1, 0)])
+    other = shifted(send, "core", 2, 1, 1)
     pair = ((2, block, 3 * hid), BF16)
-
-    def add(*terms):
-        return call(add_kernel, "add", [(terms[0].shape, BF16)], terms, moved=len(terms) * MB)
-
-    def summed(k):
-        return add(keep[2 * k : 2 * k + 2], other[2 * k : 2 * k + 2])
-
-    terms = [summed(0)]
-    for k in range(1, n_x):
-        terms.append(
-            lax.ppermute(summed(k), "x", [(i, (i + k) % n_x) for i in range(n_x)])
-        )
-    quarter = add(*terms)
-    far = lax.ppermute(quarter[1], "yh", [(0, 1), (1, 0)])
+    sums = call(pair_kernel, "pairs", [pair] * n_x, (keep, other), moved=8 * MB)
+    order = [k for k in sorted(range(1, n_x), key=lambda k: -min(k, n_x - k))]
+    terms = [shifted(sums[k], "x", n_x, 1, k) for k in order]
+    single = ((block, 3 * hid), BF16)
+    near, far = call(sum_kernel, "sums", [single] * 2, (sums[0], *terms), moved=3 * MB)
+    far = shifted(far, "yh", 2, 1, 1)
+    values = jnp.concatenate(spread(value, "yl", n_yl, 1), axis=0)
+    values = jnp.concatenate(spread(values, "z", n_high, n_low), axis=0)
+    values = spread(values, "z", n_low, 1)
     gate_up_grad, down_grad = call(
         functools.partial(finish_kernel, hid),
         "finish",
         [((block, 2 * hid), BF16), ((hid, block), BF16)],
-        (quarter[0], far),
+        (near, far),
         moved=MB,
     )
     gate_grads = call(
-        functools.partial(gate_grad_kernel, cap),
+        functools.partial(gate_grad_kernel, cap, (n_yl, n_high, n_low)),
         "gate_grad",
         [((1, tokens), F32)],
-        (home, values, row(routes_second), row(gates_second)),
+        (home, *values, row(routes_second), row(gates_second)),
         scalars=1,
         moved=MB // 8,
     )
@@ -335,6 +359,7 @@
         [chunk_shape],
         (got_first, gu, down),
         scratch=(row_shape,),
+        after=tuple(terms),
         flops=2**31,
         moved=7 * MB,
     )

time: 353 us -> 236 us (0.67)
  the two profiles are of different devices: /device:TPU:2 before, /device:TPU:1 now
where the time goes in v2:
time: 236 us; the launch traced here: 233 us
  starting transfers between devices  109 us (46%)
  waiting for transfers between devices  93.6 us (40%)
  Pallas kernels  19.3 us (8%)
  local copies, waits for them, and re-layouts  9.36 us (4%)
    all_to_all x3, waiting for transfers between devices, exchange(): moved = lax.all_to_all(chunks, EP, split_axis=0, concat_axis=0, tiled=True)  70 us
    ppermute x14, starting transfers between devices, shifted(): return lax.ppermute(a, axis, pairs)  62.9 us
    all_to_all x3, starting transfers between devices, exchange(): moved = lax.all_to_all(chunks, EP, split_axis=0, concat_axis=0, tiled=True)  46.6 us
    ppermute x14, waiting for transfers between devices, shifted(): return lax.ppermute(a, axis, pairs)  23.5 us
    pallas_call x10, Pallas kernels, call(): pl.pallas_call(kernel, name=name, out_shape=shapes, in_specs=[SMEM] * sca...  19.3 us
    unnamed x34, local copies, waits for them, and re-layouts  9.31 us
  transfers between devices with their start and end apart: 17, of which 6 were waited for; matrix products, arithmetic and copies ran while one was open for 0% of the time, Pallas kernels for 5%

profile of v2, /device:TPU:1, one launch (start us, length us, event | category | flops | bytes accessed | tf_op | source)
XLA Modules:
  0.0 232.8 jit_solution(10791733888563792539)
XLA Ops:
  0.6 0.0 copy-start.15
  0.6 0.0 copy-start.16
  0.7 0.0 copy-start.9
  0.7 0.7 copy-done.9
  1.3 0.7 copy-done.11
  2.0 1.0 copy-done.13
  3.0 2.4 %dispatch_second.1 = bf16[1024,512]{1,0:T(8,128)(2,1)} custom-call(s32[1,128]{1,0:T(1,128)S(1)} %bitcast.30, bf16[1,128]{1,0:T(2,128)(2,1)S(1)} %bitcast.32, bf16[128,2048]{1,0:T(8,128)(2,1)S(1)} %copy-done.13), custom_call_target="tpu_custom_call" | custom-call | flops 536870912 | bytes 2097152 | tf_op jit(solution)/shard_map/dispatch_second/pallas_call | solution.py:229
  5.4 23.6 %all-to-all-start.1 = ((bf16[64,16,512]{2,1,0:T(8,128)(2,1)}), bf16[64,16,512]{2,1,0:T(8,128)(2,1)}, u32[]{:S(2)}, u32[]{:S(2)}) async-start(bf16[64,16,512]{2,1,0:T(8,128)(2,1)} %bitcast.11), calls=%async_computation.1 | async-start | bytes 2097152 | tf_op jit(solution)/shard_map/all_to_all | solution.py:269
  29.1 0.0 copy-start
  29.1 0.0 copy-start.14
  29.1 1.2 copy-done.14
  30.3 1.4 dispatch_first.1
  31.7 1.0 copy-done.4
  32.7 46.8 %all-to-all-done.1 = bf16[64,16,512]{2,1,0:T(8,128)(2,1)} async-done(((bf16[64,16,512]{2,1,0:T(8,128)(2,1)}), bf16[64,16,512]{2,1,0:T(8,128)(2,1)}, u32[]{:S(2)}, u32[]{:S(2)}) %all-to-all-start.1) | async-done | bytes 1048608 | tf_op jit(solution)/shard_map/all_to_all | solution.py:269
  79.5 10.5 %all-to-all-start = ((bf16[64,16,512]{2,1,0:T(8,128)(2,1)}), bf16[64,16,512]{2,1,0:T(8,128)(2,1)}, u32[]{:S(2)}, u32[]{:S(2)}) async-start(bf16[64,16,512]{2,1,0:T(8,128)(2,1)} %bitcast.27), calls=%async_computation | async-start | bytes 2097152 | tf_op jit(solution)/shard_map/all_to_all | solution.py:269
  90.0 0.0 copy-start.2
  90.0 0.0 copy-start.5
  90.0 1.3 copy-done.5
  91.4 1.0 saved.1
  92.4 0.1 pad_add_fusion.at_ref
  92.5 0.2 copy-done.6
  92.7 3.9 %backward.1 = (bf16[8,128,1152]{2,1,0:T(8,128)(2,1)S(1)}, bf16[8,128,1152]{2,1,0:T(8,128)(2,1)S(1)}, f32[1,256]{1,0:T(1,128)S(1)}) custom-call(s32[3]{0:T(128)S(1)} %pad_add_fusion.at_ref, bf16[1024,512]{1,0:T(8,128)(2,1)} %bitcast.12.chunks_ref, bf16[384,2048]{1,0:T(8,128)(2,1)S(1)} %bitcast.24, bf16[256,2048]{1,0:T(8,128)(2,1)S(1)} %bitcast.29, ...), custom_call_target="tpu_custom_call" | custom-call | flops 2147483648 | bytes 12582912 | tf_op jit(solution)/shard_map/backward/pallas_call | solution.py:229
  96.6 3.1 %collective-permute-start = (bf16[8,128,1152]{2,1,0:T(8,128)(2,1)S(1)}, bf16[8,128,1152]{2,1,0:T(8,128)(2,1)S(1)}, u32[]{:S(2)}, u32[]{:S(2)}) collective-permute-start(bf16[8,128,1152]{2,1,0:T(8,128)(2,1)S(1)} %get-tuple-element.25), channel_id=1, source_target_pairs={{0,1},{1,0},{2,3},{3,2},{4,5},{5,4},{6,7},{7,6},{8,9},{9,8},{10,11... | collective-permute-start | bytes 7077896 | tf_op jit(solution)/shard_map/ppermute | solution.py:286
  99.6 4.1 %collective-permute-done.b_ref = bf16[8,128,1152]{2,1,0:T(8,128)(2,1)S(1)} collective-permute-done((bf16[8,128,1152]{2,1,0:T(8,128)(2,1)S(1)}, bf16[8,128,1152]{2,1,0:T(8,128)(2,1)S(1)}, u32[]{:S(2)}, u32[]{:S(2)}) %collective-permute-start) | collective-permute-done | bytes 2359328 | tf_op jit(solution)/shard_map/ppermute | solution.py:286
  103.8 1.4 pairs.1
  105.2 0.8 copy-done.7
  106.0 4.7 %collective-permute-start.1 = (bf16[2,128,1152]{2,1,0:T(8,128)(2,1)}, bf16[2,128,1152]{2,1,0:T(8,128)(2,1)}, u32[]{:S(2)}, u32[]{:S(2)}) collective-permute-start(bf16[2,128,1152]{2,1,0:T(8,128)(2,1)} %get-tuple-element.26), channel_id=1, source_target_pairs={{0,4},{2,6},{4,0},{6,2},{1,5},{3,7},{5,1},{7,3},{8,12},{10,14},{12... | collective-permute-start | bytes 1769480 | tf_op jit(solution)/shard_map/ppermute | solution.py:286
  110.7 2.2 collective-permute-start.2
  112.9 4.3 %collective-permute-start.3 = (bf16[2,128,1152]{2,1,0:T(8,128)(2,1)}, bf16[2,128,1152]{2,1,0:T(8,128)(2,1)}, u32[]{:S(2)}, u32[]{:S(2)}) collective-permute-start(bf16[2,128,1152]{2,1,0:T(8,128)(2,1)} %get-tuple-element.28), channel_id=1, source_target_pairs={{0,6},{2,0},{4,2},{6,4},{1,7},{3,1},{5,3},{7,5},{8,14},{10,8},{12,... | collective-permute-start | bytes 1769480 | tf_op jit(solution)/shard_map/ppermute | solution.py:286
  117.2 23.2 %all-to-all-done = bf16[64,16,512]{2,1,0:T(8,128)(2,1)} async-done(((bf16[64,16,512]{2,1,0:T(8,128)(2,1)}), bf16[64,16,512]{2,1,0:T(8,128)(2,1)}, u32[]{:S(2)}, u32[]{:S(2)}) %all-to-all-start) | async-done | bytes 1048608 | tf_op jit(solution)/shard_map/all_to_all | solution.py:269
  140.5 0.0 collective-permute-done.1.refs_0_.refs_1_
  140.5 0.0 collective-permute-done.2.refs_1_.refs_2_
  140.5 0.0 collective-permute-done.3.refs_2_.refs_3_
  140.5 0.0 copy-start.3
  140.5 1.4 copy-done.3
  141.9 4.0 %forward.1 = bf16[1024,512]{1,0:T(8,128)(2,1)S(1)} custom-call(bf16[1024,512]{1,0:T(8,128)(2,1)} %bitcast.3.chunks_ref, bf16[2048,768]{1,0:T(8,128)(2,1)S(1)} %bitcast.22, bf16[384,2048]{1,0:T(8,128)(2,1)S(1)} %bitcast.25, bf16[2,128,1152]{2,1,0:T(8,128)(2,1)} %collective-permute-done.1.refs_0_.refs_1_, ...), custom_call_target="tpu_custom_call" | custom-call | flops 2147483648 | bytes 7340032 | tf_op jit(solution)/shard_map/forward/pallas_call | solution.py:229
  145.9 1.0 copy-done.1
  146.9 12.4 %all-to-all-start.2 = ((bf16[64,16,512]{2,1,0:T(8,128)(2,1)}), bf16[64,16,512]{2,1,0:T(8,128)(2,1)S(1)}, u32[]{:S(2)}, u32[]{:S(2)}) async-start(bf16[64,16,512]{2,1,0:T(8,128)(2,1)} %bitcast.23), calls=%async_computation.2 | async-start | bytes 2097152 | tf_op jit(solution)/shard_map/all_to_all | solution.py:269
  159.3 1.7 sums.1
  161.0 4.8 %collective-permute-start.13 = (bf16[128,1152]{1,0:T(8,128)(2,1)S(1)}, bf16[128,1152]{1,0:T(8,128)(2,1)S(1)}, u32[]{:S(2)}, u32[]{:S(2)}) collective-permute-start(bf16[128,1152]{1,0:T(8,128)(2,1)S(1)} %get-tuple-element.33), channel_id=1, source_target_pairs={{0,8},{8,0},{1,9},{9,1},{2,10},{10,2},{3,11},{11,3},{4,12},{12,4},... | collective-permute-start | bytes 884744 | tf_op jit(solution)/shard_map/ppermute | solution.py:286
  165.8 2.9 %collective-permute-start.4 = (f32[1,256]{1,0:T(1,128)S(1)}, f32[1,256]{1,0:T(1,128)S(1)}, u32[]{:S(2)}, u32[]{:S(2)}) collective-permute-start(f32[1,256]{1,0:T(1,128)S(1)} %get-tuple-element.30), channel_id=1, source_target_pairs={{0,256},{256,512},{512,768},{768,0},{1,257},{257,513},{513,769},{7... | collective-permute-start | bytes 3080 | tf_op jit(solution)/shard_map/ppermute | solution.py:286
  168.7 4.2 %collective-permute-start.5 = (f32[1,256]{1,0:T(1,128)S(1)}, f32[1,256]{1,0:T(1,128)S(1)}, u32[]{:S(2)}, u32[]{:S(2)}) collective-permute-start(f32[1,256]{1,0:T(1,128)S(1)} %get-tuple-element.30), channel_id=1, source_target_pairs={{0,512},{256,768},{512,0},{768,256},{1,513},{257,769},{513,1},{769... | collective-permute-start | bytes 3080 | tf_op jit(solution)/shard_map/ppermute | solution.py:286
  172.9 3.0 %collective-permute-start.6 = (f32[1,256]{1,0:T(1,128)S(1)}, f32[1,256]{1,0:T(1,128)S(1)}, u32[]{:S(2)}, u32[]{:S(2)}) collective-permute-start(f32[1,256]{1,0:T(1,128)S(1)} %get-tuple-element.30), channel_id=1, source_target_pairs={{0,768},{256,0},{512,256},{768,512},{1,769},{257,1},{513,257},{769... | collective-permute-start | bytes 3080 | tf_op jit(solution)/shard_map/ppermute | solution.py:286
  175.9 17.1 %collective-permute-done.4 = f32[1,256]{1,0:T(1,128)S(1)} collective-permute-done((f32[1,256]{1,0:T(1,128)S(1)}, f32[1,256]{1,0:T(1,128)S(1)}, u32[]{:S(2)}, u32[]{:S(2)}) %collective-permute-start.4) | collective-permute-done | bytes 1056 | tf_op jit(solution)/shard_map/ppermute | solution.py:286
  193.1 0.0 collective-permute-done.5
  193.1 0.0 collective-permute-done.6
  193.1 8.1 %collective-permute-start.7 = (f32[4,256]{1,0:T(4,128)S(1)}, f32[4,256]{1,0:T(4,128)S(1)}, u32[]{:S(2)}, u32[]{:S(2)}) collective-permute-start(f32[4,256]{1,0:T(4,128)S(1)} %pad_maximum_fusion), channel_id=1, source_target_pairs={{0,64},{16,80},{32,96},{48,112},{64,128},{80,144},{96,160},{112,17... | collective-permute-start | bytes 12296 | tf_op jit(solution)/shard_map/ppermute | solution.py:286
  201.2 9.3 %collective-permute-start.8 = (f32[4,256]{1,0:T(4,128)S(1)}, f32[4,256]{1,0:T(4,128)S(1)}, u32[]{:S(2)}, u32[]{:S(2)}) collective-permute-start(f32[4,256]{1,0:T(4,128)S(1)} %pad_maximum_fusion), channel_id=1, source_target_pairs={{0,128},{16,144},{32,160},{48,176},{64,192},{80,208},{96,224},{112... | collective-permute-start | bytes 12296 | tf_op jit(solution)/shard_map/ppermute | solution.py:286
  210.6 7.3 %collective-permute-start.9 = (f32[4,256]{1,0:T(4,128)S(1)}, f32[4,256]{1,0:T(4,128)S(1)}, u32[]{:S(2)}, u32[]{:S(2)}) collective-permute-start(f32[4,256]{1,0:T(4,128)S(1)} %pad_maximum_fusion), channel_id=1, source_target_pairs={{0,192},{16,208},{32,224},{48,240},{64,0},{80,16},{96,32},{112,48}... | collective-permute-start | bytes 12296 | tf_op jit(solution)/shard_map/ppermute | solution.py:286
  217.8 0.0 collective-permute-done.7
  217.9 0.0 collective-permute-done.8
  217.9 1.0 collective-permute-done.9
  218.9 1.9 collective-permute-start.10
  220.8 1.9 collective-permute-start.11
  222.7 5.2 %collective-permute-start.12 = (f32[16,256]{1,0:T(8,128)S(1)}, f32[16,256]{1,0:T(8,128)S(1)}, u32[]{:S(2)}, u32[]{:S(2)}) collective-permute-start(f32[16,256]{1,0:T(8,128)S(1)} %concatenate.8.refs_0_), channel_id=1, source_target_pairs={{0,48},{16,0},{32,16},{48,32},{64,112},{80,64},{96,80},{112,96},{1... | collective-permute-start | bytes 49160 | tf_op jit(solution)/shard_map/ppermute | solution.py:286
  227.9 0.1 pad_add_fusion.1.at_ref
  228.0 0.0 collective-permute-done.10.refs_1_
  228.0 0.0 collective-permute-done.11.refs_2_
  228.0 1.3 collective-permute-done.12.refs_3_
  229.3 1.2 gate_grad.1
  230.5 0.0 collective-permute-done.13.b_ref
  230.5 0.8 finish.1
  231.3 0.0 all-to-all-done.2
  231.3 1.5 combine.1
  (18 shorter events, 0.1 us)
Async XLA Ops:
  0.6 28.4 %copy-start.15 = (s32[128,1]{0,1:T(1,128)S(1)}, s32[128,1]{0,1:T(1,128)}, u32[]{:S(2)}) copy-start(s32[128,1]{0,1:T(1,128)} %param.10) | copy-start | bytes 1540
  0.6 28.4 %copy-start.16 = (bf16[128,1]{0,1:T(2,128)(2,1)S(1)}, bf16[128,1]{0,1:T(2,128)(2,1)}, u32[]{:S(2)}) copy-start(bf16[128,1]{0,1:T(2,128)(2,1)} %param.11) | copy-start | bytes 772
  0.7 0.7 copy-start.9
  1.3 0.7 copy-start.11
  2.0 1.0 copy-start.13
  5.4 74.0 %all-to-all-start.1 = ((bf16[64,16,512]{2,1,0:T(8,128)(2,1)}), bf16[64,16,512]{2,1,0:T(8,128)(2,1)}, u32[]{:S(2)}, u32[]{:S(2)}) async-start(bf16[64,16,512]{2,1,0:T(8,128)(2,1)} %bitcast.11), calls=%async_computation.1 | async-start | bytes 2097152 | tf_op jit(solution)/shard_map/all_to_all | solution.py:269
  29.1 61.0 %copy-start = (bf16[1,2048,768]{2,1,0:T(8,128)(2,1)S(1)}, bf16[1,2048,768]{2,1,0:T(8,128)(2,1)}, u32[]{:S(2)}) copy-start(bf16[1,2048,768]{2,1,0:T(8,128)(2,1)} %param.12) | copy-start | bytes 9437188
  29.1 1.2 copy-start.14
  31.7 1.0 copy-start.4
  79.5 61.0 %all-to-all-start = ((bf16[64,16,512]{2,1,0:T(8,128)(2,1)}), bf16[64,16,512]{2,1,0:T(8,128)(2,1)}, u32[]{:S(2)}, u32[]{:S(2)}) async-start(bf16[64,16,512]{2,1,0:T(8,128)(2,1)} %bitcast.27), calls=%async_computation | async-start | bytes 2097152 | tf_op jit(solution)/shard_map/all_to_all | solution.py:269
  90.0 2.5 %copy-start.2 = (bf16[1,384,2048]{2,1,0:T(8,128)(2,1)S(1)}, bf16[1,384,2048]{2,1,0:T(8,128)(2,1)}, u32[]{:S(2)}) copy-start(bf16[1,384,2048]{2,1,0:T(8,128)(2,1)} %param.13) | copy-start | bytes 4718596
  90.0 1.3 copy-start.5
  91.4 1.3 copy-start.6
  96.6 7.2 %collective-permute-start = (bf16[8,128,1152]{2,1,0:T(8,128)(2,1)S(1)}, bf16[8,128,1152]{2,1,0:T(8,128)(2,1)S(1)}, u32[]{:S(2)}, u32[]{:S(2)}) collective-permute-start(bf16[8,128,1152]{2,1,0:T(8,128)(2,1)S(1)} %get-tuple-element.25), channel_id=1, source_target_pairs={{0,1},{1,0},{2,3},{3,2},{4,5},{5,4},{6,7},{7,6},{8,9},{9,8},{10,11... | collective-permute-start | bytes 7077896 | tf_op jit(solution)/shard_map/ppermute | solution.py:286
  105.2 0.8 copy-start.7
  106.0 34.5 %collective-permute-start.1 = (bf16[2,128,1152]{2,1,0:T(8,128)(2,1)}, bf16[2,128,1152]{2,1,0:T(8,128)(2,1)}, u32[]{:S(2)}, u32[]{:S(2)}) collective-permute-start(bf16[2,128,1152]{2,1,0:T(8,128)(2,1)} %get-tuple-element.26), channel_id=1, source_target_pairs={{0,4},{2,6},{4,0},{6,2},{1,5},{3,7},{5,1},{7,3},{8,12},{10,14},{12... | collective-permute-start | bytes 1769480 | tf_op jit(solution)/shard_map/ppermute | solution.py:286
  110.7 29.7 %collective-permute-start.2 = (bf16[2,128,1152]{2,1,0:T(8,128)(2,1)}, bf16[2,128,1152]{2,1,0:T(8,128)(2,1)}, u32[]{:S(2)}, u32[]{:S(2)}) collective-permute-start(bf16[2,128,1152]{2,1,0:T(8,128)(2,1)} %get-tuple-element.27), channel_id=1, source_target_pairs={{0,2},{2,4},{4,6},{6,0},{1,3},{3,5},{5,7},{7,1},{8,10},{10,12},{12... | collective-permute-start | bytes 1769480 | tf_op jit(solution)/shard_map/ppermute | solution.py:286
  112.9 27.5 %collective-permute-start.3 = (bf16[2,128,1152]{2,1,0:T(8,128)(2,1)}, bf16[2,128,1152]{2,1,0:T(8,128)(2,1)}, u32[]{:S(2)}, u32[]{:S(2)}) collective-permute-start(bf16[2,128,1152]{2,1,0:T(8,128)(2,1)} %get-tuple-element.28), channel_id=1, source_target_pairs={{0,6},{2,0},{4,2},{6,4},{1,7},{3,1},{5,3},{7,5},{8,14},{10,8},{12,... | collective-permute-start | bytes 1769480 | tf_op jit(solution)/shard_map/ppermute | solution.py:286
  140.5 1.4 copy-start.3
  145.9 1.0 copy-start.1
  146.9 12.4 %copy-start.8 = (bf16[2,128,1152]{2,1,0:T(8,128)(2,1)S(1)}, bf16[2,128,1152]{2,1,0:T(8,128)(2,1)}, u32[]{:S(2)}) copy-start(bf16[2,128,1152]{2,1,0:T(8,128)(2,1)} %copy-done.7) | copy-start | bytes 1769476
  146.9 82.4 %copy-start.10 = (s32[128,1]{0,1:T(1,128)S(1)}, s32[128,1]{0,1:T(1,128)}, u32[]{:S(2)}) copy-start(s32[128,1]{0,1:T(1,128)} %param.16) | copy-start | bytes 1540
  146.9 82.4 %copy-start.12 = (bf16[128,1]{0,1:T(2,128)(2,1)S(1)}, bf16[128,1]{0,1:T(2,128)(2,1)}, u32[]{:S(2)}) copy-start(bf16[128,1]{0,1:T(2,128)(2,1)} %param.17) | copy-start | bytes 772
  146.9 84.4 %all-to-all-start.2 = ((bf16[64,16,512]{2,1,0:T(8,128)(2,1)}), bf16[64,16,512]{2,1,0:T(8,128)(2,1)S(1)}, u32[]{:S(2)}, u32[]{:S(2)}) async-start(bf16[64,16,512]{2,1,0:T(8,128)(2,1)} %bitcast.23), calls=%async_computation.2 | async-start | bytes 2097152 | tf_op jit(solution)/shard_map/all_to_all | solution.py:269
  161.0 69.4 %collective-permute-start.13 = (bf16[128,1152]{1,0:T(8,128)(2,1)S(1)}, bf16[128,1152]{1,0:T(8,128)(2,1)S(1)}, u32[]{:S(2)}, u32[]{:S(2)}) collective-permute-start(bf16[128,1152]{1,0:T(8,128)(2,1)S(1)} %get-tuple-element.33), channel_id=1, source_target_pairs={{0,8},{8,0},{1,9},{9,1},{2,10},{10,2},{3,11},{11,3},{4,12},{12,4},... | collective-permute-start | bytes 884744 | tf_op jit(solution)/shard_map/ppermute | solution.py:286
  165.8 27.2 %collective-permute-start.4 = (f32[1,256]{1,0:T(1,128)S(1)}, f32[1,256]{1,0:T(1,128)S(1)}, u32[]{:S(2)}, u32[]{:S(2)}) collective-permute-start(f32[1,256]{1,0:T(1,128)S(1)} %get-tuple-element.30), channel_id=1, source_target_pairs={{0,256},{256,512},{512,768},{768,0},{1,257},{257,513},{513,769},{7... | collective-permute-start | bytes 3080 | tf_op jit(solution)/shard_map/ppermute | solution.py:286
  168.7 24.3 %collective-permute-start.5 = (f32[1,256]{1,0:T(1,128)S(1)}, f32[1,256]{1,0:T(1,128)S(1)}, u32[]{:S(2)}, u32[]{:S(2)}) collective-permute-start(f32[1,256]{1,0:T(1,128)S(1)} %get-tuple-element.30), channel_id=1, source_target_pairs={{0,512},{256,768},{512,0},{768,256},{1,513},{257,769},{513,1},{769... | collective-permute-start | bytes 3080 | tf_op jit(solution)/shard_map/ppermute | solution.py:286
  172.9 20.1 %collective-permute-start.6 = (f32[1,256]{1,0:T(1,128)S(1)}, f32[1,256]{1,0:T(1,128)S(1)}, u32[]{:S(2)}, u32[]{:S(2)}) collective-permute-start(f32[1,256]{1,0:T(1,128)S(1)} %get-tuple-element.30), channel_id=1, source_target_pairs={{0,768},{256,0},{512,256},{768,512},{1,769},{257,1},{513,257},{769... | collective-permute-start | bytes 3080 | tf_op jit(solution)/shard_map/ppermute | solution.py:286
  193.1 24.8 %collective-permute-start.7 = (f32[4,256]{1,0:T(4,128)S(1)}, f32[4,256]{1,0:T(4,128)S(1)}, u32[]{:S(2)}, u32[]{:S(2)}) collective-permute-start(f32[4,256]{1,0:T(4,128)S(1)} %pad_maximum_fusion), channel_id=1, source_target_pairs={{0,64},{16,80},{32,96},{48,112},{64,128},{80,144},{96,160},{112,17... | collective-permute-start | bytes 12296 | tf_op jit(solution)/shard_map/ppermute | solution.py:286
  201.2 16.7 %collective-permute-start.8 = (f32[4,256]{1,0:T(4,128)S(1)}, f32[4,256]{1,0:T(4,128)S(1)}, u32[]{:S(2)}, u32[]{:S(2)}) collective-permute-start(f32[4,256]{1,0:T(4,128)S(1)} %pad_maximum_fusion), channel_id=1, source_target_pairs={{0,128},{16,144},{32,160},{48,176},{64,192},{80,208},{96,224},{112... | collective-permute-start | bytes 12296 | tf_op jit(solution)/shard_map/ppermute | solution.py:286
  210.6 8.3 %collective-permute-start.9 = (f32[4,256]{1,0:T(4,128)S(1)}, f32[4,256]{1,0:T(4,128)S(1)}, u32[]{:S(2)}, u32[]{:S(2)}) collective-permute-start(f32[4,256]{1,0:T(4,128)S(1)} %pad_maximum_fusion), channel_id=1, source_target_pairs={{0,192},{16,208},{32,224},{48,240},{64,0},{80,16},{96,32},{112,48}... | collective-permute-start | bytes 12296 | tf_op jit(solution)/shard_map/ppermute | solution.py:286
  218.9 9.1 %collective-permute-start.10 = (f32[16,256]{1,0:T(8,128)S(1)}, f32[16,256]{1,0:T(8,128)S(1)}, u32[]{:S(2)}, u32[]{:S(2)}) collective-permute-start(f32[16,256]{1,0:T(8,128)S(1)} %concatenate.8.refs_0_), channel_id=1, source_target_pairs={{0,16},{16,32},{32,48},{48,0},{64,80},{80,96},{96,112},{112,64},{1... | collective-permute-start | bytes 49160 | tf_op jit(solution)/shard_map/ppermute | solution.py:286
  220.8 7.2 %collective-permute-start.11 = (f32[16,256]{1,0:T(8,128)S(1)}, f32[16,256]{1,0:T(8,128)S(1)}, u32[]{:S(2)}, u32[]{:S(2)}) collective-permute-start(f32[16,256]{1,0:T(8,128)S(1)} %concatenate.8.refs_0_), channel_id=1, source_target_pairs={{0,32},{16,48},{32,0},{48,16},{64,96},{80,112},{96,64},{112,80},{1... | collective-permute-start | bytes 49160 | tf_op jit(solution)/shard_map/ppermute | solution.py:286
  222.7 6.6 %collective-permute-start.12 = (f32[16,256]{1,0:T(8,128)S(1)}, f32[16,256]{1,0:T(8,128)S(1)}, u32[]{:S(2)}, u32[]{:S(2)}) collective-permute-start(f32[16,256]{1,0:T(8,128)S(1)} %concatenate.8.refs_0_), channel_id=1, source_target_pairs={{0,48},{16,0},{32,16},{48,32},{64,112},{80,64},{96,80},{112,96},{1... | collective-permute-start | bytes 49160 | tf_op jit(solution)/shard_map/ppermute | solution.py:286

commit v3 on v2

--- a/solution.py
+++ b/solution.py
@@ -12,7 +12,8 @@
 I32 = jnp.int32
 EP = ("yl", "z")
 ALL = ("yl", "z", "yh", "x", "core")
-CHUNK = 16
+CHUNK = 8
+EXTRA = 128
 
 
 def iota(shape, dim):
@@ -33,17 +34,8 @@
 
 def order_of(rows, cap, dim):
     j = iota((rows, rows), dim)
-    pieces = CHUNK // cap
-    per = rows // pieces
-    return (j % CHUNK) // cap * per + j // CHUNK * cap + j % cap
-
-
-def gather_order(rows, cap):
-    return (iota((rows, rows), 0) == order_of(rows, cap, 1)).astype(F32).astype(BF16)
-
-
-def scatter_order(rows, cap):
-    return (iota((rows, rows), 1) == order_of(rows, cap, 0)).astype(F32).astype(BF16)
+    per = rows * cap // CHUNK
+    return j % CHUNK // cap * per + j // CHUNK * cap + j % cap
 
 
 GROUP = 256
@@ -53,7 +45,8 @@
     width = chunks_ref.shape[1]
     pieces = CHUNK // cap
     per = GROUP // pieces
-    order = gather_order(GROUP, cap)
+    order = (iota((GROUP, GROUP), 0) == order_of(GROUP, cap, 1)).astype(F32)
+    order = order.astype(BF16)
     for g in range(chunks_ref.shape[0] // GROUP):
         part = dot(order, chunks_ref[g * GROUP : (g + 1) * GROUP, :]).astype(BF16)
         for q in range(pieces):
@@ -66,7 +59,8 @@
     width = chunks_ref.shape[1]
     pieces = CHUNK // cap
     per = GROUP // pieces
-    order = scatter_order(GROUP, cap)
+    order = (iota((GROUP, GROUP), 1) == order_of(GROUP, cap, 0)).astype(F32)
+    order = order.astype(BF16)
     for g in range(chunks_ref.shape[0] // GROUP):
         part = jnp.concatenate(
             [
@@ -94,22 +88,33 @@
     return slots
 
 
-def dispatch_second_kernel(experts, cap, routes_ref, gates_ref, tokens_ref, chunks_ref):
-    send_rows(
-        experts, cap, routes_ref[...], gates_ref[...].astype(F32), tokens_ref, chunks_ref
-    )
+def dispatch_second_kernel(
+    experts, cap, routes_ref, gates_ref, tokens_ref, chunks_ref
+):
+    send_rows(experts, cap, routes_ref[...], gates_ref[...].astype(F32), tokens_ref, chunks_ref)
 
 
 def dispatch_first_kernel(
-    experts, cap, routes_ref, gates_ref, tokens_ref, chunks_ref, mix_ref
+    experts,
+    cap,
+    routes_ref,
+    gates_ref,
+    other_routes_ref,
+    tokens_ref,
+    chunks_ref,
+    mix_ref,
+    pick_ref,
 ):
     routes = routes_ref[...]
     slots = send_rows(
         experts, cap, routes, jnp.ones(routes.shape, F32), tokens_ref, chunks_ref
     )
-    places = experts * cap
-    hit = iota((places, routes.shape[1]), 0) == routes * cap + slots
+    place = iota((experts * cap, routes.shape[1]), 0)
+    hit = place == routes * cap + slots
     mix_ref[...] = jnp.where(hit, gates_ref[...].astype(F32), 0.0).T.astype(BF16)
+    routes = other_routes_ref[...]
+    _, slots = slots_of(routes, experts)
+    pick_ref[...] = (place == routes * cap + slots).astype(F32).T.astype(BF16)
 
 
 def saved_kernel(x_ref, gu_ref, act_ref, gate_ref, up_ref):
@@ -140,16 +145,19 @@
 ):
     hid = act_ref.shape[1]
     block = keep_ref.shape[1]
+    core, y, x = at_ref[0], at_ref[1], at_ref[2]
     from_chunks(chunks_ref, rows_ref, cap)
     scaled = dot(rows_ref[...], down_ref[...], 1, 1)
-    product = scaled * act_ref[...].astype(F32)
-    folded = product[:, :128]
-    for k in range(1, hid // 128):
-        folded = folded + product[:, k * 128 : (k + 1) * 128]
-    value_ref[...] = jnp.sum(folded.T, axis=0, keepdims=True)
+    value = jnp.sum(scaled * act_ref[...].astype(F32), axis=1, keepdims=True)
+    lane = iota(value_ref.shape, 1)
+    parts = jnp.zeros(value_ref.shape, F32)
+    for k in range(3):
+        part = value.astype(BF16).astype(F32)
+        parts = jnp.where(lane == k, part, parts)
+        value = value - part
+    value_ref[...] = parts.astype(BF16)
     both_ref[:, :hid] = (scaled * gate_ref[...]).astype(BF16)
     both_ref[:, hid:] = (scaled * up_ref[...]).astype(BF16)
-    y, x, core = at_ref[0], at_ref[1], at_ref[2]
     n_x = keep_ref.shape[0] // 2
     for out_ref, other in ((send_ref, 1), (keep_ref, 0)):
         for n in range(2 * n_x):
@@ -159,43 +167,35 @@
             out_ref[n, :, 2 * hid :] = dot(rows_ref[:, columns], act_ref[...], 0, 0).astype(BF16)
 
 
-def forward_kernel(cap, chunks_ref, gu_ref, down_ref, *refs):
-    out_ref, rows_ref = refs[-2:]
-    hid = down_ref.shape[0]
+def forward_kernel(cap, chunks_ref, gu_ref, down_ref, value_ref, *refs):
+    out_ref, in_rows_ref, out_rows_ref = refs[-3:]
+    model, hid = down_ref.shape[1], down_ref.shape[0]
+    from_chunks(chunks_ref, in_rows_ref, cap)
+    both = dot(in_rows_ref[...], gu_ref[...])
+    act = (jax.nn.silu(both[:, :hid]) * both[:, hid:]).astype(BF16)
+    width = chunks_ref.shape[1]
+    for q in range(model // width):
+        at = q * (width + EXTRA)
+        out_rows_ref[:, at : at + width] = dot(
+            act, down_ref[:, q * width : (q + 1) * width]
+        ).astype(BF16)
+        out_rows_ref[:, at + width : at + width + EXTRA] = value_ref[...]
+    to_chunks(out_rows_ref, out_ref, cap)
+
+
+def combine_kernel(
+    cap, chunks_ref, mix_ref, pick_ref, gates_ref, out_ref, grads_ref, rows_ref
+):
     from_chunks(chunks_ref, rows_ref, cap)
-    both = dot(rows_ref[...], gu_ref[...])
-    act = (jax.nn.silu(both[:, :hid]) * both[:, hid:]).astype(BF16)
-    rows_ref[...] = dot(act, down_ref[...]).astype(BF16)
-    to_chunks(rows_ref, out_ref, cap)
-
-
-def combine_kernel(cap, chunks_ref, mix_ref, out_ref, rows_ref):
-    from_chunks(chunks_ref, rows_ref, cap)
-    out_ref[...] = dot(mix_ref[...], rows_ref[...]).astype(BF16)
-
-
-def gate_grad_kernel(cap, digits, at_ref, *refs):
-    *value_refs, routes_ref, gates_ref, out_ref = refs
-    n_yl, n_high, n_low = digits
-    values = jnp.concatenate([ref[...] for ref in value_refs], axis=0)
-    experts, places = values.shape
-    tokens = out_ref.shape[1]
-    routes = routes_ref[...]
-    _, slots = slots_of(routes, experts)
-    yl, high, low = at_ref[0], at_ref[1] // n_low, at_ref[1] % n_low
-    home = yl * (n_high * n_low) + at_ref[1]
-    far_yl = (yl + n_yl - routes // (n_high * n_low)) % n_yl
-    far_high = (high + n_high - routes // n_low % n_high) % n_high
-    far_low = (low + n_low - routes % n_low) % n_low
-    source = (far_low * n_high + far_high) * n_yl + far_yl
-    hit = (iota((experts, tokens), 0) == source).astype(F32)
-    lane = iota((experts, places), 1)
-    total = jnp.zeros(out_ref.shape, F32)
-    for c in range(cap):
-        mine = jnp.sum(jnp.where(lane == home * cap + c, values, 0.0), axis=1, keepdims=True)
-        here = jnp.sum(hit * mine, axis=0, keepdims=True)
-        total = total + jnp.where(slots == c, here, 0.0)
-    out_ref[...] = total / gates_ref[...].astype(F32)
+    width = chunks_ref.shape[1] - EXTRA
+    for q in range(CHUNK // cap):
+        at = q * (width + EXTRA)
+        out_ref[:, q * width : (q + 1) * width] = dot(
+            mix_ref[...], rows_ref[:, at : at + width]
+        ).astype(BF16)
+    value = dot(pick_ref[...], rows_ref[:, width : width + EXTRA])
+    value = jnp.sum(value.T, axis=0, keepdims=True)
+    grads_ref[...] = value / gates_ref[...].astype(F32)
 
 
 def pair_kernel(a_ref, b_ref, *out_refs):
@@ -265,28 +265,24 @@
         return a.reshape(1, tokens)
 
     def exchange(chunks):
-        chunks = chunks.reshape(experts, CHUNK, width)
+        wide = chunks.shape[1]
+        chunks = chunks.reshape(experts, CHUNK, wide)
         moved = lax.all_to_all(chunks, EP, split_axis=0, concat_axis=0, tiled=True)
-        return moved.reshape(experts * CHUNK, width)
+        return moved.reshape(experts * CHUNK, wide)
+
+    def shifted(a, axis, k):
+        size = lax.axis_size(axis)
+        return lax.ppermute(a, axis, [(i, (i + k) % size) for i in range(size)])
 
     chunk_shape = ((experts * CHUNK, width), BF16)
+    back_shape = ((experts * CHUNK, width + EXTRA), BF16)
     row_shape = ((places, model), BF16)
+    back_rows = ((places, model + CHUNK // cap * EXTRA), BF16)
+    extra_shape = ((places, EXTRA), BF16)
+    pick_shape = ((tokens, places), BF16)
     here = jnp.stack(
-        [lax.axis_index("yh"), lax.axis_index("x"), lax.axis_index("core")]
+        [lax.axis_index("core"), lax.axis_index("yh"), lax.axis_index("x")]
     ).astype(I32)
-    home = jnp.stack([lax.axis_index("yl"), lax.axis_index("z")]).astype(I32)
-    n_yl, n_z = lax.axis_size("yl"), lax.axis_size("z")
-    n_high = min(4, n_z)
-    n_low = n_z // n_high
-
-    def shifted(a, axis, n, unit, k):
-        size = lax.axis_size(axis)
-        span = n * unit
-        pairs = [(i, i // span * span + (i + k * unit) % span) for i in range(size)]
-        return lax.ppermute(a, axis, pairs)
-
-    def spread(a, axis, n, unit):
-        return [a] + [shifted(a, axis, n, unit, k) for k in range(1, n)]
 
     send_second = call(
         functools.partial(dispatch_second_kernel, experts, cap),
@@ -297,11 +293,11 @@
         moved=2 * MB,
     )
     got_second = exchange(send_second)
-    send_first, mix = call(
+    send_first, mix, pick = call(
         functools.partial(dispatch_first_kernel, experts, cap),
         "dispatch_first",
-        [chunk_shape, ((tokens, places), BF16)],
-        (row(routes_first), row(gates_first), tokens_first),
+        [chunk_shape, pick_shape, pick_shape],
+        (row(routes_first), row(gates_first), row(routes_second), tokens_first),
         flops=2**29,
         moved=2 * MB,
     )
@@ -319,24 +315,21 @@
     keep, send, value = call(
         functools.partial(backward_kernel, cap),
         "backward",
-        [half, half, ((1, places), F32)],
+        [half, half, extra_shape],
         (here, got_second, down, x, act, by_gate, by_up),
         scratch=(row_shape, ((places, 2 * hid), BF16)),
         scalars=1,
         flops=2**31,
         moved=12 * MB,
     )
-    other = shifted(send, "core", 2, 1, 1)
+    other = shifted(send, "core", 1)
     pair = ((2, block, 3 * hid), BF16)
     sums = call(pair_kernel, "pairs", [pair] * n_x, (keep, other), moved=8 * MB)
-    order = [k for k in sorted(range(1, n_x), key=lambda k: -min(k, n_x - k))]
-    terms = [shifted(sums[k], "x", n_x, 1, k) for k in order]
+    order = sorted(range(1, n_x), key=lambda k: -min(k, n_x - k))
+    terms = [shifted(sums[k], "x", k) for k in order]
     single = ((block, 3 * hid), BF16)
     near, far = call(sum_kernel, "sums", [single] * 2, (sums[0], *terms), moved=3 * MB)
-    far = shifted(far, "yh", 2, 1, 1)
-    values = jnp.concatenate(spread(value, "yl", n_yl, 1), axis=0)
-    values = jnp.concatenate(spread(values, "z", n_high, n_low), axis=0)
-    values = spread(values, "z", n_low, 1)
+    far = shifted(far, "yh", 1)
     gate_up_grad, down_grad = call(
         functools.partial(finish_kernel, hid),
         "finish",
@@ -344,32 +337,23 @@
         (near, far),
         moved=MB,
     )
-    gate_grads = call(
-        functools.partial(gate_grad_kernel, cap, (n_yl, n_high, n_low)),
-        "gate_grad",
-        [((1, tokens), F32)],
-        (home, *values, row(routes_second), row(gates_second)),
-        scalars=1,
-        moved=MB // 8,
-    )
-
     send_back = call(
         functools.partial(forward_kernel, cap),
         "forward",
-        [chunk_shape],
-        (got_first, gu, down),
-        scratch=(row_shape,),
+        [back_shape],
+        (got_first, gu, down, value),
+        scratch=(row_shape, back_rows),
         after=tuple(terms),
         flops=2**31,
         moved=7 * MB,
     )
     got_back = exchange(send_back)
-    mixed_first = call(
+    mixed_first, gate_grads = call(
         functools.partial(combine_kernel, cap),
         "combine",
-        [((tokens, model), BF16)],
-        (got_back, mix),
-        scratch=(row_shape,),
+        [((tokens, model), BF16), ((1, tokens), F32)],
+        (got_back, mix, pick, row(gates_second)),
+        scratch=(back_rows,),
         flops=2**29,
         moved=2 * MB,
     )

time: 236 us -> 222 us (0.941)
  the two profiles are of different devices: /device:TPU:1 before, /device:TPU:4 now
where the time goes in v3:
time: 222 us; the launch traced here: 221 us
  waiting for transfers between devices  137 us (62%)
  starting transfers between devices  55 us (25%)
  Pallas kernels  18.4 us (8%)
  local copies, waits for them, and re-layouts  9.34 us (4%)
    all_to_all x3, waiting for transfers between devices, exchange(): moved = lax.all_to_all(chunks, EP, split_axis=0, concat_axis=0, tiled=True)  116 us
    all_to_all x3, starting transfers between devices, exchange(): moved = lax.all_to_all(chunks, EP, split_axis=0, concat_axis=0, tiled=True)  39.7 us
    ppermute x5, waiting for transfers between devices, shifted(): return lax.ppermute(a, axis, [(i, (i + k) % size) for i in range(size)])  20.9 us
    pallas_call x9, Pallas kernels, call(): pl.pallas_call(kernel, name=name, out_shape=shapes, in_specs=[SMEM] * sca...  18.4 us
    ppermute x5, starting transfers between devices, shifted(): return lax.ppermute(a, axis, [(i, (i + k) % size) for i in range(size)])  15.4 us
    unnamed x34, local copies, waits for them, and re-layouts  9.34 us
  transfers between devices with their start and end apart: 8, of which 5 were waited for; matrix products, arithmetic and copies ran while one was open for 0% of the time, Pallas kernels for 4%

profile of v3, /device:TPU:4, one launch (start us, length us, event | category | flops | bytes accessed | tf_op | source)
XLA Modules:
  0.0 220.9 jit_solution(273124955440380992)
XLA Ops:
  0.6 0.0 copy-start.14
  0.6 0.0 copy-start.11
  0.7 0.0 copy-start.12
  0.7 0.0 copy-start.9
  0.7 1.1 copy-done.9
  1.7 0.0 copy-start.13
  1.7 0.7 copy-done.13
  2.4 0.0 copy-start.15
  2.4 0.7 copy-done.15
  3.0 1.8 dispatch_second.1
  4.9 23.1 %all-to-all-start.1 = ((bf16[64,8,1024]{2,1,0:T(8,128)(2,1)}), bf16[64,8,1024]{2,1,0:T(8,128)(2,1)}, u32[]{:S(2)}, u32[]{:S(2)}) async-start(bf16[64,8,1024]{2,1,0:T(8,128)(2,1)} %bitcast.11), calls=%async_computation.1 | async-start | bytes 2097152 | tf_op jit(solution)/shard_map/all_to_all | solution.py:270
  27.9 0.0 copy-start
  28.0 0.0 copy-done.14
  28.0 0.0 copy-done.11
  28.0 0.0 copy-done.12
  28.0 0.0 copy-start.10
  28.0 1.2 copy-done.10
  29.2 1.0 dispatch_first.1
  30.1 0.0 copy-start.4
  30.2 1.0 copy-done.4
  31.1 50.5 %all-to-all-done.1 = bf16[64,8,1024]{2,1,0:T(8,128)(2,1)} async-done(((bf16[64,8,1024]{2,1,0:T(8,128)(2,1)}), bf16[64,8,1024]{2,1,0:T(8,128)(2,1)}, u32[]{:S(2)}, u32[]{:S(2)}) %all-to-all-start.1) | async-done | bytes 1048608 | tf_op jit(solution)/shard_map/all_to_all | solution.py:270
  81.6 7.5 %all-to-all-start = ((bf16[64,8,1024]{2,1,0:T(8,128)(2,1)}), bf16[64,8,1024]{2,1,0:T(8,128)(2,1)}, u32[]{:S(2)}, u32[]{:S(2)}) async-start(bf16[64,8,1024]{2,1,0:T(8,128)(2,1)} %bitcast.24), calls=%async_computation | async-start | bytes 2097152 | tf_op jit(solution)/shard_map/all_to_all | solution.py:270
  89.1 0.0 copy-start.2
  89.1 0.0 copy-done
  89.1 0.0 copy-start.5
  89.1 1.3 copy-done.5
  90.5 0.0 copy-start.6
  90.5 1.0 saved.1
  91.5 0.1 pad_add_fusion.at_ref
  91.6 0.0 copy-done.2
  91.6 0.2 copy-done.6
  91.8 3.9 %backward.1 = (bf16[8,128,1152]{2,1,0:T(8,128)(2,1)S(1)}, bf16[8,128,1152]{2,1,0:T(8,128)(2,1)S(1)}, bf16[256,128]{1,0:T(8,128)(2,1)S(1)}) custom-call(s32[3]{0:T(128)S(1)} %pad_add_fusion.at_ref, bf16[512,1024]{1,0:T(8,128)(2,1)} %bitcast.12.chunks_ref, bf16[384,2048]{1,0:T(8,128)(2,1)S(1)} %bitcast.22, bf16[256,2048]{1,0:T(8,128)(2,1)S(1)} %bitcast.26, ...), custom_call_target="tpu_custom_call" | custom-call | flops 2147483648 | bytes 12582912 | tf_op jit(solution)/shard_map/backward/pallas_call | solution.py:229
  95.7 1.9 collective-permute-start
  97.7 4.5 %collective-permute-done.b_ref = bf16[8,128,1152]{2,1,0:T(8,128)(2,1)S(1)} collective-permute-done((bf16[8,128,1152]{2,1,0:T(8,128)(2,1)S(1)}, bf16[8,128,1152]{2,1,0:T(8,128)(2,1)S(1)}, u32[]{:S(2)}, u32[]{:S(2)}) %collective-permute-start) | collective-permute-done | bytes 2359328 | tf_op jit(solution)/shard_map/ppermute | solution.py:275
  102.2 1.4 pairs.1
  103.5 0.0 copy-start.7
  103.5 0.8 copy-done.7
  104.3 2.3 %collective-permute-start.1 = (bf16[2,128,1152]{2,1,0:T(8,128)(2,1)}, bf16[2,128,1152]{2,1,0:T(8,128)(2,1)}, u32[]{:S(2)}, u32[]{:S(2)}) collective-permute-start(bf16[2,128,1152]{2,1,0:T(8,128)(2,1)} %get-tuple-element.30), channel_id=1, source_target_pairs={{0,4},{2,6},{4,0},{6,2},{1,5},{3,7},{5,1},{7,3},{8,12},{10,14},{12... | collective-permute-start | bytes 1769480 | tf_op jit(solution)/shard_map/ppermute | solution.py:275
  106.7 4.0 %collective-permute-start.2 = (bf16[2,128,1152]{2,1,0:T(8,128)(2,1)}, bf16[2,128,1152]{2,1,0:T(8,128)(2,1)}, u32[]{:S(2)}, u32[]{:S(2)}) collective-permute-start(bf16[2,128,1152]{2,1,0:T(8,128)(2,1)} %get-tuple-element.31), channel_id=1, source_target_pairs={{0,2},{2,4},{4,6},{6,0},{1,3},{3,5},{5,7},{7,1},{8,10},{10,12},{12... | collective-permute-start | bytes 1769480 | tf_op jit(solution)/shard_map/ppermute | solution.py:275
  110.7 2.0 collective-permute-start.3
  112.8 29.9 %all-to-all-done = bf16[64,8,1024]{2,1,0:T(8,128)(2,1)} async-done(((bf16[64,8,1024]{2,1,0:T(8,128)(2,1)}), bf16[64,8,1024]{2,1,0:T(8,128)(2,1)}, u32[]{:S(2)}, u32[]{:S(2)}) %all-to-all-start) | async-done | bytes 1048608 | tf_op jit(solution)/shard_map/all_to_all | solution.py:270
  142.7 0.0 collective-permute-done.1.refs_0_.refs_1_
  142.7 0.0 collective-permute-done.2.refs_1_.refs_2_
  142.7 0.0 collective-permute-done.3.refs_2_.refs_3_
  142.7 0.0 copy-start.3
  142.7 1.4 copy-done.3
  144.1 4.0 %forward.1 = bf16[512,1152]{1,0:T(8,128)(2,1)S(1)} custom-call(bf16[512,1024]{1,0:T(8,128)(2,1)} %bitcast.4.chunks_ref, bf16[2048,768]{1,0:T(8,128)(2,1)S(1)} %bitcast.20, bf16[384,2048]{1,0:T(8,128)(2,1)S(1)} %bitcast.23, bf16[256,128]{1,0:T(8,128)(2,1)S(1)} %get-tuple-element.27.value_ref, bf16[2,128,1152]{2,1,0:T(8,128)(2,1)} %collective-permute-done.1.refs_0_.refs_1_, ...), custom_call_target="tpu_custom_call" | custom-call | flops 2147483648 | bytes 7340032 | tf_op jit(solution)/shard_map/forward/pallas_call | solution.py:229
  148.2 0.0 copy-start.1
  148.2 1.0 copy-done.1
  149.2 0.0 copy-start.8
  149.2 0.0 copy-start.16
  149.2 9.2 %all-to-all-start.2 = ((bf16[64,8,1152]{2,1,0:T(8,128)(2,1)}), bf16[64,8,1152]{2,1,0:T(8,128)(2,1)}, u32[]{:S(2)}, u32[]{:S(2)}) async-start(bf16[64,8,1152]{2,1,0:T(8,128)(2,1)} %bitcast.21), calls=%async_computation.2 | async-start | bytes 2359296 | tf_op jit(solution)/shard_map/all_to_all | solution.py:270
  158.4 0.0 copy-done.8
  158.4 1.7 sums.1
  160.1 5.0 %collective-permute-start.4 = (bf16[128,1152]{1,0:T(8,128)(2,1)S(1)}, bf16[128,1152]{1,0:T(8,128)(2,1)S(1)}, u32[]{:S(2)}, u32[]{:S(2)}) collective-permute-start(bf16[128,1152]{1,0:T(8,128)(2,1)S(1)} %get-tuple-element.39), channel_id=1, source_target_pairs={{0,8},{8,0},{1,9},{9,1},{2,10},{10,2},{3,11},{11,3},{4,12},{12,4},... | collective-permute-start | bytes 884744 | tf_op jit(solution)/shard_map/ppermute | solution.py:275
  165.1 16.4 %collective-permute-done.4.b_ref = bf16[128,1152]{1,0:T(8,128)(2,1)S(1)} collective-permute-done((bf16[128,1152]{1,0:T(8,128)(2,1)S(1)}, bf16[128,1152]{1,0:T(8,128)(2,1)S(1)}, u32[]{:S(2)}, u32[]{:S(2)}) %collective-permute-start.4) | collective-permute-done | bytes 294944 | tf_op jit(solution)/shard_map/ppermute | solution.py:275
  181.6 0.8 finish.1
  182.4 35.8 %all-to-all-done.2 = bf16[64,8,1152]{2,1,0:T(8,128)(2,1)} async-done(((bf16[64,8,1152]{2,1,0:T(8,128)(2,1)}), bf16[64,8,1152]{2,1,0:T(8,128)(2,1)}, u32[]{:S(2)}, u32[]{:S(2)}) %all-to-all-start.2) | async-done | bytes 1179680 | tf_op jit(solution)/shard_map/all_to_all | solution.py:270
  218.1 0.0 copy-done.16
  218.1 2.8 %combine.1 = (bf16[128,2048]{1,0:T(8,128)(2,1)}, f32[1,128]{1,0:T(1,128)}) custom-call(bf16[512,1152]{1,0:T(8,128)(2,1)} %bitcast.15.chunks_ref, bf16[128,256]{1,0:T(8,128)(2,1)S(1)} %get-tuple-element.33.mix_ref, bf16[128,256]{1,0:T(8,128)(2,1)S(1)} %get-tuple-element.34.pick_ref, bf16[1,128]{1,0:T(2,128)(2,1)S(1)} %bitcast.32), custom_call_target="tpu_custom_call" | custom-call | flops 536870912 | bytes 2097152 | tf_op jit(solution)/shard_map/combine/pallas_call | solution.py:229
Async XLA Ops:
  0.6 27.3 %copy-start.14 = (s32[128,1]{0,1:T(1,128)S(1)}, s32[128,1]{0,1:T(1,128)}, u32[]{:S(2)}) copy-start(s32[128,1]{0,1:T(1,128)} %param.16) | copy-start | bytes 1540
  0.6 27.3 %copy-start.11 = (s32[128,1]{0,1:T(1,128)S(1)}, s32[128,1]{0,1:T(1,128)}, u32[]{:S(2)}) copy-start(s32[128,1]{0,1:T(1,128)} %param.10) | copy-start | bytes 1540
  0.7 27.3 %copy-start.12 = (bf16[128,1]{0,1:T(2,128)(2,1)S(1)}, bf16[128,1]{0,1:T(2,128)(2,1)}, u32[]{:S(2)}) copy-start(bf16[128,1]{0,1:T(2,128)(2,1)} %param.11) | copy-start | bytes 772
  0.7 1.1 copy-start.9
  1.7 0.7 copy-start.13
  2.4 0.7 copy-start.15
  4.9 76.8 %all-to-all-start.1 = ((bf16[64,8,1024]{2,1,0:T(8,128)(2,1)}), bf16[64,8,1024]{2,1,0:T(8,128)(2,1)}, u32[]{:S(2)}, u32[]{:S(2)}) async-start(bf16[64,8,1024]{2,1,0:T(8,128)(2,1)} %bitcast.11), calls=%async_computation.1 | async-start | bytes 2097152 | tf_op jit(solution)/shard_map/all_to_all | solution.py:270
  27.9 61.2 %copy-start = (bf16[1,2048,768]{2,1,0:T(8,128)(2,1)S(1)}, bf16[1,2048,768]{2,1,0:T(8,128)(2,1)}, u32[]{:S(2)}) copy-start(bf16[1,2048,768]{2,1,0:T(8,128)(2,1)} %param.12) | copy-start | bytes 9437188
  28.0 1.2 copy-start.10
  30.1 1.0 copy-start.4
  81.6 61.1 %all-to-all-start = ((bf16[64,8,1024]{2,1,0:T(8,128)(2,1)}), bf16[64,8,1024]{2,1,0:T(8,128)(2,1)}, u32[]{:S(2)}, u32[]{:S(2)}) async-start(bf16[64,8,1024]{2,1,0:T(8,128)(2,1)} %bitcast.24), calls=%async_computation | async-start | bytes 2097152 | tf_op jit(solution)/shard_map/all_to_all | solution.py:270
  89.1 2.5 %copy-start.2 = (bf16[1,384,2048]{2,1,0:T(8,128)(2,1)S(1)}, bf16[1,384,2048]{2,1,0:T(8,128)(2,1)}, u32[]{:S(2)}) copy-start(bf16[1,384,2048]{2,1,0:T(8,128)(2,1)} %param.13) | copy-start | bytes 4718596
  89.1 1.3 copy-start.5
  90.5 1.3 copy-start.6
  95.7 6.4 %collective-permute-start = (bf16[8,128,1152]{2,1,0:T(8,128)(2,1)S(1)}, bf16[8,128,1152]{2,1,0:T(8,128)(2,1)S(1)}, u32[]{:S(2)}, u32[]{:S(2)}) collective-permute-start(bf16[8,128,1152]{2,1,0:T(8,128)(2,1)S(1)} %get-tuple-element.29), channel_id=1, source_target_pairs={{0,1},{1,0},{2,3},{3,2},{4,5},{5,4},{6,7},{7,6},{8,9},{9,8},{10,11... | collective-permute-start | bytes 7077896 | tf_op jit(solution)/shard_map/ppermute | solution.py:275
  103.5 0.8 copy-start.7
  104.3 38.4 %collective-permute-start.1 = (bf16[2,128,1152]{2,1,0:T(8,128)(2,1)}, bf16[2,128,1152]{2,1,0:T(8,128)(2,1)}, u32[]{:S(2)}, u32[]{:S(2)}) collective-permute-start(bf16[2,128,1152]{2,1,0:T(8,128)(2,1)} %get-tuple-element.30), channel_id=1, source_target_pairs={{0,4},{2,6},{4,0},{6,2},{1,5},{3,7},{5,1},{7,3},{8,12},{10,14},{12... | collective-permute-start | bytes 1769480 | tf_op jit(solution)/shard_map/ppermute | solution.py:275
  106.7 36.0 %collective-permute-start.2 = (bf16[2,128,1152]{2,1,0:T(8,128)(2,1)}, bf16[2,128,1152]{2,1,0:T(8,128)(2,1)}, u32[]{:S(2)}, u32[]{:S(2)}) collective-permute-start(bf16[2,128,1152]{2,1,0:T(8,128)(2,1)} %get-tuple-element.31), channel_id=1, source_target_pairs={{0,2},{2,4},{4,6},{6,0},{1,3},{3,5},{5,7},{7,1},{8,10},{10,12},{12... | collective-permute-start | bytes 1769480 | tf_op jit(solution)/shard_map/ppermute | solution.py:275
  110.7 32.0 %collective-permute-start.3 = (bf16[2,128,1152]{2,1,0:T(8,128)(2,1)}, bf16[2,128,1152]{2,1,0:T(8,128)(2,1)}, u32[]{:S(2)}, u32[]{:S(2)}) collective-permute-start(bf16[2,128,1152]{2,1,0:T(8,128)(2,1)} %get-tuple-element.32), channel_id=1, source_target_pairs={{0,6},{2,0},{4,2},{6,4},{1,7},{3,1},{5,3},{7,5},{8,14},{10,8},{12,... | collective-permute-start | bytes 1769480 | tf_op jit(solution)/shard_map/ppermute | solution.py:275
  142.7 1.4 copy-start.3
  148.2 1.0 copy-start.1
  149.2 9.2 %copy-start.8 = (bf16[2,128,1152]{2,1,0:T(8,128)(2,1)S(1)}, bf16[2,128,1152]{2,1,0:T(8,128)(2,1)}, u32[]{:S(2)}) copy-start(bf16[2,128,1152]{2,1,0:T(8,128)(2,1)} %copy-done.7) | copy-start | bytes 1769476
  149.2 68.9 %copy-start.16 = (bf16[128,1]{0,1:T(2,128)(2,1)S(1)}, bf16[128,1]{0,1:T(2,128)(2,1)}, u32[]{:S(2)}) copy-start(bf16[128,1]{0,1:T(2,128)(2,1)} %param.17) | copy-start | bytes 772
  149.2 68.9 %all-to-all-start.2 = ((bf16[64,8,1152]{2,1,0:T(8,128)(2,1)}), bf16[64,8,1152]{2,1,0:T(8,128)(2,1)}, u32[]{:S(2)}, u32[]{:S(2)}) async-start(bf16[64,8,1152]{2,1,0:T(8,128)(2,1)} %bitcast.21), calls=%async_computation.2 | async-start | bytes 2359296 | tf_op jit(solution)/shard_map/all_to_all | solution.py:270
  160.1 21.5 %collective-permute-start.4 = (bf16[128,1152]{1,0:T(8,128)(2,1)S(1)}, bf16[128,1152]{1,0:T(8,128)(2,1)S(1)}, u32[]{:S(2)}, u32[]{:S(2)}) collective-permute-start(bf16[128,1152]{1,0:T(8,128)(2,1)S(1)} %get-tuple-element.39), channel_id=1, source_target_pairs={{0,8},{8,0},{1,9},{9,1},{2,10},{10,2},{3,11},{11,3},{4,12},{12,4},... | collective-permute-start | bytes 884744 | tf_op jit(solution)/shard_map/ppermute | solution.py:275

commit v4 on v3

--- a/solution.py
+++ b/solution.py
@@ -24,6 +24,16 @@
     return lax.dot_general(a, b, (((ca,), (cb,)), ((), ())), preferred_element_type=F32)
 
 
+def start_copy(source, target, semaphore):
+    copy = pltpu.make_async_copy(source, target, semaphore)
+    copy.start()
+    return copy
+
+
+def group(ref, g):
+    return ref.at[pl.ds(g * GROUP, GROUP)]
+
+
 def slots_of(routes, experts):
     tokens = routes.shape[1]
     onehot = (iota((experts, tokens), 0) == routes).astype(F32)
@@ -41,13 +51,15 @@
 GROUP = 256
 
 
-def from_chunks(chunks_ref, rows_ref, cap):
+def from_chunks(chunks_ref, rows_ref, cap, arrivals=None):
     width = chunks_ref.shape[1]
     pieces = CHUNK // cap
     per = GROUP // pieces
     order = (iota((GROUP, GROUP), 0) == order_of(GROUP, cap, 1)).astype(F32)
     order = order.astype(BF16)
     for g in range(chunks_ref.shape[0] // GROUP):
+        if arrivals:
+            arrivals[g].wait()
         part = dot(order, chunks_ref[g * GROUP : (g + 1) * GROUP, :]).astype(BF16)
         for q in range(pieces):
             rows_ref[g * per : (g + 1) * per, q * width : (q + 1) * width] = part[
@@ -55,10 +67,11 @@
             ]
 
 
-def to_chunks(rows_ref, chunks_ref, cap):
+def to_chunks(rows_ref, chunks_ref, out_ref, semaphores, cap):
     width = chunks_ref.shape[1]
     pieces = CHUNK // cap
     per = GROUP // pieces
+    copies = []
     order = (iota((GROUP, GROUP), 1) == order_of(GROUP, cap, 0)).astype(F32)
     order = order.astype(BF16)
     for g in range(chunks_ref.shape[0] // GROUP):
@@ -70,13 +83,20 @@
             axis=0,
         )
         chunks_ref[g * GROUP : (g + 1) * GROUP, :] = dot(order, part).astype(BF16)
-
-
-def send_rows(experts, cap, routes, weights, tokens_ref, chunks_ref):
+        copies.append(start_copy(group(chunks_ref, g), group(out_ref, g), semaphores.at[g]))
+    for copy in copies:
+        copy.wait()
+
+
+def send_rows(
+    experts, cap, routes, weights, tokens_ref, chunks_ref, out_ref, semaphores, arrival
+):
     tokens = routes.shape[1]
     width = chunks_ref.shape[1]
     _, slots = slots_of(routes, experts)
     base = routes * CHUNK + slots
+    copies = []
+    arrival.wait()
     for g in range(chunks_ref.shape[0] // GROUP):
         row = iota((GROUP, tokens), 0) + g * GROUP
         total = None
@@ -85,13 +105,43 @@
             term = dot(select, tokens_ref[:, q * width : (q + 1) * width])
             total = term if total is None else total + term
         chunks_ref[g * GROUP : (g + 1) * GROUP, :] = total.astype(BF16)
-    return slots
+        copies.append(start_copy(group(chunks_ref, g), group(out_ref, g), semaphores.at[g]))
+    return slots, copies
 
 
 def dispatch_second_kernel(
-    experts, cap, routes_ref, gates_ref, tokens_ref, chunks_ref
-):
-    send_rows(experts, cap, routes_ref[...], gates_ref[...].astype(F32), tokens_ref, chunks_ref)
+    experts,
+    cap,
+    routes_hbm,
+    gates_hbm,
+    tokens_hbm,
+    out_ref,
+    routes_ref,
+    gates_ref,
+    tokens_ref,
+    chunks_ref,
+    in_semaphores,
+    out_semaphores,
+):
+    pairs = ((routes_hbm, routes_ref), (gates_hbm, gates_ref), (tokens_hbm, tokens_ref))
+    first, second, third = [
+        start_copy(a, b, in_semaphores.at[k]) for k, (a, b) in enumerate(pairs)
+    ]
+    first.wait()
+    second.wait()
+    _, copies = send_rows(
+        experts,
+        cap,
+        routes_ref[...],
+        gates_ref[...].astype(F32),
+        tokens_ref,
+        chunks_ref,
+        out_ref,
+        out_semaphores,
+        third,
+    )
+    for copy in copies:
+        copy.wait()
 
 
 def dispatch_first_kernel(
@@ -100,14 +150,27 @@
     routes_ref,
     gates_ref,
     other_routes_ref,
+    tokens_hbm,
+    out_ref,
+    mix_ref,
+    pick_ref,
     tokens_ref,
     chunks_ref,
-    mix_ref,
-    pick_ref,
-):
+    in_semaphores,
+    out_semaphores,
+):
+    arrival = start_copy(tokens_hbm, tokens_ref, in_semaphores.at[0])
     routes = routes_ref[...]
-    slots = send_rows(
-        experts, cap, routes, jnp.ones(routes.shape, F32), tokens_ref, chunks_ref
+    slots, copies = send_rows(
+        experts,
+        cap,
+        routes,
+        jnp.ones(routes.shape, F32),
+        tokens_ref,
+        chunks_ref,
+        out_ref,
+        out_semaphores,
+        arrival,
     )
     place = iota((experts * cap, routes.shape[1]), 0)
     hit = place == routes * cap + slots
@@ -115,6 +178,8 @@
     routes = other_routes_ref[...]
     _, slots = slots_of(routes, experts)
     pick_ref[...] = (place == routes * cap + slots).astype(F32).T.astype(BF16)
+    for copy in copies:
+        copy.wait()
 
 
 def saved_kernel(x_ref, gu_ref, act_ref, gate_ref, up_ref):
@@ -167,20 +232,28 @@
             out_ref[n, :, 2 * hid :] = dot(rows_ref[:, columns], act_ref[...], 0, 0).astype(BF16)
 
 
-def forward_kernel(cap, chunks_ref, gu_ref, down_ref, value_ref, *refs):
-    out_ref, in_rows_ref, out_rows_ref = refs[-3:]
+def forward_kernel(cap, chunks_hbm, gu_ref, down_hbm, value_ref, *refs):
+    out_ref, chunks_ref, down_ref, back_ref, in_rows_ref, out_rows_ref = refs[-8:-2]
+    in_semaphores, out_semaphores = refs[-2:]
+    groups = chunks_ref.shape[0] // GROUP
+    arrivals = [
+        start_copy(group(chunks_hbm, g), group(chunks_ref, g), in_semaphores.at[g])
+        for g in range(groups)
+    ]
+    down_arrival = start_copy(down_hbm, down_ref, in_semaphores.at[groups])
     model, hid = down_ref.shape[1], down_ref.shape[0]
-    from_chunks(chunks_ref, in_rows_ref, cap)
+    from_chunks(chunks_ref, in_rows_ref, cap, arrivals)
     both = dot(in_rows_ref[...], gu_ref[...])
     act = (jax.nn.silu(both[:, :hid]) * both[:, hid:]).astype(BF16)
     width = chunks_ref.shape[1]
+    down_arrival.wait()
     for q in range(model // width):
         at = q * (width + EXTRA)
         out_rows_ref[:, at : at + width] = dot(
             act, down_ref[:, q * width : (q + 1) * width]
         ).astype(BF16)
         out_rows_ref[:, at + width : at + width + EXTRA] = value_ref[...]
-    to_chunks(out_rows_ref, out_ref, cap)
+    to_chunks(out_rows_ref, back_ref, out_ref, out_semaphores, cap)
 
 
 def combine_kernel(
@@ -222,18 +295,41 @@
 VMEM = pl.BlockSpec(memory_space=pltpu.VMEM)
 SMEM = pl.BlockSpec(memory_space=pltpu.SMEM)
 ANY = pl.BlockSpec(memory_space=pl.ANY)
-
-
-def call(kernel, name, outs, args, scratch=(), scalars=0, after=(), flops=0, moved=0):
-    shapes = [jax.ShapeDtypeStruct(*o) for o in outs]
+HBM = pl.BlockSpec(memory_space=pltpu.HBM)
+
+
+def call(
+    kernel,
+    name,
+    outs,
+    args,
+    scratch=(),
+    scalars=0,
+    after=(),
+    hbm_in=(),
+    hbm_out=(),
+    semaphores=(),
+    limit=16,
+    flops=0,
+    moved=0,
+):
+    shapes = [
+        pltpu.HBM(*o) if k in hbm_out else jax.ShapeDtypeStruct(*o) for k, o in enumerate(outs)
+    ]
+    args = [
+        pltpu.with_memory_space_constraint(a, pltpu.HBM) if k in hbm_in else a
+        for k, a in enumerate(args)
+    ]
+    spaces = [SMEM if k < scalars else HBM if k in hbm_in else VMEM for k in range(len(args))]
     result = pl.pallas_call(
         kernel,
         name=name,
         out_shape=shapes,
-        in_specs=[SMEM] * scalars + [VMEM] * (len(args) - scalars) + [ANY] * len(after),
-        out_specs=[VMEM] * len(outs),
-        scratch_shapes=[pltpu.VMEM(*s) for s in scratch],
-        compiler_params=pltpu.CompilerParams(vmem_limit_bytes=24 * 2**20),
+        in_specs=spaces + [ANY] * len(after),
+        out_specs=[HBM if k in hbm_out else VMEM for k in range(len(outs))],
+        scratch_shapes=[pltpu.VMEM(*s) for s in scratch]
+        + [pltpu.SemaphoreType.DMA((n,)) for n in semaphores],
+        compiler_params=pltpu.CompilerParams(vmem_limit_bytes=limit * 2**20),
         cost_estimate=pl.CostEstimate(flops=flops, bytes_accessed=moved, transcendentals=0),
     )(*args, *after)
     return result[0] if len(outs) == 1 else result
@@ -260,6 +356,7 @@
     hid = down.shape[0]
     block = model // (4 * n_x)
     MB = 2**20
+    groups = experts * CHUNK // GROUP
 
     def row(a):
         return a.reshape(1, tokens)
@@ -289,6 +386,15 @@
         "dispatch_second",
         [chunk_shape],
         (row(routes_second), row(gates_second), upstream),
+        scratch=(
+            ((1, tokens), I32),
+            ((1, tokens), BF16),
+            ((tokens, model), BF16),
+            chunk_shape,
+        ),
+        hbm_in=(0, 1, 2),
+        hbm_out=(0,),
+        semaphores=(3, groups),
         flops=2**29,
         moved=2 * MB,
     )
@@ -298,6 +404,10 @@
         "dispatch_first",
         [chunk_shape, pick_shape, pick_shape],
         (row(routes_first), row(gates_first), row(routes_second), tokens_first),
+        scratch=(((tokens, model), BF16), chunk_shape),
+        hbm_in=(3,),
+        hbm_out=(0,),
+        semaphores=(1, groups),
         flops=2**29,
         moved=2 * MB,
     )
@@ -342,8 +452,11 @@
         "forward",
         [back_shape],
         (got_first, gu, down, value),
-        scratch=(row_shape, back_rows),
+        scratch=(chunk_shape, ((hid, model), BF16), back_shape, row_shape, back_rows),
         after=tuple(terms),
+        hbm_in=(0, 2),
+        hbm_out=(0,),
+        semaphores=(groups + 1, groups),
         flops=2**31,
         moved=7 * MB,
     )

time: 222 us -> 217 us (0.977)
  the two profiles are of different devices: /device:TPU:4 before, /device:TPU:1 now
where the time goes in v4:
time: 217 us; the launch traced here: 213 us
  waiting for transfers between devices  124 us (57%)
  starting transfers between devices  65.4 us (30%)
  Pallas kernels  20.6 us (9%)
  local copies, waits for them, and re-layouts  2.19 us (1%)
    all_to_all x3, waiting for transfers between devices, exchange(): moved = lax.all_to_all(chunks, EP, split_axis=0, concat_axis=0, tiled=True)  104 us
    all_to_all x3, starting transfers between devices, exchange(): moved = lax.all_to_all(chunks, EP, split_axis=0, concat_axis=0, tiled=True)  46.3 us
    pallas_call x9, Pallas kernels, call(): pl.pallas_call(kernel, name=name, out_shape=shapes, in_specs=spaces + [AN...  20.6 us
    ppermute x5, waiting for transfers between devices, shifted(): return lax.ppermute(a, axis, [(i, (i + k) % size) for i in range(size)])  19.8 us
    ppermute x5, starting transfers between devices, shifted(): return lax.ppermute(a, axis, [(i, (i + k) % size) for i in range(size)])  19 us
  transfers between devices with their start and end apart: 8, of which 5 were waited for; matrix products, arithmetic and copies ran while one was open for 0% of the time, Pallas kernels for 5%

profile of v4, /device:TPU:1, one launch (start us, length us, event | category | flops | bytes accessed | tf_op | source)
XLA Modules:
  0.0 212.7 jit_solution(1482581957725162011)
XLA Ops:
  0.6 0.0 copy-start.7
  0.6 0.0 copy-start.5
  0.7 0.0 copy-start.6
  0.7 2.6 %dispatch_second.1 = bf16[512,1024]{1,0:T(8,128)(2,1)} custom-call(s32[1,128]{1,0:T(1,128)} %bitcast.28, bf16[1,128]{1,0:T(2,128)(2,1)} %bitcast.30, bf16[128,2048]{1,0:T(8,128)(2,1)} %tokens_hbm.3), custom_call_target="tpu_custom_call" | custom-call | flops 536870912 | bytes 2097152 | tf_op jit(solution)/shard_map/dispatch_second/pallas_call | solution.py:324
  3.3 23.6 %all-to-all-start.1 = ((bf16[64,8,1024]{2,1,0:T(8,128)(2,1)}), bf16[64,8,1024]{2,1,0:T(8,128)(2,1)}, u32[]{:S(2)}, u32[]{:S(2)}) async-start(bf16[64,8,1024]{2,1,0:T(8,128)(2,1)} %bitcast.34), calls=%async_computation.1 | async-start | bytes 2097152 | tf_op jit(solution)/shard_map/all_to_all | solution.py:367
  26.9 0.0 copy-start
  27.0 0.0 copy-done.7
  27.0 0.0 copy-done.5
  27.0 0.0 copy-done.6
  27.0 2.7 %dispatch_first.1 = (bf16[512,1024]{1,0:T(8,128)(2,1)}, bf16[128,256]{1,0:T(8,128)(2,1)S(1)}, bf16[128,256]{1,0:T(8,128)(2,1)S(1)}) custom-call(s32[1,128]{1,0:T(1,128)S(1)} %bitcast.26, bf16[1,128]{1,0:T(2,128)(2,1)S(1)} %bitcast.27, s32[1,128]{1,0:T(1,128)S(1)} %bitcast.29, bf16[128,2048]{1,0:T(8,128)(2,1)} %tokens_hbm.2), custom_call_target="tpu_custom_call" | custom-call | flops 536870912 | bytes 2097152 | tf_op jit(solution)/shard_map/dispatch_first/pallas_call | solution.py:324
  29.7 47.7 %all-to-all-done.1 = bf16[64,8,1024]{2,1,0:T(8,128)(2,1)} async-done(((bf16[64,8,1024]{2,1,0:T(8,128)(2,1)}), bf16[64,8,1024]{2,1,0:T(8,128)(2,1)}, u32[]{:S(2)}, u32[]{:S(2)}) %all-to-all-start.1) | async-done | bytes 1048608 | tf_op jit(solution)/shard_map/all_to_all | solution.py:367
  77.4 10.5 %all-to-all-start = ((bf16[64,8,1024]{2,1,0:T(8,128)(2,1)}), bf16[64,8,1024]{2,1,0:T(8,128)(2,1)}, u32[]{:S(2)}, u32[]{:S(2)}) async-start(bf16[64,8,1024]{2,1,0:T(8,128)(2,1)} %bitcast.33), calls=%async_computation | async-start | bytes 2097152 | tf_op jit(solution)/shard_map/all_to_all | solution.py:367
  87.9 0.0 copy-start.1
  87.9 0.0 copy-done
  87.9 0.0 copy-start.2
  87.9 1.3 copy-done.2
  89.3 1.0 saved.1
  90.3 0.1 pad_add_fusion.at_ref
  90.4 0.0 copy-done.1
  90.4 3.9 %backward.1 = (bf16[8,128,1152]{2,1,0:T(8,128)(2,1)S(1)}, bf16[8,128,1152]{2,1,0:T(8,128)(2,1)S(1)}, bf16[256,128]{1,0:T(8,128)(2,1)S(1)}) custom-call(s32[3]{0:T(128)S(1)} %pad_add_fusion.at_ref, bf16[512,1024]{1,0:T(8,128)(2,1)} %bitcast.12.chunks_ref, bf16[384,2048]{1,0:T(8,128)(2,1)S(1)} %bitcast.22, bf16[256,2048]{1,0:T(8,128)(2,1)S(1)} %bitcast.25, ...), custom_call_target="tpu_custom_call" | custom-call | flops 2147483648 | bytes 12582912 | tf_op jit(solution)/shard_map/backward/pallas_call | solution.py:324
  94.2 3.1 %collective-permute-start = (bf16[8,128,1152]{2,1,0:T(8,128)(2,1)S(1)}, bf16[8,128,1152]{2,1,0:T(8,128)(2,1)S(1)}, u32[]{:S(2)}, u32[]{:S(2)}) collective-permute-start(bf16[8,128,1152]{2,1,0:T(8,128)(2,1)S(1)} %get-tuple-element.29), channel_id=1, source_target_pairs={{0,1},{1,0},{2,3},{3,2},{4,5},{5,4},{6,7},{7,6},{8,9},{9,8},{10,11... | collective-permute-start | bytes 7077896 | tf_op jit(solution)/shard_map/ppermute | solution.py:372
  97.3 4.1 %collective-permute-done.b_ref = bf16[8,128,1152]{2,1,0:T(8,128)(2,1)S(1)} collective-permute-done((bf16[8,128,1152]{2,1,0:T(8,128)(2,1)S(1)}, bf16[8,128,1152]{2,1,0:T(8,128)(2,1)S(1)}, u32[]{:S(2)}, u32[]{:S(2)}) %collective-permute-start) | collective-permute-done | bytes 2359328 | tf_op jit(solution)/shard_map/ppermute | solution.py:372
  101.5 1.4 pairs.1
  102.8 0.0 copy-start.3
  102.8 0.8 copy-done.3
  103.7 4.7 %collective-permute-start.1 = (bf16[2,128,1152]{2,1,0:T(8,128)(2,1)}, bf16[2,128,1152]{2,1,0:T(8,128)(2,1)}, u32[]{:S(2)}, u32[]{:S(2)}) collective-permute-start(bf16[2,128,1152]{2,1,0:T(8,128)(2,1)} %get-tuple-element.30), channel_id=1, source_target_pairs={{0,4},{2,6},{4,0},{6,2},{1,5},{3,7},{5,1},{7,3},{8,12},{10,14},{12... | collective-permute-start | bytes 1769480 | tf_op jit(solution)/shard_map/ppermute | solution.py:372
  108.4 2.2 %collective-permute-start.2 = (bf16[2,128,1152]{2,1,0:T(8,128)(2,1)}, bf16[2,128,1152]{2,1,0:T(8,128)(2,1)}, u32[]{:S(2)}, u32[]{:S(2)}) collective-permute-start(bf16[2,128,1152]{2,1,0:T(8,128)(2,1)} %get-tuple-element.31), channel_id=1, source_target_pairs={{0,2},{2,4},{4,6},{6,0},{1,3},{3,5},{5,7},{7,1},{8,10},{10,12},{12... | collective-permute-start | bytes 1769480 | tf_op jit(solution)/shard_map/ppermute | solution.py:372
  110.6 4.3 %collective-permute-start.3 = (bf16[2,128,1152]{2,1,0:T(8,128)(2,1)}, bf16[2,128,1152]{2,1,0:T(8,128)(2,1)}, u32[]{:S(2)}, u32[]{:S(2)}) collective-permute-start(bf16[2,128,1152]{2,1,0:T(8,128)(2,1)} %get-tuple-element.32), channel_id=1, source_target_pairs={{0,6},{2,0},{4,2},{6,4},{1,7},{3,1},{5,3},{7,5},{8,14},{10,8},{12,... | collective-permute-start | bytes 1769480 | tf_op jit(solution)/shard_map/ppermute | solution.py:372
  114.9 23.5 %all-to-all-done = bf16[64,8,1024]{2,1,0:T(8,128)(2,1)} async-done(((bf16[64,8,1024]{2,1,0:T(8,128)(2,1)}), bf16[64,8,1024]{2,1,0:T(8,128)(2,1)}, u32[]{:S(2)}, u32[]{:S(2)}) %all-to-all-start) | async-done | bytes 1048608 | tf_op jit(solution)/shard_map/all_to_all | solution.py:367
  138.4 0.0 collective-permute-done.1.refs_0_.refs_1_
  138.4 0.0 collective-permute-done.2.refs_1_.refs_2_
  138.4 0.0 collective-permute-done.3.refs_2_.refs_3_
  138.4 5.0 %forward.1 = bf16[512,1152]{1,0:T(8,128)(2,1)} custom-call(bf16[512,1024]{1,0:T(8,128)(2,1)} %bitcast.4.chunks_hbm, bf16[2048,768]{1,0:T(8,128)(2,1)S(1)} %bitcast.20, bf16[384,2048]{1,0:T(8,128)(2,1)} %bitcast.21, bf16[256,128]{1,0:T(8,128)(2,1)S(1)} %get-tuple-element.27.value_ref, bf16[2,128,1152]{2,1,0:T(8,128)(2,1)} %collective-permute-done.1.refs_0_.refs_1_, ...), custom_call_target="tpu_custom_call" | custom-call | flops 2147483648 | bytes 7340032 | tf_op jit(solution)/shard_map/forward/pallas_call | solution.py:324
  143.4 0.0 copy-start.4
  143.4 0.0 copy-start.8
  143.4 12.2 %all-to-all-start.2 = ((bf16[64,8,1152]{2,1,0:T(8,128)(2,1)}), bf16[64,8,1152]{2,1,0:T(8,128)(2,1)S(1)}, u32[]{:S(2)}, u32[]{:S(2)}) async-start(bf16[64,8,1152]{2,1,0:T(8,128)(2,1)} %bitcast.32), calls=%async_computation.2 | async-start | bytes 2359296 | tf_op jit(solution)/shard_map/all_to_all | solution.py:367
  155.6 0.0 copy-done.4
  155.6 1.7 sums.1
  157.4 4.8 %collective-permute-start.4 = (bf16[128,1152]{1,0:T(8,128)(2,1)S(1)}, bf16[128,1152]{1,0:T(8,128)(2,1)S(1)}, u32[]{:S(2)}, u32[]{:S(2)}) collective-permute-start(bf16[128,1152]{1,0:T(8,128)(2,1)S(1)} %get-tuple-element.39), channel_id=1, source_target_pairs={{0,8},{8,0},{1,9},{9,1},{2,10},{10,2},{3,11},{11,3},{4,12},{12,4},... | collective-permute-start | bytes 884744 | tf_op jit(solution)/shard_map/ppermute | solution.py:372
  162.1 15.7 %collective-permute-done.4.b_ref = bf16[128,1152]{1,0:T(8,128)(2,1)S(1)} collective-permute-done((bf16[128,1152]{1,0:T(8,128)(2,1)S(1)}, bf16[128,1152]{1,0:T(8,128)(2,1)S(1)}, u32[]{:S(2)}, u32[]{:S(2)}) %collective-permute-start.4) | collective-permute-done | bytes 294944 | tf_op jit(solution)/shard_map/ppermute | solution.py:372
  177.8 0.8 finish.1
  178.6 32.6 %all-to-all-done.2 = bf16[64,8,1152]{2,1,0:T(8,128)(2,1)S(1)} async-done(((bf16[64,8,1152]{2,1,0:T(8,128)(2,1)}), bf16[64,8,1152]{2,1,0:T(8,128)(2,1)S(1)}, u32[]{:S(2)}, u32[]{:S(2)}) %all-to-all-start.2) | async-done | bytes 1179680 | tf_op jit(solution)/shard_map/all_to_all | solution.py:367
  211.2 0.0 copy-done.8
  211.2 1.5 combine.1
Async XLA Ops:
  0.6 26.3 %copy-start.7 = (s32[128,1]{0,1:T(1,128)S(1)}, s32[128,1]{0,1:T(1,128)}, u32[]{:S(2)}) copy-start(s32[128,1]{0,1:T(1,128)} %param.16) | copy-start | bytes 1540
  0.6 26.3 %copy-start.5 = (s32[128,1]{0,1:T(1,128)S(1)}, s32[128,1]{0,1:T(1,128)}, u32[]{:S(2)}) copy-start(s32[128,1]{0,1:T(1,128)} %param.10) | copy-start | bytes 1540
  0.7 26.3 %copy-start.6 = (bf16[128,1]{0,1:T(2,128)(2,1)S(1)}, bf16[128,1]{0,1:T(2,128)(2,1)}, u32[]{:S(2)}) copy-start(bf16[128,1]{0,1:T(2,128)(2,1)} %param.11) | copy-start | bytes 772
  3.3 74.1 %all-to-all-start.1 = ((bf16[64,8,1024]{2,1,0:T(8,128)(2,1)}), bf16[64,8,1024]{2,1,0:T(8,128)(2,1)}, u32[]{:S(2)}, u32[]{:S(2)}) async-start(bf16[64,8,1024]{2,1,0:T(8,128)(2,1)} %bitcast.34), calls=%async_computation.1 | async-start | bytes 2097152 | tf_op jit(solution)/shard_map/all_to_all | solution.py:367
  26.9 61.0 %copy-start = (bf16[1,2048,768]{2,1,0:T(8,128)(2,1)S(1)}, bf16[1,2048,768]{2,1,0:T(8,128)(2,1)}, u32[]{:S(2)}) copy-start(bf16[1,2048,768]{2,1,0:T(8,128)(2,1)} %param.12) | copy-start | bytes 9437188
  77.4 61.0 %all-to-all-start = ((bf16[64,8,1024]{2,1,0:T(8,128)(2,1)}), bf16[64,8,1024]{2,1,0:T(8,128)(2,1)}, u32[]{:S(2)}, u32[]{:S(2)}) async-start(bf16[64,8,1024]{2,1,0:T(8,128)(2,1)} %bitcast.33), calls=%async_computation | async-start | bytes 2097152 | tf_op jit(solution)/shard_map/all_to_all | solution.py:367
  87.9 2.5 %copy-start.1 = (bf16[1,384,2048]{2,1,0:T(8,128)(2,1)S(1)}, bf16[1,384,2048]{2,1,0:T(8,128)(2,1)}, u32[]{:S(2)}) copy-start(bf16[1,384,2048]{2,1,0:T(8,128)(2,1)} %param.13) | copy-start | bytes 4718596
  87.9 1.3 copy-start.2
  94.2 7.2 %collective-permute-start = (bf16[8,128,1152]{2,1,0:T(8,128)(2,1)S(1)}, bf16[8,128,1152]{2,1,0:T(8,128)(2,1)S(1)}, u32[]{:S(2)}, u32[]{:S(2)}) collective-permute-start(bf16[8,128,1152]{2,1,0:T(8,128)(2,1)S(1)} %get-tuple-element.29), channel_id=1, source_target_pairs={{0,1},{1,0},{2,3},{3,2},{4,5},{5,4},{6,7},{7,6},{8,9},{9,8},{10,11... | collective-permute-start | bytes 7077896 | tf_op jit(solution)/shard_map/ppermute | solution.py:372
  102.8 0.8 copy-start.3
  103.7 34.7 %collective-permute-start.1 = (bf16[2,128,1152]{2,1,0:T(8,128)(2,1)}, bf16[2,128,1152]{2,1,0:T(8,128)(2,1)}, u32[]{:S(2)}, u32[]{:S(2)}) collective-permute-start(bf16[2,128,1152]{2,1,0:T(8,128)(2,1)} %get-tuple-element.30), channel_id=1, source_target_pairs={{0,4},{2,6},{4,0},{6,2},{1,5},{3,7},{5,1},{7,3},{8,12},{10,14},{12... | collective-permute-start | bytes 1769480 | tf_op jit(solution)/shard_map/ppermute | solution.py:372
  108.4 30.0 %collective-permute-start.2 = (bf16[2,128,1152]{2,1,0:T(8,128)(2,1)}, bf16[2,128,1152]{2,1,0:T(8,128)(2,1)}, u32[]{:S(2)}, u32[]{:S(2)}) collective-permute-start(bf16[2,128,1152]{2,1,0:T(8,128)(2,1)} %get-tuple-element.31), channel_id=1, source_target_pairs={{0,2},{2,4},{4,6},{6,0},{1,3},{3,5},{5,7},{7,1},{8,10},{10,12},{12... | collective-permute-start | bytes 1769480 | tf_op jit(solution)/shard_map/ppermute | solution.py:372
  110.6 27.8 %collective-permute-start.3 = (bf16[2,128,1152]{2,1,0:T(8,128)(2,1)}, bf16[2,128,1152]{2,1,0:T(8,128)(2,1)}, u32[]{:S(2)}, u32[]{:S(2)}) collective-permute-start(bf16[2,128,1152]{2,1,0:T(8,128)(2,1)} %get-tuple-element.32), channel_id=1, source_target_pairs={{0,6},{2,0},{4,2},{6,4},{1,7},{3,1},{5,3},{7,5},{8,14},{10,8},{12,... | collective-permute-start | bytes 1769480 | tf_op jit(solution)/shard_map/ppermute | solution.py:372
  143.4 12.2 %copy-start.4 = (bf16[2,128,1152]{2,1,0:T(8,128)(2,1)S(1)}, bf16[2,128,1152]{2,1,0:T(8,128)(2,1)}, u32[]{:S(2)}) copy-start(bf16[2,128,1152]{2,1,0:T(8,128)(2,1)} %copy-done.3) | copy-start | bytes 1769476
  143.4 67.8 %copy-start.8 = (bf16[128,1]{0,1:T(2,128)(2,1)S(1)}, bf16[128,1]{0,1:T(2,128)(2,1)}, u32[]{:S(2)}) copy-start(bf16[128,1]{0,1:T(2,128)(2,1)} %param.17) | copy-start | bytes 772
  143.4 67.8 %all-to-all-start.2 = ((bf16[64,8,1152]{2,1,0:T(8,128)(2,1)}), bf16[64,8,1152]{2,1,0:T(8,128)(2,1)S(1)}, u32[]{:S(2)}, u32[]{:S(2)}) async-start(bf16[64,8,1152]{2,1,0:T(8,128)(2,1)} %bitcast.32), calls=%async_computation.2 | async-start | bytes 2359296 | tf_op jit(solution)/shard_map/all_to_all | solution.py:367
  157.4 20.5 %collective-permute-start.4 = (bf16[128,1152]{1,0:T(8,128)(2,1)S(1)}, bf16[128,1152]{1,0:T(8,128)(2,1)S(1)}, u32[]{:S(2)}, u32[]{:S(2)}) collective-permute-start(bf16[128,1152]{1,0:T(8,128)(2,1)S(1)} %get-tuple-element.39), channel_id=1, source_target_pairs={{0,8},{8,0},{1,9},{9,1},{2,10},{10,2},{3,11},{11,3},{4,12},{12,4},... | collective-permute-start | bytes 884744 | tf_op jit(solution)/shard_map/ppermute | solution.py:372

commit v5 on v4

--- a/solution.py
+++ b/solution.py
@@ -13,7 +13,7 @@
 EP = ("yl", "z")
 ALL = ("yl", "z", "yh", "x", "core")
 CHUNK = 8
-EXTRA = 128
+EARLY = 3
 
 
 def iota(shape, dim):
@@ -149,16 +149,10 @@
     cap,
     routes_ref,
     gates_ref,
-    other_routes_ref,
     tokens_hbm,
-    out_ref,
-    mix_ref,
-    pick_ref,
-    tokens_ref,
-    chunks_ref,
-    in_semaphores,
-    out_semaphores,
+    *refs,
 ):
+    out_ref, mix_ref, tokens_ref, chunks_ref, in_semaphores, out_semaphores = refs[-6:]
     arrival = start_copy(tokens_hbm, tokens_ref, in_semaphores.at[0])
     routes = routes_ref[...]
     slots, copies = send_rows(
@@ -175,9 +169,6 @@
     place = iota((experts * cap, routes.shape[1]), 0)
     hit = place == routes * cap + slots
     mix_ref[...] = jnp.where(hit, gates_ref[...].astype(F32), 0.0).T.astype(BF16)
-    routes = other_routes_ref[...]
-    _, slots = slots_of(routes, experts)
-    pick_ref[...] = (place == routes * cap + slots).astype(F32).T.astype(BF16)
     for copy in copies:
         copy.wait()
 
@@ -213,14 +204,11 @@
     core, y, x = at_ref[0], at_ref[1], at_ref[2]
     from_chunks(chunks_ref, rows_ref, cap)
     scaled = dot(rows_ref[...], down_ref[...], 1, 1)
-    value = jnp.sum(scaled * act_ref[...].astype(F32), axis=1, keepdims=True)
-    lane = iota(value_ref.shape, 1)
-    parts = jnp.zeros(value_ref.shape, F32)
-    for k in range(3):
-        part = value.astype(BF16).astype(F32)
-        parts = jnp.where(lane == k, part, parts)
-        value = value - part
-    value_ref[...] = parts.astype(BF16)
+    product = scaled * act_ref[...].astype(F32)
+    folded = product[:, :128]
+    for k in range(1, hid // 128):
+        folded = folded + product[:, k * 128 : (k + 1) * 128]
+    value_ref[...] = jnp.sum(folded.T, axis=0, keepdims=True)
     both_ref[:, :hid] = (scaled * gate_ref[...]).astype(BF16)
     both_ref[:, hid:] = (scaled * up_ref[...]).astype(BF16)
     n_x = keep_ref.shape[0] // 2
@@ -232,7 +220,7 @@
             out_ref[n, :, 2 * hid :] = dot(rows_ref[:, columns], act_ref[...], 0, 0).astype(BF16)
 
 
-def forward_kernel(cap, chunks_hbm, gu_ref, down_hbm, value_ref, *refs):
+def forward_kernel(cap, chunks_hbm, gu_ref, down_hbm, *refs):
     out_ref, chunks_ref, down_ref, back_ref, in_rows_ref, out_rows_ref = refs[-8:-2]
     in_semaphores, out_semaphores = refs[-2:]
     groups = chunks_ref.shape[0] // GROUP
@@ -241,34 +229,38 @@
         for g in range(groups)
     ]
     down_arrival = start_copy(down_hbm, down_ref, in_semaphores.at[groups])
-    model, hid = down_ref.shape[1], down_ref.shape[0]
+    hid = down_ref.shape[0]
     from_chunks(chunks_ref, in_rows_ref, cap, arrivals)
     both = dot(in_rows_ref[...], gu_ref[...])
     act = (jax.nn.silu(both[:, :hid]) * both[:, hid:]).astype(BF16)
-    width = chunks_ref.shape[1]
     down_arrival.wait()
-    for q in range(model // width):
-        at = q * (width + EXTRA)
-        out_rows_ref[:, at : at + width] = dot(
-            act, down_ref[:, q * width : (q + 1) * width]
-        ).astype(BF16)
-        out_rows_ref[:, at + width : at + width + EXTRA] = value_ref[...]
+    out_rows_ref[...] = dot(act, down_ref[...]).astype(BF16)
     to_chunks(out_rows_ref, back_ref, out_ref, out_semaphores, cap)
 
 
-def combine_kernel(
-    cap, chunks_ref, mix_ref, pick_ref, gates_ref, out_ref, grads_ref, rows_ref
-):
+def combine_kernel(cap, chunks_ref, mix_ref, out_ref, rows_ref):
     from_chunks(chunks_ref, rows_ref, cap)
-    width = chunks_ref.shape[1] - EXTRA
-    for q in range(CHUNK // cap):
-        at = q * (width + EXTRA)
-        out_ref[:, q * width : (q + 1) * width] = dot(
-            mix_ref[...], rows_ref[:, at : at + width]
-        ).astype(BF16)
-    value = dot(pick_ref[...], rows_ref[:, width : width + EXTRA])
-    value = jnp.sum(value.T, axis=0, keepdims=True)
-    grads_ref[...] = value / gates_ref[...].astype(F32)
+    out_ref[...] = dot(mix_ref[...], rows_ref[...]).astype(BF16)
+
+
+def gate_grad_kernel(cap, n_z, bits, at_ref, a_ref, b_ref, routes_ref, gates_ref, out_ref):
+    values = jnp.concatenate([a_ref[...], b_ref[...]], axis=0)
+    experts, places = values.shape
+    routes = routes_ref[...]
+    _, slots = slots_of(routes, experts)
+    home = at_ref[0] * n_z + at_ref[1]
+    apart = jnp.bitwise_xor(routes, home)
+    source = jnp.zeros_like(routes)
+    for r, bit in enumerate(bits):
+        source = source + jnp.bitwise_and(jnp.right_shift(apart, bit), 1) * 2**r
+    hit = (iota((experts, routes.shape[1]), 0) == source).astype(F32)
+    lane = iota((experts, places), 1)
+    total = jnp.zeros(out_ref.shape, F32)
+    for c in range(cap):
+        mine = jnp.sum(jnp.where(lane == home * cap + c, values, 0.0), axis=1, keepdims=True)
+        here = jnp.sum(hit * mine, axis=0, keepdims=True)
+        total = total + jnp.where(slots == c, here, 0.0)
+    out_ref[...] = total / gates_ref[...].astype(F32)
 
 
 def pair_kernel(a_ref, b_ref, *out_refs):
@@ -372,11 +364,7 @@
         return lax.ppermute(a, axis, [(i, (i + k) % size) for i in range(size)])
 
     chunk_shape = ((experts * CHUNK, width), BF16)
-    back_shape = ((experts * CHUNK, width + EXTRA), BF16)
     row_shape = ((places, model), BF16)
-    back_rows = ((places, model + CHUNK // cap * EXTRA), BF16)
-    extra_shape = ((places, EXTRA), BF16)
-    pick_shape = ((tokens, places), BF16)
     here = jnp.stack(
         [lax.axis_index("core"), lax.axis_index("yh"), lax.axis_index("x")]
     ).astype(I32)
@@ -399,18 +387,6 @@
         moved=2 * MB,
     )
     got_second = exchange(send_second)
-    send_first, mix, pick = call(
-        functools.partial(dispatch_first_kernel, experts, cap),
-        "dispatch_first",
-        [chunk_shape, pick_shape, pick_shape],
-        (row(routes_first), row(gates_first), row(routes_second), tokens_first),
-        scratch=(((tokens, model), BF16), chunk_shape),
-        hbm_in=(3,),
-        hbm_out=(0,),
-        semaphores=(1, groups),
-        flops=2**29,
-        moved=2 * MB,
-    )
     act, by_gate, by_up = call(
         saved_kernel,
         "saved",
@@ -419,13 +395,26 @@
         flops=2**30,
         moved=6 * MB,
     )
+    send_first, mix = call(
+        functools.partial(dispatch_first_kernel, experts, cap),
+        "dispatch_first",
+        [chunk_shape, ((tokens, places), BF16)],
+        (row(routes_first), row(gates_first), tokens_first),
+        scratch=(((tokens, model), BF16), chunk_shape),
+        after=(by_up,),
+        hbm_in=(2,),
+        hbm_out=(0,),
+        semaphores=(1, groups),
+        flops=2**29,
+        moved=2 * MB,
+    )
     got_first = exchange(send_first)
 
     half = ((2 * n_x, block, 3 * hid), BF16)
     keep, send, value = call(
         functools.partial(backward_kernel, cap),
         "backward",
-        [half, half, extra_shape],
+        [half, half, ((1, places), F32)],
         (here, got_second, down, x, act, by_gate, by_up),
         scratch=(row_shape, ((places, 2 * hid), BF16)),
         scalars=1,
@@ -447,13 +436,24 @@
         (near, far),
         moved=MB,
     )
+    n_z = lax.axis_size("z")
+    z_masks = [2**k for k in range(n_z.bit_length() - 1)]
+    steps = [("z", m) for m in z_masks[:2]] + [("yl", 1), ("yl", 2)]
+    steps += [("z", m) for m in z_masks[2:]]
+    bits = [m.bit_length() - 1 + (n_z.bit_length() - 1 if a == "yl" else 0) for a, m in steps]
+
+    def crossed(a, axis, mask):
+        return lax.ppermute(a, axis, [(i, i ^ mask) for i in range(lax.axis_size(axis))])
+
+    for step in steps[:EARLY]:
+        value = jnp.concatenate([value, crossed(value, *step)], axis=0)
     send_back = call(
         functools.partial(forward_kernel, cap),
         "forward",
-        [back_shape],
-        (got_first, gu, down, value),
-        scratch=(chunk_shape, ((hid, model), BF16), back_shape, row_shape, back_rows),
-        after=tuple(terms),
+        [chunk_shape],
+        (got_first, gu, down),
+        scratch=(chunk_shape, ((hid, model), BF16), chunk_shape, row_shape, row_shape),
+        after=(*terms, value),
         hbm_in=(0, 2),
         hbm_out=(0,),
         semaphores=(groups + 1, groups),
@@ -461,12 +461,28 @@
         moved=7 * MB,
     )
     got_back = exchange(send_back)
-    mixed_first, gate_grads = call(
+    for step in steps[EARLY:-1]:
+        value = jnp.concatenate([value, crossed(value, *step)], axis=0)
+    gate_grads = call(
+        functools.partial(gate_grad_kernel, cap, n_z, bits),
+        "gate_grad",
+        [((1, tokens), F32)],
+        (
+            jnp.stack([lax.axis_index("yl"), lax.axis_index("z")]).astype(I32),
+            value,
+            crossed(value, *steps[-1]),
+            row(routes_second),
+            row(gates_second),
+        ),
+        scalars=1,
+        moved=MB // 8,
+    )
+    mixed_first = call(
         functools.partial(combine_kernel, cap),
         "combine",
-        [((tokens, model), BF16), ((1, tokens), F32)],
-        (got_back, mix, pick, row(gates_second)),
-        scratch=(back_rows,),
+        [((tokens, model), BF16)],
+        (got_back, mix),
+        scratch=(row_shape,),
         flops=2**29,
         moved=2 * MB,
     )

time: 217 us -> 231 us (1.065)
  starting transfers between devices: 65.4 us -> 126 us
  waiting for transfers between devices: 124 us -> 69.1 us
  local copies, waits for them, and re-layouts: 2.19 us -> 8.73 us
    all_to_all x3, waiting for transfers between devices: 104 us -> 43.5 us  [exchange(): moved = lax.all_to_all(chunks, EP, split_axis=0, concat_axis=0, tiled=True)]
    ppermute x0 -> x6, starting transfers between devices: none -> 57.3 us  [crossed(): lax.ppermute(a, axis, [(i, i ^ mask) for i in range(lax.axis_size(axis))])]
    ppermute x0 -> x6, waiting for transfers between devices: none -> 21.4 us  [crossed(): lax.ppermute(a, axis, [(i, i ^ mask) for i in range(lax.axis_size(axis))])]
    ppermute x5, waiting for transfers between devices: 19.8 us -> 4.15 us  [shifted(): return lax.ppermute(a, axis, [(i, (i + k) % size) for i in range(size)])]
    unnamed x18 -> x32, local copies, waits for them, and re-layouts: 2.19 us -> 8.68 us
    all_to_all x3, starting transfers between devices: 46.3 us -> 49.4 us  [exchange(): moved = lax.all_to_all(chunks, EP, split_axis=0, concat_axis=0, tiled=True)]
    pallas_call x9 -> x10, Pallas kernels: 20.6 us -> 21.9 us  [call(): pl.pallas_call(kernel, name=name, out_shape=shapes, in_specs=spaces + [AN...]
  transfers between devices with their start and end apart: 8 -> 14, of which waited for: 5 -> 8; matrix products, arithmetic and copies ran while one was open for 0% -> 0% of each run, Pallas kernels for 5% -> 6%
where the time goes in v5:
time: 231 us; the launch traced here: 226 us
  starting transfers between devices  126 us (55%)
  waiting for transfers between devices  69.1 us (30%)
  Pallas kernels  21.9 us (9%)
  local copies, waits for them, and re-layouts  8.73 us (4%)
    ppermute x6, starting transfers between devices, crossed(): lax.ppermute(a, axis, [(i, i ^ mask) for i in range(lax.axis_size(axis))])  57.3 us
    all_to_all x3, starting transfers between devices, exchange(): moved = lax.all_to_all(chunks, EP, split_axis=0, concat_axis=0, tiled=True)  49.4 us
    all_to_all x3, waiting for transfers between devices, exchange(): moved = lax.all_to_all(chunks, EP, split_axis=0, concat_axis=0, tiled=True)  43.5 us
    pallas_call x10, Pallas kernels, call(): pl.pallas_call(kernel, name=name, out_shape=shapes, in_specs=spaces + [AN...  21.9 us
    ppermute x6, waiting for transfers between devices, crossed(): lax.ppermute(a, axis, [(i, i ^ mask) for i in range(lax.axis_size(axis))])  21.4 us
    ppermute x5, starting transfers between devices, shifted(): return lax.ppermute(a, axis, [(i, (i + k) % size) for i in range(size)])  18.9 us
    unnamed x32, local copies, waits for them, and re-layouts  8.68 us
  transfers between devices with their start and end apart: 14, of which 8 were waited for; matrix products, arithmetic and copies ran while one was open for 0% of the time, Pallas kernels for 6%

profile of v5, /device:TPU:1, one launch (start us, length us, event | category | flops | bytes accessed | tf_op | source)
XLA Modules:
  0.0 226.4 jit_solution(7119312113714621033)
XLA Ops:
  0.6 0.0 copy-start
  0.6 2.8 %dispatch_second.1 = bf16[512,1024]{1,0:T(8,128)(2,1)} custom-call(s32[1,128]{1,0:T(1,128)} %bitcast.28, bf16[1,128]{1,0:T(2,128)(2,1)} %bitcast.30, bf16[128,2048]{1,0:T(8,128)(2,1)} %tokens_hbm.3), custom_call_target="tpu_custom_call" | custom-call | flops 536870912 | bytes 2097152 | tf_op jit(solution)/shard_map/dispatch_second/pallas_call | solution.py:316
  3.4 23.6 %all-to-all-start.1 = ((bf16[64,8,1024]{2,1,0:T(8,128)(2,1)}), bf16[64,8,1024]{2,1,0:T(8,128)(2,1)}, u32[]{:S(2)}, u32[]{:S(2)}) async-start(bf16[64,8,1024]{2,1,0:T(8,128)(2,1)} %bitcast.36), calls=%async_computation.1 | async-start | bytes 2097152 | tf_op jit(solution)/shard_map/all_to_all | solution.py:359
  27.1 0.0 copy-start.12
  27.1 0.0 copy-start.13
  27.1 0.0 copy-done
  27.1 0.0 copy-start.2
  27.1 1.2 copy-done.2
  28.3 1.0 saved.1
  29.4 0.0 copy-start.10
  29.4 0.7 copy-done.10
  30.0 0.0 copy-done.12
  30.0 0.0 copy-done.13
  30.0 2.6 %dispatch_first.1 = (bf16[512,1024]{1,0:T(8,128)(2,1)}, bf16[128,256]{1,0:T(8,128)(2,1)S(1)}) custom-call(s32[1,128]{1,0:T(1,128)S(1)} %bitcast.32, bf16[1,128]{1,0:T(2,128)(2,1)S(1)} %bitcast.33, bf16[128,2048]{1,0:T(8,128)(2,1)} %tokens_hbm.2, f32[256,384]{1,0:T(8,128)S(1)} %get-tuple-element.20.refs_0_.up_ref), custom_call_target="tpu_custom_call" | custom-call | flops 536870912 | bytes 2097152 | tf_op jit(solution)/shard_map/dispatch_first/pallas_call | solution.py:316
  32.6 0.0 copy-start.8
  32.6 0.7 copy-done.8
  33.4 0.6 copy-done.14
  34.0 43.5 %all-to-all-done.1 = bf16[64,8,1024]{2,1,0:T(8,128)(2,1)} async-done(((bf16[64,8,1024]{2,1,0:T(8,128)(2,1)}), bf16[64,8,1024]{2,1,0:T(8,128)(2,1)}, u32[]{:S(2)}, u32[]{:S(2)}) %all-to-all-start.1) | async-done | bytes 1048608 | tf_op jit(solution)/shard_map/all_to_all | solution.py:359
  77.5 10.5 %all-to-all-start = ((bf16[64,8,1024]{2,1,0:T(8,128)(2,1)}), bf16[64,8,1024]{2,1,0:T(8,128)(2,1)}, u32[]{:S(2)}, u32[]{:S(2)}) async-start(bf16[64,8,1024]{2,1,0:T(8,128)(2,1)} %bitcast.35), calls=%async_computation | async-start | bytes 2097152 | tf_op jit(solution)/shard_map/all_to_all | solution.py:359
  88.0 0.1 pad_add_fusion.at_ref
  88.1 1.4 copy-done.1
  89.5 1.2 copy-done.3
  90.7 1.0 copy-done.9
  91.7 0.9 copy-done.11
  92.7 4.0 %backward.1 = (bf16[8,128,1152]{2,1,0:T(8,128)(2,1)S(1)}, bf16[8,128,1152]{2,1,0:T(8,128)(2,1)S(1)}, f32[1,256]{1,0:T(1,128)S(1)}) custom-call(s32[3]{0:T(128)S(1)} %pad_add_fusion.at_ref, bf16[512,1024]{1,0:T(8,128)(2,1)} %bitcast.13.chunks_ref, bf16[384,2048]{1,0:T(8,128)(2,1)S(1)} %bitcast.24, bf16[256,2048]{1,0:T(8,128)(2,1)S(1)} %bitcast.27, ...), custom_call_target="tpu_custom_call" | custom-call | flops 2147483648 | bytes 12582912 | tf_op jit(solution)/shard_map/backward/pallas_call | solution.py:316
  96.7 3.1 %collective-permute-start = (bf16[8,128,1152]{2,1,0:T(8,128)(2,1)S(1)}, bf16[8,128,1152]{2,1,0:T(8,128)(2,1)S(1)}, u32[]{:S(2)}, u32[]{:S(2)}) collective-permute-start(bf16[8,128,1152]{2,1,0:T(8,128)(2,1)S(1)} %get-tuple-element.25), channel_id=1, source_target_pairs={{0,1},{1,0},{2,3},{3,2},{4,5},{5,4},{6,7},{7,6},{8,9},{9,8},{10,11... | collective-permute-start | bytes 7077896 | tf_op jit(solution)/shard_map/ppermute | solution.py:364
  99.8 4.1 %collective-permute-done.b_ref = bf16[8,128,1152]{2,1,0:T(8,128)(2,1)S(1)} collective-permute-done((bf16[8,128,1152]{2,1,0:T(8,128)(2,1)S(1)}, bf16[8,128,1152]{2,1,0:T(8,128)(2,1)S(1)}, u32[]{:S(2)}, u32[]{:S(2)}) %collective-permute-start) | collective-permute-done | bytes 2359328 | tf_op jit(solution)/shard_map/ppermute | solution.py:364
  103.9 1.4 pairs.1
  105.3 0.8 copy-done.4
  106.1 4.6 %collective-permute-start.1 = (bf16[2,128,1152]{2,1,0:T(8,128)(2,1)}, bf16[2,128,1152]{2,1,0:T(8,128)(2,1)}, u32[]{:S(2)}, u32[]{:S(2)}) collective-permute-start(bf16[2,128,1152]{2,1,0:T(8,128)(2,1)} %get-tuple-element.26), channel_id=1, source_target_pairs={{0,4},{2,6},{4,0},{6,2},{1,5},{3,7},{5,1},{7,3},{8,12},{10,14},{12... | collective-permute-start | bytes 1769480 | tf_op jit(solution)/shard_map/ppermute | solution.py:364
  110.7 2.2 collective-permute-start.2
  113.0 4.3 %collective-permute-start.3 = (bf16[2,128,1152]{2,1,0:T(8,128)(2,1)}, bf16[2,128,1152]{2,1,0:T(8,128)(2,1)}, u32[]{:S(2)}, u32[]{:S(2)}) collective-permute-start(bf16[2,128,1152]{2,1,0:T(8,128)(2,1)} %get-tuple-element.28), channel_id=1, source_target_pairs={{0,6},{2,0},{4,2},{6,4},{1,7},{3,1},{5,3},{7,5},{8,14},{10,8},{12,... | collective-permute-start | bytes 1769480 | tf_op jit(solution)/shard_map/ppermute | solution.py:364
  117.2 3.1 %collective-permute-start.4 = (f32[1,256]{1,0:T(1,128)S(1)}, f32[1,256]{1,0:T(1,128)S(1)}, u32[]{:S(2)}, u32[]{:S(2)}) collective-permute-start(f32[1,256]{1,0:T(1,128)S(1)} %get-tuple-element.29), channel_id=1, source_target_pairs={{0,16},{16,0},{32,48},{48,32},{64,80},{80,64},{96,112},{112,96},{1... | collective-permute-start | bytes 3080 | tf_op jit(solution)/shard_map/ppermute | solution.py:446
  120.4 9.8 %collective-permute-done.4 = f32[1,256]{1,0:T(1,128)S(1)} collective-permute-done((f32[1,256]{1,0:T(1,128)S(1)}, f32[1,256]{1,0:T(1,128)S(1)}, u32[]{:S(2)}, u32[]{:S(2)}) %collective-permute-start.4) | collective-permute-done | bytes 1056 | tf_op jit(solution)/shard_map/ppermute | solution.py:446
  130.2 5.7 %collective-permute-start.5 = (f32[2,256]{1,0:T(2,128)S(1)}, f32[2,256]{1,0:T(2,128)S(1)}, u32[]{:S(2)}, u32[]{:S(2)}) collective-permute-start(f32[2,256]{1,0:T(2,128)S(1)} %pad_maximum_fusion.2), channel_id=1, source_target_pairs={{0,32},{16,48},{32,0},{48,16},{64,96},{80,112},{96,64},{112,80},{1... | collective-permute-start | bytes 6152 | tf_op jit(solution)/shard_map/ppermute | solution.py:446
  135.9 1.4 collective-permute-done.5
  137.3 3.0 %collective-permute-start.6 = (f32[4,256]{1,0:T(4,128)S(1)}, f32[4,256]{1,0:T(4,128)S(1)}, u32[]{:S(2)}, u32[]{:S(2)}) collective-permute-start(f32[4,256]{1,0:T(4,128)S(1)} %pad_maximum_fusion.1), channel_id=1, source_target_pairs={{0,256},{256,0},{512,768},{768,512},{1,257},{257,1},{513,769},{769... | collective-permute-start | bytes 12296 | tf_op jit(solution)/shard_map/ppermute | solution.py:446
  140.3 1.8 collective-permute-done.6
  142.1 0.0 all-to-all-done
  142.1 0.0 collective-permute-done.1.refs_0_.refs_1_
  142.1 0.0 collective-permute-done.2.refs_1_.refs_2_
  142.1 0.0 collective-permute-done.3.refs_2_.refs_3_
  142.1 4.9 %forward.1 = bf16[512,1024]{1,0:T(8,128)(2,1)} custom-call(bf16[512,1024]{1,0:T(8,128)(2,1)} %bitcast.5.chunks_hbm, bf16[2048,768]{1,0:T(8,128)(2,1)S(1)} %bitcast.22, bf16[384,2048]{1,0:T(8,128)(2,1)} %bitcast.23, bf16[2,128,1152]{2,1,0:T(8,128)(2,1)} %collective-permute-done.1.refs_0_.refs_1_, ...), custom_call_target="tpu_custom_call" | custom-call | flops 2147483648 | bytes 7340032 | tf_op jit(solution)/shard_map/forward/pallas_call | solution.py:316
  147.1 0.0 copy-start.5
  147.1 0.0 copy-start.6
  147.1 0.0 copy-start.7
  147.1 0.0 copy-start.15
  147.1 15.2 %all-to-all-start.2 = ((bf16[64,8,1024]{2,1,0:T(8,128)(2,1)}), bf16[64,8,1024]{2,1,0:T(8,128)(2,1)S(1)}, u32[]{:S(2)}, u32[]{:S(2)}) async-start(bf16[64,8,1024]{2,1,0:T(8,128)(2,1)} %bitcast.34), calls=%async_computation.2 | async-start | bytes 2097152 | tf_op jit(solution)/shard_map/all_to_all | solution.py:359
  162.3 0.0 copy-done.5
  162.3 1.7 sums.1
  164.1 4.8 %collective-permute-start.10 = (bf16[128,1152]{1,0:T(8,128)(2,1)S(1)}, bf16[128,1152]{1,0:T(8,128)(2,1)S(1)}, u32[]{:S(2)}, u32[]{:S(2)}) collective-permute-start(bf16[128,1152]{1,0:T(8,128)(2,1)S(1)} %get-tuple-element.33), channel_id=1, source_target_pairs={{0,8},{8,0},{1,9},{9,1},{2,10},{10,2},{3,11},{11,3},{4,12},{12,4},... | collective-permute-start | bytes 884744 | tf_op jit(solution)/shard_map/ppermute | solution.py:364
  168.8 3.9 %collective-permute-start.7 = (f32[8,256]{1,0:T(8,128)S(1)}, f32[8,256]{1,0:T(8,128)S(1)}, u32[]{:S(2)}, u32[]{:S(2)}) collective-permute-start(f32[8,256]{1,0:T(8,128)S(1)} %pad_maximum_fusion.refs_3_), channel_id=1, source_target_pairs={{0,512},{256,768},{512,0},{768,256},{1,513},{257,769},{513,1},{769... | collective-permute-start | bytes 24584 | tf_op jit(solution)/shard_map/ppermute | solution.py:446
  172.8 3.6 %collective-permute-done.7 = f32[8,256]{1,0:T(8,128)S(1)} collective-permute-done((f32[8,256]{1,0:T(8,128)S(1)}, f32[8,256]{1,0:T(8,128)S(1)}, u32[]{:S(2)}, u32[]{:S(2)}) %collective-permute-start.7) | collective-permute-done | bytes 8224 | tf_op jit(solution)/shard_map/ppermute | solution.py:446
  176.4 28.3 %collective-permute-start.8 = (f32[16,256]{1,0:T(8,128)S(1)}, f32[16,256]{1,0:T(8,128)S(1)}, u32[]{:S(2)}, u32[]{:S(2)}) collective-permute-start(f32[16,256]{1,0:T(8,128)S(1)} %concatenate.22), channel_id=1, source_target_pairs={{0,64},{16,80},{32,96},{48,112},{64,0},{80,16},{96,32},{112,48},{1... | collective-permute-start | bytes 49160 | tf_op jit(solution)/shard_map/ppermute | solution.py:446
  204.7 3.6 %collective-permute-done.8 = f32[16,256]{1,0:T(8,128)S(1)} collective-permute-done((f32[16,256]{1,0:T(8,128)S(1)}, f32[16,256]{1,0:T(8,128)S(1)}, u32[]{:S(2)}, u32[]{:S(2)}) %collective-permute-start.8) | collective-permute-done | bytes 16416 | tf_op jit(solution)/shard_map/ppermute | solution.py:446
  208.3 13.2 %collective-permute-start.9 = (f32[32,256]{1,0:T(8,128)S(1)}, f32[32,256]{1,0:T(8,128)S(1)}, u32[]{:S(2)}, u32[]{:S(2)}) collective-permute-start(f32[32,256]{1,0:T(8,128)S(1)} %concatenate.23.a_ref), channel_id=1, source_target_pairs={{0,128},{16,144},{32,160},{48,176},{64,192},{80,208},{96,224},{112... | collective-permute-start | bytes 98312 | tf_op jit(solution)/shard_map/ppermute | solution.py:446
  221.5 0.1 pad_add_fusion.1.at_ref
  221.6 1.3 collective-permute-done.9.b_ref
  222.9 1.2 gate_grad.1
  224.1 0.0 collective-permute-done.10.b_ref
  224.1 0.8 finish.1
  224.9 0.0 all-to-all-done.2
  224.9 0.0 copy-done.15
  224.9 1.5 combine.1
  (13 shorter events, 0.1 us)
Async XLA Ops:
  0.6 26.5 %copy-start = (bf16[1,2048,768]{2,1,0:T(8,128)(2,1)S(1)}, bf16[1,2048,768]{2,1,0:T(8,128)(2,1)}, u32[]{:S(2)}) copy-start(bf16[1,2048,768]{2,1,0:T(8,128)(2,1)} %param.12) | copy-start | bytes 9437188
  3.4 74.1 %all-to-all-start.1 = ((bf16[64,8,1024]{2,1,0:T(8,128)(2,1)}), bf16[64,8,1024]{2,1,0:T(8,128)(2,1)}, u32[]{:S(2)}, u32[]{:S(2)}) async-start(bf16[64,8,1024]{2,1,0:T(8,128)(2,1)} %bitcast.36), calls=%async_computation.1 | async-start | bytes 2097152 | tf_op jit(solution)/shard_map/all_to_all | solution.py:359
  27.1 3.0 %copy-start.12 = (s32[128,1]{0,1:T(1,128)S(1)}, s32[128,1]{0,1:T(1,128)}, u32[]{:S(2)}) copy-start(s32[128,1]{0,1:T(1,128)} %param.10) | copy-start | bytes 1540
  27.1 3.0 %copy-start.13 = (bf16[128,1]{0,1:T(2,128)(2,1)S(1)}, bf16[128,1]{0,1:T(2,128)(2,1)}, u32[]{:S(2)}) copy-start(bf16[128,1]{0,1:T(2,128)(2,1)} %param.11) | copy-start | bytes 772
  27.1 1.2 copy-start.2
  29.4 0.7 copy-start.10
  32.6 0.7 copy-start.8
  33.4 0.6 copy-start.14
  77.5 64.6 %all-to-all-start = ((bf16[64,8,1024]{2,1,0:T(8,128)(2,1)}), bf16[64,8,1024]{2,1,0:T(8,128)(2,1)}, u32[]{:S(2)}, u32[]{:S(2)}) async-start(bf16[64,8,1024]{2,1,0:T(8,128)(2,1)} %bitcast.35), calls=%async_computation | async-start | bytes 2097152 | tf_op jit(solution)/shard_map/all_to_all | solution.py:359
  88.1 1.4 copy-start.1
  89.5 1.2 copy-start.3
  90.7 1.0 copy-start.9
  91.7 0.9 copy-start.11
  96.7 7.2 %collective-permute-start = (bf16[8,128,1152]{2,1,0:T(8,128)(2,1)S(1)}, bf16[8,128,1152]{2,1,0:T(8,128)(2,1)S(1)}, u32[]{:S(2)}, u32[]{:S(2)}) collective-permute-start(bf16[8,128,1152]{2,1,0:T(8,128)(2,1)S(1)} %get-tuple-element.25), channel_id=1, source_target_pairs={{0,1},{1,0},{2,3},{3,2},{4,5},{5,4},{6,7},{7,6},{8,9},{9,8},{10,11... | collective-permute-start | bytes 7077896 | tf_op jit(solution)/shard_map/ppermute | solution.py:364
  105.3 0.8 copy-start.4
  106.1 36.0 %collective-permute-start.1 = (bf16[2,128,1152]{2,1,0:T(8,128)(2,1)}, bf16[2,128,1152]{2,1,0:T(8,128)(2,1)}, u32[]{:S(2)}, u32[]{:S(2)}) collective-permute-start(bf16[2,128,1152]{2,1,0:T(8,128)(2,1)} %get-tuple-element.26), channel_id=1, source_target_pairs={{0,4},{2,6},{4,0},{6,2},{1,5},{3,7},{5,1},{7,3},{8,12},{10,14},{12... | collective-permute-start | bytes 1769480 | tf_op jit(solution)/shard_map/ppermute | solution.py:364
  110.7 31.4 %collective-permute-start.2 = (bf16[2,128,1152]{2,1,0:T(8,128)(2,1)}, bf16[2,128,1152]{2,1,0:T(8,128)(2,1)}, u32[]{:S(2)}, u32[]{:S(2)}) collective-permute-start(bf16[2,128,1152]{2,1,0:T(8,128)(2,1)} %get-tuple-element.27), channel_id=1, source_target_pairs={{0,2},{2,4},{4,6},{6,0},{1,3},{3,5},{5,7},{7,1},{8,10},{10,12},{12... | collective-permute-start | bytes 1769480 | tf_op jit(solution)/shard_map/ppermute | solution.py:364
  113.0 29.2 %collective-permute-start.3 = (bf16[2,128,1152]{2,1,0:T(8,128)(2,1)}, bf16[2,128,1152]{2,1,0:T(8,128)(2,1)}, u32[]{:S(2)}, u32[]{:S(2)}) collective-permute-start(bf16[2,128,1152]{2,1,0:T(8,128)(2,1)} %get-tuple-element.28), channel_id=1, source_target_pairs={{0,6},{2,0},{4,2},{6,4},{1,7},{3,1},{5,3},{7,5},{8,14},{10,8},{12,... | collective-permute-start | bytes 1769480 | tf_op jit(solution)/shard_map/ppermute | solution.py:364
  117.2 12.9 %collective-permute-start.4 = (f32[1,256]{1,0:T(1,128)S(1)}, f32[1,256]{1,0:T(1,128)S(1)}, u32[]{:S(2)}, u32[]{:S(2)}) collective-permute-start(f32[1,256]{1,0:T(1,128)S(1)} %get-tuple-element.29), channel_id=1, source_target_pairs={{0,16},{16,0},{32,48},{48,32},{64,80},{80,64},{96,112},{112,96},{1... | collective-permute-start | bytes 3080 | tf_op jit(solution)/shard_map/ppermute | solution.py:446
  130.2 7.1 %collective-permute-start.5 = (f32[2,256]{1,0:T(2,128)S(1)}, f32[2,256]{1,0:T(2,128)S(1)}, u32[]{:S(2)}, u32[]{:S(2)}) collective-permute-start(f32[2,256]{1,0:T(2,128)S(1)} %pad_maximum_fusion.2), channel_id=1, source_target_pairs={{0,32},{16,48},{32,0},{48,16},{64,96},{80,112},{96,64},{112,80},{1... | collective-permute-start | bytes 6152 | tf_op jit(solution)/shard_map/ppermute | solution.py:446
  137.3 4.8 %collective-permute-start.6 = (f32[4,256]{1,0:T(4,128)S(1)}, f32[4,256]{1,0:T(4,128)S(1)}, u32[]{:S(2)}, u32[]{:S(2)}) collective-permute-start(f32[4,256]{1,0:T(4,128)S(1)} %pad_maximum_fusion.1), channel_id=1, source_target_pairs={{0,256},{256,0},{512,768},{768,512},{1,257},{257,1},{513,769},{769... | collective-permute-start | bytes 12296 | tf_op jit(solution)/shard_map/ppermute | solution.py:446
  147.1 15.3 %copy-start.5 = (bf16[2,128,1152]{2,1,0:T(8,128)(2,1)S(1)}, bf16[2,128,1152]{2,1,0:T(8,128)(2,1)}, u32[]{:S(2)}) copy-start(bf16[2,128,1152]{2,1,0:T(8,128)(2,1)} %copy-done.4) | copy-start | bytes 1769476
  147.1 75.8 %copy-start.6 = (s32[128,1]{0,1:T(1,128)S(1)}, s32[128,1]{0,1:T(1,128)}, u32[]{:S(2)}) copy-start(s32[128,1]{0,1:T(1,128)} %param.16) | copy-start | bytes 1540
  147.1 75.8 %copy-start.7 = (bf16[128,1]{0,1:T(2,128)(2,1)S(1)}, bf16[128,1]{0,1:T(2,128)(2,1)}, u32[]{:S(2)}) copy-start(bf16[128,1]{0,1:T(2,128)(2,1)} %param.17) | copy-start | bytes 772
  147.1 77.8 %copy-start.15 = (bf16[128,256]{1,0:T(8,128)(2,1)S(1)}, bf16[128,256]{1,0:T(8,128)(2,1)}, u32[]{:S(2)}) copy-start(bf16[128,256]{1,0:T(8,128)(2,1)} %copy-done.14) | copy-start | bytes 196612
  147.1 77.8 %all-to-all-start.2 = ((bf16[64,8,1024]{2,1,0:T(8,128)(2,1)}), bf16[64,8,1024]{2,1,0:T(8,128)(2,1)S(1)}, u32[]{:S(2)}, u32[]{:S(2)}) async-start(bf16[64,8,1024]{2,1,0:T(8,128)(2,1)} %bitcast.34), calls=%async_computation.2 | async-start | bytes 2097152 | tf_op jit(solution)/shard_map/all_to_all | solution.py:359
  164.1 60.0 %collective-permute-start.10 = (bf16[128,1152]{1,0:T(8,128)(2,1)S(1)}, bf16[128,1152]{1,0:T(8,128)(2,1)S(1)}, u32[]{:S(2)}, u32[]{:S(2)}) collective-permute-start(bf16[128,1152]{1,0:T(8,128)(2,1)S(1)} %get-tuple-element.33), channel_id=1, source_target_pairs={{0,8},{8,0},{1,9},{9,1},{2,10},{10,2},{3,11},{11,3},{4,12},{12,4},... | collective-permute-start | bytes 884744 | tf_op jit(solution)/shard_map/ppermute | solution.py:364
  168.8 7.6 %collective-permute-start.7 = (f32[8,256]{1,0:T(8,128)S(1)}, f32[8,256]{1,0:T(8,128)S(1)}, u32[]{:S(2)}, u32[]{:S(2)}) collective-permute-start(f32[8,256]{1,0:T(8,128)S(1)} %pad_maximum_fusion.refs_3_), channel_id=1, source_target_pairs={{0,512},{256,768},{512,0},{768,256},{1,513},{257,769},{513,1},{769... | collective-permute-start | bytes 24584 | tf_op jit(solution)/shard_map/ppermute | solution.py:446
  176.4 31.9 %collective-permute-start.8 = (f32[16,256]{1,0:T(8,128)S(1)}, f32[16,256]{1,0:T(8,128)S(1)}, u32[]{:S(2)}, u32[]{:S(2)}) collective-permute-start(f32[16,256]{1,0:T(8,128)S(1)} %concatenate.22), channel_id=1, source_target_pairs={{0,64},{16,80},{32,96},{48,112},{64,0},{80,16},{96,32},{112,48},{1... | collective-permute-start | bytes 49160 | tf_op jit(solution)/shard_map/ppermute | solution.py:446
  208.3 14.6 %collective-permute-start.9 = (f32[32,256]{1,0:T(8,128)S(1)}, f32[32,256]{1,0:T(8,128)S(1)}, u32[]{:S(2)}, u32[]{:S(2)}) collective-permute-start(f32[32,256]{1,0:T(8,128)S(1)} %concatenate.23.a_ref), channel_id=1, source_target_pairs={{0,128},{16,144},{32,160},{48,176},{64,192},{80,208},{96,224},{112... | collective-permute-start | bytes 98312 | tf_op jit(solution)/shard_map/ppermute | solution.py:446

commit v6 on v4

--- a/solution.py
+++ b/solution.py
@@ -95,14 +95,21 @@
     width = chunks_ref.shape[1]
     _, slots = slots_of(routes, experts)
     base = routes * CHUNK + slots
+    groups, pieces = range(chunks_ref.shape[0] // GROUP), range(CHUNK // cap)
+    row = iota((GROUP, tokens), 0)
+    select = [
+        [
+            jnp.where(row == base + (q * cap - g * GROUP), weights, 0.0).astype(BF16)
+            for q in pieces
+        ]
+        for g in groups
+    ]
     copies = []
     arrival.wait()
-    for g in range(chunks_ref.shape[0] // GROUP):
-        row = iota((GROUP, tokens), 0) + g * GROUP
+    for g in groups:
         total = None
-        for q in range(CHUNK // cap):
-            select = jnp.where(row == base + q * cap, weights, 0.0).astype(BF16)
-            term = dot(select, tokens_ref[:, q * width : (q + 1) * width])
+        for q in pieces:
+            term = dot(select[g][q], tokens_ref[:, q * width : (q + 1) * width])
             total = term if total is None else total + term
         chunks_ref[g * GROUP : (g + 1) * GROUP, :] = total.astype(BF16)
         copies.append(start_copy(group(chunks_ref, g), group(out_ref, g), semaphores.at[g]))
@@ -257,18 +264,30 @@
 
 
 def combine_kernel(
-    cap, chunks_ref, mix_ref, pick_ref, gates_ref, out_ref, grads_ref, rows_ref
+    cap,
+    chunks_ref,
+    mix_ref,
+    pick_ref,
+    gates_ref,
+    out_hbm,
+    grads_ref,
+    rows_ref,
+    out_ref,
+    semaphores,
 ):
     from_chunks(chunks_ref, rows_ref, cap)
     width = chunks_ref.shape[1] - EXTRA
+    copies = []
     for q in range(CHUNK // cap):
         at = q * (width + EXTRA)
-        out_ref[:, q * width : (q + 1) * width] = dot(
-            mix_ref[...], rows_ref[:, at : at + width]
-        ).astype(BF16)
+        out_ref[q] = dot(mix_ref[...], rows_ref[:, at : at + width]).astype(BF16)
+        target = out_hbm.at[:, pl.ds(q * width, width)]
+        copies.append(start_copy(out_ref.at[q], target, semaphores.at[q]))
     value = dot(pick_ref[...], rows_ref[:, width : width + EXTRA])
     value = jnp.sum(value.T, axis=0, keepdims=True)
     grads_ref[...] = value / gates_ref[...].astype(F32)
+    for copy in copies:
+        copy.wait()
 
 
 def pair_kernel(a_ref, b_ref, *out_refs):
@@ -466,7 +485,9 @@
         "combine",
         [((tokens, model), BF16), ((1, tokens), F32)],
         (got_back, mix, pick, row(gates_second)),
-        scratch=(back_rows,),
+        scratch=(back_rows, ((CHUNK // cap, tokens, width), BF16)),
+        hbm_out=(0,),
+        semaphores=(CHUNK // cap,),
         flops=2**29,
         moved=2 * MB,
     )

time: 217 us -> 217 us (level)
  no operation moved by 1% of the time
where the time goes in v6:
time: 217 us; the launch traced here: 213 us
  waiting for transfers between devices  124 us (57%)
  starting transfers between devices  65.4 us (30%)
  Pallas kernels  21.1 us (10%)
  local copies, waits for them, and re-layouts  2.19 us (1%)
    all_to_all x3, waiting for transfers between devices, exchange(): moved = lax.all_to_all(chunks, EP, split_axis=0, concat_axis=0, tiled=True)  104 us
    all_to_all x3, starting transfers between devices, exchange(): moved = lax.all_to_all(chunks, EP, split_axis=0, concat_axis=0, tiled=True)  46.3 us
    pallas_call x9, Pallas kernels, call(): pl.pallas_call(kernel, name=name, out_shape=shapes, in_specs=spaces + [AN...  21.1 us
    ppermute x5, waiting for transfers between devices, shifted(): return lax.ppermute(a, axis, [(i, (i + k) % size) for i in range(size)])  19.8 us
    ppermute x5, starting transfers between devices, shifted(): return lax.ppermute(a, axis, [(i, (i + k) % size) for i in range(size)])  19 us
  transfers between devices with their start and end apart: 8, of which 5 were waited for; matrix products, arithmetic and copies ran while one was open for 0% of the time, Pallas kernels for 5%

profile of v6, /device:TPU:1, one launch (start us, length us, event | category | flops | bytes accessed | tf_op | source)
XLA Modules:
  0.0 213.1 jit_solution(3033102297214252809)
XLA Ops:
  0.6 0.0 copy-start.7
  0.6 0.0 copy-start.5
  0.7 0.0 copy-start.6
  0.7 2.6 %dispatch_second.1 = bf16[512,1024]{1,0:T(8,128)(2,1)} custom-call(s32[1,128]{1,0:T(1,128)} %bitcast.28, bf16[1,128]{1,0:T(2,128)(2,1)} %bitcast.30, bf16[128,2048]{1,0:T(8,128)(2,1)} %tokens_hbm.3), custom_call_target="tpu_custom_call" | custom-call | flops 536870912 | bytes 2097152 | tf_op jit(solution)/shard_map/dispatch_second/pallas_call | solution.py:343
  3.3 23.6 %all-to-all-start.1 = ((bf16[64,8,1024]{2,1,0:T(8,128)(2,1)}), bf16[64,8,1024]{2,1,0:T(8,128)(2,1)}, u32[]{:S(2)}, u32[]{:S(2)}) async-start(bf16[64,8,1024]{2,1,0:T(8,128)(2,1)} %bitcast.34), calls=%async_computation.1 | async-start | bytes 2097152 | tf_op jit(solution)/shard_map/all_to_all | solution.py:386
  26.9 0.0 copy-start
  27.0 0.0 copy-done.7
  27.0 0.0 copy-done.5
  27.0 0.0 copy-done.6
  27.0 2.7 %dispatch_first.1 = (bf16[512,1024]{1,0:T(8,128)(2,1)}, bf16[128,256]{1,0:T(8,128)(2,1)S(1)}, bf16[128,256]{1,0:T(8,128)(2,1)S(1)}) custom-call(s32[1,128]{1,0:T(1,128)S(1)} %bitcast.26, bf16[1,128]{1,0:T(2,128)(2,1)S(1)} %bitcast.27, s32[1,128]{1,0:T(1,128)S(1)} %bitcast.29, bf16[128,2048]{1,0:T(8,128)(2,1)} %tokens_hbm.2), custom_call_target="tpu_custom_call" | custom-call | flops 536870912 | bytes 2097152 | tf_op jit(solution)/shard_map/dispatch_first/pallas_call | solution.py:343
  29.7 47.7 %all-to-all-done.1 = bf16[64,8,1024]{2,1,0:T(8,128)(2,1)} async-done(((bf16[64,8,1024]{2,1,0:T(8,128)(2,1)}), bf16[64,8,1024]{2,1,0:T(8,128)(2,1)}, u32[]{:S(2)}, u32[]{:S(2)}) %all-to-all-start.1) | async-done | bytes 1048608 | tf_op jit(solution)/shard_map/all_to_all | solution.py:386
  77.4 10.5 %all-to-all-start = ((bf16[64,8,1024]{2,1,0:T(8,128)(2,1)}), bf16[64,8,1024]{2,1,0:T(8,128)(2,1)}, u32[]{:S(2)}, u32[]{:S(2)}) async-start(bf16[64,8,1024]{2,1,0:T(8,128)(2,1)} %bitcast.33), calls=%async_computation | async-start | bytes 2097152 | tf_op jit(solution)/shard_map/all_to_all | solution.py:386
  87.9 0.0 copy-start.1
  87.9 0.0 copy-done
  87.9 0.0 copy-start.2
  87.9 1.3 copy-done.2
  89.3 1.0 saved.1
  90.3 0.1 pad_add_fusion.at_ref
  90.4 0.0 copy-done.1
  90.4 3.9 %backward.1 = (bf16[8,128,1152]{2,1,0:T(8,128)(2,1)S(1)}, bf16[8,128,1152]{2,1,0:T(8,128)(2,1)S(1)}, bf16[256,128]{1,0:T(8,128)(2,1)S(1)}) custom-call(s32[3]{0:T(128)S(1)} %pad_add_fusion.at_ref, bf16[512,1024]{1,0:T(8,128)(2,1)} %bitcast.12.chunks_ref, bf16[384,2048]{1,0:T(8,128)(2,1)S(1)} %bitcast.22, bf16[256,2048]{1,0:T(8,128)(2,1)S(1)} %bitcast.25, ...), custom_call_target="tpu_custom_call" | custom-call | flops 2147483648 | bytes 12582912 | tf_op jit(solution)/shard_map/backward/pallas_call | solution.py:343
  94.2 3.1 %collective-permute-start = (bf16[8,128,1152]{2,1,0:T(8,128)(2,1)S(1)}, bf16[8,128,1152]{2,1,0:T(8,128)(2,1)S(1)}, u32[]{:S(2)}, u32[]{:S(2)}) collective-permute-start(bf16[8,128,1152]{2,1,0:T(8,128)(2,1)S(1)} %get-tuple-element.29), channel_id=1, source_target_pairs={{0,1},{1,0},{2,3},{3,2},{4,5},{5,4},{6,7},{7,6},{8,9},{9,8},{10,11... | collective-permute-start | bytes 7077896 | tf_op jit(solution)/shard_map/ppermute | solution.py:391
  97.3 4.1 %collective-permute-done.b_ref = bf16[8,128,1152]{2,1,0:T(8,128)(2,1)S(1)} collective-permute-done((bf16[8,128,1152]{2,1,0:T(8,128)(2,1)S(1)}, bf16[8,128,1152]{2,1,0:T(8,128)(2,1)S(1)}, u32[]{:S(2)}, u32[]{:S(2)}) %collective-permute-start) | collective-permute-done | bytes 2359328 | tf_op jit(solution)/shard_map/ppermute | solution.py:391
  101.5 1.4 pairs.1
  102.8 0.0 copy-start.3
  102.8 0.8 copy-done.3
  103.7 4.7 %collective-permute-start.1 = (bf16[2,128,1152]{2,1,0:T(8,128)(2,1)}, bf16[2,128,1152]{2,1,0:T(8,128)(2,1)}, u32[]{:S(2)}, u32[]{:S(2)}) collective-permute-start(bf16[2,128,1152]{2,1,0:T(8,128)(2,1)} %get-tuple-element.30), channel_id=1, source_target_pairs={{0,4},{2,6},{4,0},{6,2},{1,5},{3,7},{5,1},{7,3},{8,12},{10,14},{12... | collective-permute-start | bytes 1769480 | tf_op jit(solution)/shard_map/ppermute | solution.py:391
  108.4 2.2 %collective-permute-start.2 = (bf16[2,128,1152]{2,1,0:T(8,128)(2,1)}, bf16[2,128,1152]{2,1,0:T(8,128)(2,1)}, u32[]{:S(2)}, u32[]{:S(2)}) collective-permute-start(bf16[2,128,1152]{2,1,0:T(8,128)(2,1)} %get-tuple-element.31), channel_id=1, source_target_pairs={{0,2},{2,4},{4,6},{6,0},{1,3},{3,5},{5,7},{7,1},{8,10},{10,12},{12... | collective-permute-start | bytes 1769480 | tf_op jit(solution)/shard_map/ppermute | solution.py:391
  110.6 4.3 %collective-permute-start.3 = (bf16[2,128,1152]{2,1,0:T(8,128)(2,1)}, bf16[2,128,1152]{2,1,0:T(8,128)(2,1)}, u32[]{:S(2)}, u32[]{:S(2)}) collective-permute-start(bf16[2,128,1152]{2,1,0:T(8,128)(2,1)} %get-tuple-element.32), channel_id=1, source_target_pairs={{0,6},{2,0},{4,2},{6,4},{1,7},{3,1},{5,3},{7,5},{8,14},{10,8},{12,... | collective-permute-start | bytes 1769480 | tf_op jit(solution)/shard_map/ppermute | solution.py:391
  114.9 23.5 %all-to-all-done = bf16[64,8,1024]{2,1,0:T(8,128)(2,1)} async-done(((bf16[64,8,1024]{2,1,0:T(8,128)(2,1)}), bf16[64,8,1024]{2,1,0:T(8,128)(2,1)}, u32[]{:S(2)}, u32[]{:S(2)}) %all-to-all-start) | async-done | bytes 1048608 | tf_op jit(solution)/shard_map/all_to_all | solution.py:386
  138.4 0.0 collective-permute-done.1.refs_0_.refs_1_
  138.4 0.0 collective-permute-done.2.refs_1_.refs_2_
  138.4 0.0 collective-permute-done.3.refs_2_.refs_3_
  138.4 5.0 %forward.1 = bf16[512,1152]{1,0:T(8,128)(2,1)} custom-call(bf16[512,1024]{1,0:T(8,128)(2,1)} %bitcast.4.chunks_hbm, bf16[2048,768]{1,0:T(8,128)(2,1)S(1)} %bitcast.20, bf16[384,2048]{1,0:T(8,128)(2,1)} %bitcast.21, bf16[256,128]{1,0:T(8,128)(2,1)S(1)} %get-tuple-element.27.value_ref, bf16[2,128,1152]{2,1,0:T(8,128)(2,1)} %collective-permute-done.1.refs_0_.refs_1_, ...), custom_call_target="tpu_custom_call" | custom-call | flops 2147483648 | bytes 7340032 | tf_op jit(solution)/shard_map/forward/pallas_call | solution.py:343
  143.4 0.0 copy-start.4
  143.4 0.0 copy-start.8
  143.4 12.2 %all-to-all-start.2 = ((bf16[64,8,1152]{2,1,0:T(8,128)(2,1)}), bf16[64,8,1152]{2,1,0:T(8,128)(2,1)S(1)}, u32[]{:S(2)}, u32[]{:S(2)}) async-start(bf16[64,8,1152]{2,1,0:T(8,128)(2,1)} %bitcast.32), calls=%async_computation.2 | async-start | bytes 2359296 | tf_op jit(solution)/shard_map/all_to_all | solution.py:386
  155.6 0.0 copy-done.4
  155.6 1.7 sums.1
  157.4 4.8 %collective-permute-start.4 = (bf16[128,1152]{1,0:T(8,128)(2,1)S(1)}, bf16[128,1152]{1,0:T(8,128)(2,1)S(1)}, u32[]{:S(2)}, u32[]{:S(2)}) collective-permute-start(bf16[128,1152]{1,0:T(8,128)(2,1)S(1)} %get-tuple-element.39), channel_id=1, source_target_pairs={{0,8},{8,0},{1,9},{9,1},{2,10},{10,2},{3,11},{11,3},{4,12},{12,4},... | collective-permute-start | bytes 884744 | tf_op jit(solution)/shard_map/ppermute | solution.py:391
  162.1 15.7 %collective-permute-done.4.b_ref = bf16[128,1152]{1,0:T(8,128)(2,1)S(1)} collective-permute-done((bf16[128,1152]{1,0:T(8,128)(2,1)S(1)}, bf16[128,1152]{1,0:T(8,128)(2,1)S(1)}, u32[]{:S(2)}, u32[]{:S(2)}) %collective-permute-start.4) | collective-permute-done | bytes 294944 | tf_op jit(solution)/shard_map/ppermute | solution.py:391
  177.8 0.8 finish.1
  178.6 32.6 %all-to-all-done.2 = bf16[64,8,1152]{2,1,0:T(8,128)(2,1)S(1)} async-done(((bf16[64,8,1152]{2,1,0:T(8,128)(2,1)}), bf16[64,8,1152]{2,1,0:T(8,128)(2,1)S(1)}, u32[]{:S(2)}, u32[]{:S(2)}) %all-to-all-start.2) | async-done | bytes 1179680 | tf_op jit(solution)/shard_map/all_to_all | solution.py:386
  211.2 0.0 copy-done.8
  211.2 1.9 combine.1
Async XLA Ops:
  0.6 26.3 %copy-start.7 = (s32[128,1]{0,1:T(1,128)S(1)}, s32[128,1]{0,1:T(1,128)}, u32[]{:S(2)}) copy-start(s32[128,1]{0,1:T(1,128)} %param.16) | copy-start | bytes 1540
  0.6 26.3 %copy-start.5 = (s32[128,1]{0,1:T(1,128)S(1)}, s32[128,1]{0,1:T(1,128)}, u32[]{:S(2)}) copy-start(s32[128,1]{0,1:T(1,128)} %param.10) | copy-start | bytes 1540
  0.7 26.3 %copy-start.6 = (bf16[128,1]{0,1:T(2,128)(2,1)S(1)}, bf16[128,1]{0,1:T(2,128)(2,1)}, u32[]{:S(2)}) copy-start(bf16[128,1]{0,1:T(2,128)(2,1)} %param.11) | copy-start | bytes 772
  3.3 74.1 %all-to-all-start.1 = ((bf16[64,8,1024]{2,1,0:T(8,128)(2,1)}), bf16[64,8,1024]{2,1,0:T(8,128)(2,1)}, u32[]{:S(2)}, u32[]{:S(2)}) async-start(bf16[64,8,1024]{2,1,0:T(8,128)(2,1)} %bitcast.34), calls=%async_computation.1 | async-start | bytes 2097152 | tf_op jit(solution)/shard_map/all_to_all | solution.py:386
  26.9 61.0 %copy-start = (bf16[1,2048,768]{2,1,0:T(8,128)(2,1)S(1)}, bf16[1,2048,768]{2,1,0:T(8,128)(2,1)}, u32[]{:S(2)}) copy-start(bf16[1,2048,768]{2,1,0:T(8,128)(2,1)} %param.12) | copy-start | bytes 9437188
  77.4 61.0 %all-to-all-start = ((bf16[64,8,1024]{2,1,0:T(8,128)(2,1)}), bf16[64,8,1024]{2,1,0:T(8,128)(2,1)}, u32[]{:S(2)}, u32[]{:S(2)}) async-start(bf16[64,8,1024]{2,1,0:T(8,128)(2,1)} %bitcast.33), calls=%async_computation | async-start | bytes 2097152 | tf_op jit(solution)/shard_map/all_to_all | solution.py:386
  87.9 2.5 %copy-start.1 = (bf16[1,384,2048]{2,1,0:T(8,128)(2,1)S(1)}, bf16[1,384,2048]{2,1,0:T(8,128)(2,1)}, u32[]{:S(2)}) copy-start(bf16[1,384,2048]{2,1,0:T(8,128)(2,1)} %param.13) | copy-start | bytes 4718596
  87.9 1.3 copy-start.2
  94.2 7.2 %collective-permute-start = (bf16[8,128,1152]{2,1,0:T(8,128)(2,1)S(1)}, bf16[8,128,1152]{2,1,0:T(8,128)(2,1)S(1)}, u32[]{:S(2)}, u32[]{:S(2)}) collective-permute-start(bf16[8,128,1152]{2,1,0:T(8,128)(2,1)S(1)} %get-tuple-element.29), channel_id=1, source_target_pairs={{0,1},{1,0},{2,3},{3,2},{4,5},{5,4},{6,7},{7,6},{8,9},{9,8},{10,11... | collective-permute-start | bytes 7077896 | tf_op jit(solution)/shard_map/ppermute | solution.py:391
  102.8 0.8 copy-start.3
  103.7 34.7 %collective-permute-start.1 = (bf16[2,128,1152]{2,1,0:T(8,128)(2,1)}, bf16[2,128,1152]{2,1,0:T(8,128)(2,1)}, u32[]{:S(2)}, u32[]{:S(2)}) collective-permute-start(bf16[2,128,1152]{2,1,0:T(8,128)(2,1)} %get-tuple-element.30), channel_id=1, source_target_pairs={{0,4},{2,6},{4,0},{6,2},{1,5},{3,7},{5,1},{7,3},{8,12},{10,14},{12... | collective-permute-start | bytes 1769480 | tf_op jit(solution)/shard_map/ppermute | solution.py:391
  108.4 30.0 %collective-permute-start.2 = (bf16[2,128,1152]{2,1,0:T(8,128)(2,1)}, bf16[2,128,1152]{2,1,0:T(8,128)(2,1)}, u32[]{:S(2)}, u32[]{:S(2)}) collective-permute-start(bf16[2,128,1152]{2,1,0:T(8,128)(2,1)} %get-tuple-element.31), channel_id=1, source_target_pairs={{0,2},{2,4},{4,6},{6,0},{1,3},{3,5},{5,7},{7,1},{8,10},{10,12},{12... | collective-permute-start | bytes 1769480 | tf_op jit(solution)/shard_map/ppermute | solution.py:391
  110.6 27.8 %collective-permute-start.3 = (bf16[2,128,1152]{2,1,0:T(8,128)(2,1)}, bf16[2,128,1152]{2,1,0:T(8,128)(2,1)}, u32[]{:S(2)}, u32[]{:S(2)}) collective-permute-start(bf16[2,128,1152]{2,1,0:T(8,128)(2,1)} %get-tuple-element.32), channel_id=1, source_target_pairs={{0,6},{2,0},{4,2},{6,4},{1,7},{3,1},{5,3},{7,5},{8,14},{10,8},{12,... | collective-permute-start | bytes 1769480 | tf_op jit(solution)/shard_map/ppermute | solution.py:391
  143.4 12.2 %copy-start.4 = (bf16[2,128,1152]{2,1,0:T(8,128)(2,1)S(1)}, bf16[2,128,1152]{2,1,0:T(8,128)(2,1)}, u32[]{:S(2)}) copy-start(bf16[2,128,1152]{2,1,0:T(8,128)(2,1)} %copy-done.3) | copy-start | bytes 1769476
  143.4 67.8 %copy-start.8 = (bf16[128,1]{0,1:T(2,128)(2,1)S(1)}, bf16[128,1]{0,1:T(2,128)(2,1)}, u32[]{:S(2)}) copy-start(bf16[128,1]{0,1:T(2,128)(2,1)} %param.17) | copy-start | bytes 772
  143.4 67.8 %all-to-all-start.2 = ((bf16[64,8,1152]{2,1,0:T(8,128)(2,1)}), bf16[64,8,1152]{2,1,0:T(8,128)(2,1)S(1)}, u32[]{:S(2)}, u32[]{:S(2)}) async-start(bf16[64,8,1152]{2,1,0:T(8,128)(2,1)} %bitcast.32), calls=%async_computation.2 | async-start | bytes 2359296 | tf_op jit(solution)/shard_map/all_to_all | solution.py:386
  157.4 20.5 %collective-permute-start.4 = (bf16[128,1152]{1,0:T(8,128)(2,1)S(1)}, bf16[128,1152]{1,0:T(8,128)(2,1)S(1)}, u32[]{:S(2)}, u32[]{:S(2)}) collective-permute-start(bf16[128,1152]{1,0:T(8,128)(2,1)S(1)} %get-tuple-element.39), channel_id=1, source_target_pairs={{0,8},{8,0},{1,9},{9,1},{2,10},{10,2},{3,11},{11,3},{4,12},{12,4},... | collective-permute-start | bytes 884744 | tf_op jit(solution)/shard_map/ppermute | solution.py:391

commit v7 on v4

--- a/solution.py
+++ b/solution.py
@@ -245,28 +245,27 @@
     from_chunks(chunks_ref, in_rows_ref, cap, arrivals)
     both = dot(in_rows_ref[...], gu_ref[...])
     act = (jax.nn.silu(both[:, :hid]) * both[:, hid:]).astype(BF16)
-    width = chunks_ref.shape[1]
     down_arrival.wait()
-    for q in range(model // width):
-        at = q * (width + EXTRA)
-        out_rows_ref[:, at : at + width] = dot(
-            act, down_ref[:, q * width : (q + 1) * width]
-        ).astype(BF16)
-        out_rows_ref[:, at + width : at + width + EXTRA] = value_ref[...]
-    to_chunks(out_rows_ref, back_ref, out_ref, out_semaphores, cap)
+    out_rows_ref[:, :model] = dot(act, down_ref[...]).astype(BF16)
+    out_rows_ref[:, model:] = value_ref[...]
+    half = back_ref.shape[0] // 2
+    copies = []
+    for g in range(2):
+        part = out_rows_ref[g * half * cap : (g + 1) * half * cap, :]
+        back_ref[g * half : (g + 1) * half] = part.reshape(half, cap, part.shape[1])
+        piece = pl.ds(g * half, half)
+        copies.append(start_copy(back_ref.at[piece], out_ref.at[piece], out_semaphores.at[g]))
+    for copy in copies:
+        copy.wait()
 
 
 def combine_kernel(
     cap, chunks_ref, mix_ref, pick_ref, gates_ref, out_ref, grads_ref, rows_ref
 ):
-    from_chunks(chunks_ref, rows_ref, cap)
-    width = chunks_ref.shape[1] - EXTRA
-    for q in range(CHUNK // cap):
-        at = q * (width + EXTRA)
-        out_ref[:, q * width : (q + 1) * width] = dot(
-            mix_ref[...], rows_ref[:, at : at + width]
-        ).astype(BF16)
-    value = dot(pick_ref[...], rows_ref[:, width : width + EXTRA])
+    rows_ref[...] = chunks_ref[...].reshape(rows_ref.shape)
+    model = out_ref.shape[1]
+    out_ref[...] = dot(mix_ref[...], rows_ref[:, :model]).astype(BF16)
+    value = dot(pick_ref[...], rows_ref[:, model:])
     value = jnp.sum(value.T, axis=0, keepdims=True)
     grads_ref[...] = value / gates_ref[...].astype(F32)
 
@@ -372,9 +371,9 @@
         return lax.ppermute(a, axis, [(i, (i + k) % size) for i in range(size)])
 
     chunk_shape = ((experts * CHUNK, width), BF16)
-    back_shape = ((experts * CHUNK, width + EXTRA), BF16)
+    back_shape = ((experts, cap, model + EXTRA), BF16)
     row_shape = ((places, model), BF16)
-    back_rows = ((places, model + CHUNK // cap * EXTRA), BF16)
+    back_rows = ((places, model + EXTRA), BF16)
     extra_shape = ((places, EXTRA), BF16)
     pick_shape = ((tokens, places), BF16)
     here = jnp.stack(
@@ -456,11 +455,11 @@
         after=tuple(terms),
         hbm_in=(0, 2),
         hbm_out=(0,),
-        semaphores=(groups + 1, groups),
+        semaphores=(groups + 1, 2),
         flops=2**31,
         moved=7 * MB,
     )
-    got_back = exchange(send_back)
+    got_back = lax.all_to_all(send_back, EP, split_axis=0, concat_axis=0, tiled=True)
     mixed_first, gate_grads = call(
         functools.partial(combine_kernel, cap),
         "combine",

time: 217 us -> 214 us (0.986)
  waiting for transfers between devices: 124 us -> 121 us
    all_to_all x3 -> x2, waiting for transfers between devices: 104 us -> 71.1 us  [exchange(): moved = lax.all_to_all(chunks, EP, split_axis=0, concat_axis=0, tiled=True)]
    all_to_all x0 -> x1, waiting for transfers between devices: none -> 28.6 us  [local(): lax.all_to_all(send_back, EP, split_axis=0, concat_axis=0, tiled=True)]
    all_to_all x3 -> x2, starting transfers between devices: 46.3 us -> 34.1 us  [exchange(): moved = lax.all_to_all(chunks, EP, split_axis=0, concat_axis=0, tiled=True)]
    all_to_all x0 -> x1, starting transfers between devices: none -> 12.2 us  [local(): lax.all_to_all(send_back, EP, split_axis=0, concat_axis=0, tiled=True)]
where the time goes in v7:
time: 214 us; the launch traced here: 210 us
  waiting for transfers between devices  121 us (57%)
  starting transfers between devices  65.4 us (31%)
  Pallas kernels  20.1 us (9%)
  local copies, waits for them, and re-layouts  2.19 us (1%)
    all_to_all x2, waiting for transfers between devices, exchange(): moved = lax.all_to_all(chunks, EP, split_axis=0, concat_axis=0, tiled=True)  71.1 us
    all_to_all x2, starting transfers between devices, exchange(): moved = lax.all_to_all(chunks, EP, split_axis=0, concat_axis=0, tiled=True)  34.1 us
    all_to_all x1, waiting for transfers between devices, local(): lax.all_to_all(send_back, EP, split_axis=0, concat_axis=0, tiled=True)  28.6 us
    ppermute x5, waiting for transfers between devices, shifted(): return lax.ppermute(a, axis, [(i, (i + k) % size) for i in range(size)])  21.2 us
    pallas_call x9, Pallas kernels, call(): pl.pallas_call(kernel, name=name, out_shape=shapes, in_specs=spaces + [AN...  20.1 us
    ppermute x5, starting transfers between devices, shifted(): return lax.ppermute(a, axis, [(i, (i + k) % size) for i in range(size)])  19 us
    all_to_all x1, starting transfers between devices, local(): lax.all_to_all(send_back, EP, split_axis=0, concat_axis=0, tiled=True)  12.2 us
  transfers between devices with their start and end apart: 8, of which 5 were waited for; matrix products, arithmetic and copies ran while one was open for 0% of the time, Pallas kernels for 5%

profile of v7, /device:TPU:1, one launch (start us, length us, event | category | flops | bytes accessed | tf_op | source)
XLA Modules:
  0.0 209.5 jit_solution(13034836391994553139)
XLA Ops:
  0.6 0.0 copy-start.7
  0.6 0.0 copy-start.5
  0.7 0.0 copy-start.6
  0.7 2.6 %dispatch_second.1 = bf16[512,1024]{1,0:T(8,128)(2,1)} custom-call(s32[1,128]{1,0:T(1,128)} %bitcast.25, bf16[1,128]{1,0:T(2,128)(2,1)} %bitcast.27, bf16[128,2048]{1,0:T(8,128)(2,1)} %tokens_hbm.3), custom_call_target="tpu_custom_call" | custom-call | flops 536870912 | bytes 2097152 | tf_op jit(solution)/shard_map/dispatch_second/pallas_call | solution.py:323
  3.3 23.6 %all-to-all-start.1 = ((bf16[64,8,1024]{2,1,0:T(8,128)(2,1)}), bf16[64,8,1024]{2,1,0:T(8,128)(2,1)}, u32[]{:S(2)}, u32[]{:S(2)}) async-start(bf16[64,8,1024]{2,1,0:T(8,128)(2,1)} %bitcast.30), calls=%async_computation.1 | async-start | bytes 2097152 | tf_op jit(solution)/shard_map/all_to_all | solution.py:366
  26.9 0.0 copy-start
  27.0 0.0 copy-done.7
  27.0 0.0 copy-done.5
  27.0 0.0 copy-done.6
  27.0 2.7 %dispatch_first.1 = (bf16[512,1024]{1,0:T(8,128)(2,1)}, bf16[128,256]{1,0:T(8,128)(2,1)S(1)}, bf16[128,256]{1,0:T(8,128)(2,1)S(1)}) custom-call(s32[1,128]{1,0:T(1,128)S(1)} %bitcast.23, bf16[1,128]{1,0:T(2,128)(2,1)S(1)} %bitcast.24, s32[1,128]{1,0:T(1,128)S(1)} %bitcast.26, bf16[128,2048]{1,0:T(8,128)(2,1)} %tokens_hbm.2), custom_call_target="tpu_custom_call" | custom-call | flops 536870912 | bytes 2097152 | tf_op jit(solution)/shard_map/dispatch_first/pallas_call | solution.py:323
  29.7 47.7 %all-to-all-done.1 = bf16[64,8,1024]{2,1,0:T(8,128)(2,1)} async-done(((bf16[64,8,1024]{2,1,0:T(8,128)(2,1)}), bf16[64,8,1024]{2,1,0:T(8,128)(2,1)}, u32[]{:S(2)}, u32[]{:S(2)}) %all-to-all-start.1) | async-done | bytes 1048608 | tf_op jit(solution)/shard_map/all_to_all | solution.py:366
  77.4 10.5 %all-to-all-start = ((bf16[64,8,1024]{2,1,0:T(8,128)(2,1)}), bf16[64,8,1024]{2,1,0:T(8,128)(2,1)}, u32[]{:S(2)}, u32[]{:S(2)}) async-start(bf16[64,8,1024]{2,1,0:T(8,128)(2,1)} %bitcast.29), calls=%async_computation | async-start | bytes 2097152 | tf_op jit(solution)/shard_map/all_to_all | solution.py:366
  87.9 0.0 copy-start.1
  87.9 0.0 copy-done
  87.9 0.0 copy-start.2
  87.9 1.3 copy-done.2
  89.3 1.0 saved.1
  90.3 0.1 pad_add_fusion.at_ref
  90.4 0.0 copy-done.1
  90.4 3.9 %backward.1 = (bf16[8,128,1152]{2,1,0:T(8,128)(2,1)S(1)}, bf16[8,128,1152]{2,1,0:T(8,128)(2,1)S(1)}, bf16[256,128]{1,0:T(8,128)(2,1)S(1)}) custom-call(s32[3]{0:T(128)S(1)} %pad_add_fusion.at_ref, bf16[512,1024]{1,0:T(8,128)(2,1)} %bitcast.12.chunks_ref, bf16[384,2048]{1,0:T(8,128)(2,1)S(1)} %bitcast.20, bf16[256,2048]{1,0:T(8,128)(2,1)S(1)} %bitcast.22, ...), custom_call_target="tpu_custom_call" | custom-call | flops 2147483648 | bytes 12582912 | tf_op jit(solution)/shard_map/backward/pallas_call | solution.py:323
  94.2 3.1 %collective-permute-start = (bf16[8,128,1152]{2,1,0:T(8,128)(2,1)S(1)}, bf16[8,128,1152]{2,1,0:T(8,128)(2,1)S(1)}, u32[]{:S(2)}, u32[]{:S(2)}) collective-permute-start(bf16[8,128,1152]{2,1,0:T(8,128)(2,1)S(1)} %get-tuple-element.29), channel_id=1, source_target_pairs={{0,1},{1,0},{2,3},{3,2},{4,5},{5,4},{6,7},{7,6},{8,9},{9,8},{10,11... | collective-permute-start | bytes 7077896 | tf_op jit(solution)/shard_map/ppermute | solution.py:371
  97.3 4.1 %collective-permute-done.b_ref = bf16[8,128,1152]{2,1,0:T(8,128)(2,1)S(1)} collective-permute-done((bf16[8,128,1152]{2,1,0:T(8,128)(2,1)S(1)}, bf16[8,128,1152]{2,1,0:T(8,128)(2,1)S(1)}, u32[]{:S(2)}, u32[]{:S(2)}) %collective-permute-start) | collective-permute-done | bytes 2359328 | tf_op jit(solution)/shard_map/ppermute | solution.py:371
  101.5 1.4 pairs.1
  102.8 0.0 copy-start.3
  102.8 0.8 copy-done.3
  103.7 4.7 %collective-permute-start.1 = (bf16[2,128,1152]{2,1,0:T(8,128)(2,1)}, bf16[2,128,1152]{2,1,0:T(8,128)(2,1)}, u32[]{:S(2)}, u32[]{:S(2)}) collective-permute-start(bf16[2,128,1152]{2,1,0:T(8,128)(2,1)} %get-tuple-element.30), channel_id=1, source_target_pairs={{0,4},{2,6},{4,0},{6,2},{1,5},{3,7},{5,1},{7,3},{8,12},{10,14},{12... | collective-permute-start | bytes 1769480 | tf_op jit(solution)/shard_map/ppermute | solution.py:371
  108.4 2.2 %collective-permute-start.2 = (bf16[2,128,1152]{2,1,0:T(8,128)(2,1)}, bf16[2,128,1152]{2,1,0:T(8,128)(2,1)}, u32[]{:S(2)}, u32[]{:S(2)}) collective-permute-start(bf16[2,128,1152]{2,1,0:T(8,128)(2,1)} %get-tuple-element.31), channel_id=1, source_target_pairs={{0,2},{2,4},{4,6},{6,0},{1,3},{3,5},{5,7},{7,1},{8,10},{10,12},{12... | collective-permute-start | bytes 1769480 | tf_op jit(solution)/shard_map/ppermute | solution.py:371
  110.6 4.3 %collective-permute-start.3 = (bf16[2,128,1152]{2,1,0:T(8,128)(2,1)}, bf16[2,128,1152]{2,1,0:T(8,128)(2,1)}, u32[]{:S(2)}, u32[]{:S(2)}) collective-permute-start(bf16[2,128,1152]{2,1,0:T(8,128)(2,1)} %get-tuple-element.32), channel_id=1, source_target_pairs={{0,6},{2,0},{4,2},{6,4},{1,7},{3,1},{5,3},{7,5},{8,14},{10,8},{12,... | collective-permute-start | bytes 1769480 | tf_op jit(solution)/shard_map/ppermute | solution.py:371
  114.9 23.5 %all-to-all-done = bf16[64,8,1024]{2,1,0:T(8,128)(2,1)} async-done(((bf16[64,8,1024]{2,1,0:T(8,128)(2,1)}), bf16[64,8,1024]{2,1,0:T(8,128)(2,1)}, u32[]{:S(2)}, u32[]{:S(2)}) %all-to-all-start) | async-done | bytes 1048608 | tf_op jit(solution)/shard_map/all_to_all | solution.py:366
  138.4 0.0 collective-permute-done.1.refs_0_.refs_1_
  138.4 0.0 collective-permute-done.2.refs_1_.refs_2_
  138.4 0.0 collective-permute-done.3.refs_2_.refs_3_
  138.4 4.8 %forward.1 = bf16[64,4,2176]{2,1,0:T(4,128)(2,1)} custom-call(bf16[512,1024]{1,0:T(8,128)(2,1)} %bitcast.4.chunks_hbm, bf16[2048,768]{1,0:T(8,128)(2,1)S(1)} %bitcast.18, bf16[384,2048]{1,0:T(8,128)(2,1)} %bitcast.19, bf16[256,128]{1,0:T(8,128)(2,1)S(1)} %get-tuple-element.27.value_ref, bf16[2,128,1152]{2,1,0:T(8,128)(2,1)} %collective-permute-done.1.refs_0_.refs_1_, ...), custom_call_target="tpu_custom_call" | custom-call | flops 2147483648 | bytes 7340032 | tf_op jit(solution)/shard_map/forward/pallas_call | solution.py:323
  143.2 0.0 copy-start.4
  143.2 0.0 copy-start.8
  143.2 12.2 %all-to-all-start.2 = ((bf16[64,4,2176]{2,1,0:T(4,128)(2,1)}), bf16[64,4,2176]{2,1,0:T(4,128)(2,1)S(1)}, u32[]{:S(2)}, u32[]{:S(2)}) async-start(bf16[64,4,2176]{2,1,0:T(4,128)(2,1)} %forward.1), calls=%async_computation.2 | async-start | bytes 2228224 | tf_op jit(solution)/shard_map/all_to_all | solution.py:462
  155.5 0.0 copy-done.4
  155.5 1.7 sums.1
  157.2 4.8 %collective-permute-start.4 = (bf16[128,1152]{1,0:T(8,128)(2,1)S(1)}, bf16[128,1152]{1,0:T(8,128)(2,1)S(1)}, u32[]{:S(2)}, u32[]{:S(2)}) collective-permute-start(bf16[128,1152]{1,0:T(8,128)(2,1)S(1)} %get-tuple-element.39), channel_id=1, source_target_pairs={{0,8},{8,0},{1,9},{9,1},{2,10},{10,2},{3,11},{11,3},{4,12},{12,4},... | collective-permute-start | bytes 884744 | tf_op jit(solution)/shard_map/ppermute | solution.py:371
  162.0 17.0 %collective-permute-done.4.b_ref = bf16[128,1152]{1,0:T(8,128)(2,1)S(1)} collective-permute-done((bf16[128,1152]{1,0:T(8,128)(2,1)S(1)}, bf16[128,1152]{1,0:T(8,128)(2,1)S(1)}, u32[]{:S(2)}, u32[]{:S(2)}) %collective-permute-start.4) | collective-permute-done | bytes 294944 | tf_op jit(solution)/shard_map/ppermute | solution.py:371
  179.0 0.8 finish.1
  179.8 28.6 %all-to-all-done.2.chunks_ref = bf16[64,4,2176]{2,1,0:T(4,128)(2,1)S(1)} async-done(((bf16[64,4,2176]{2,1,0:T(4,128)(2,1)}), bf16[64,4,2176]{2,1,0:T(4,128)(2,1)S(1)}, u32[]{:S(2)}, u32[]{:S(2)}) %all-to-all-start.2) | async-done | bytes 1114144 | tf_op jit(solution)/shard_map/all_to_all | solution.py:462
  208.4 0.0 copy-done.8
  208.4 1.2 combine.1
Async XLA Ops:
  0.6 26.3 %copy-start.7 = (s32[128,1]{0,1:T(1,128)S(1)}, s32[128,1]{0,1:T(1,128)}, u32[]{:S(2)}) copy-start(s32[128,1]{0,1:T(1,128)} %param.16) | copy-start | bytes 1540
  0.6 26.3 %copy-start.5 = (s32[128,1]{0,1:T(1,128)S(1)}, s32[128,1]{0,1:T(1,128)}, u32[]{:S(2)}) copy-start(s32[128,1]{0,1:T(1,128)} %param.10) | copy-start | bytes 1540
  0.7 26.3 %copy-start.6 = (bf16[128,1]{0,1:T(2,128)(2,1)S(1)}, bf16[128,1]{0,1:T(2,128)(2,1)}, u32[]{:S(2)}) copy-start(bf16[128,1]{0,1:T(2,128)(2,1)} %param.11) | copy-start | bytes 772
  3.3 74.1 %all-to-all-start.1 = ((bf16[64,8,1024]{2,1,0:T(8,128)(2,1)}), bf16[64,8,1024]{2,1,0:T(8,128)(2,1)}, u32[]{:S(2)}, u32[]{:S(2)}) async-start(bf16[64,8,1024]{2,1,0:T(8,128)(2,1)} %bitcast.30), calls=%async_computation.1 | async-start | bytes 2097152 | tf_op jit(solution)/shard_map/all_to_all | solution.py:366
  26.9 61.0 %copy-start = (bf16[1,2048,768]{2,1,0:T(8,128)(2,1)S(1)}, bf16[1,2048,768]{2,1,0:T(8,128)(2,1)}, u32[]{:S(2)}) copy-start(bf16[1,2048,768]{2,1,0:T(8,128)(2,1)} %param.12) | copy-start | bytes 9437188
  77.4 61.0 %all-to-all-start = ((bf16[64,8,1024]{2,1,0:T(8,128)(2,1)}), bf16[64,8,1024]{2,1,0:T(8,128)(2,1)}, u32[]{:S(2)}, u32[]{:S(2)}) async-start(bf16[64,8,1024]{2,1,0:T(8,128)(2,1)} %bitcast.29), calls=%async_computation | async-start | bytes 2097152 | tf_op jit(solution)/shard_map/all_to_all | solution.py:366
  87.9 2.5 %copy-start.1 = (bf16[1,384,2048]{2,1,0:T(8,128)(2,1)S(1)}, bf16[1,384,2048]{2,1,0:T(8,128)(2,1)}, u32[]{:S(2)}) copy-start(bf16[1,384,2048]{2,1,0:T(8,128)(2,1)} %param.13) | copy-start | bytes 4718596
  87.9 1.3 copy-start.2
  94.2 7.2 %collective-permute-start = (bf16[8,128,1152]{2,1,0:T(8,128)(2,1)S(1)}, bf16[8,128,1152]{2,1,0:T(8,128)(2,1)S(1)}, u32[]{:S(2)}, u32[]{:S(2)}) collective-permute-start(bf16[8,128,1152]{2,1,0:T(8,128)(2,1)S(1)} %get-tuple-element.29), channel_id=1, source_target_pairs={{0,1},{1,0},{2,3},{3,2},{4,5},{5,4},{6,7},{7,6},{8,9},{9,8},{10,11... | collective-permute-start | bytes 7077896 | tf_op jit(solution)/shard_map/ppermute | solution.py:371
  102.8 0.8 copy-start.3
  103.7 34.7 %collective-permute-start.1 = (bf16[2,128,1152]{2,1,0:T(8,128)(2,1)}, bf16[2,128,1152]{2,1,0:T(8,128)(2,1)}, u32[]{:S(2)}, u32[]{:S(2)}) collective-permute-start(bf16[2,128,1152]{2,1,0:T(8,128)(2,1)} %get-tuple-element.30), channel_id=1, source_target_pairs={{0,4},{2,6},{4,0},{6,2},{1,5},{3,7},{5,1},{7,3},{8,12},{10,14},{12... | collective-permute-start | bytes 1769480 | tf_op jit(solution)/shard_map/ppermute | solution.py:371
  108.4 30.0 %collective-permute-start.2 = (bf16[2,128,1152]{2,1,0:T(8,128)(2,1)}, bf16[2,128,1152]{2,1,0:T(8,128)(2,1)}, u32[]{:S(2)}, u32[]{:S(2)}) collective-permute-start(bf16[2,128,1152]{2,1,0:T(8,128)(2,1)} %get-tuple-element.31), channel_id=1, source_target_pairs={{0,2},{2,4},{4,6},{6,0},{1,3},{3,5},{5,7},{7,1},{8,10},{10,12},{12... | collective-permute-start | bytes 1769480 | tf_op jit(solution)/shard_map/ppermute | solution.py:371
  110.6 27.8 %collective-permute-start.3 = (bf16[2,128,1152]{2,1,0:T(8,128)(2,1)}, bf16[2,128,1152]{2,1,0:T(8,128)(2,1)}, u32[]{:S(2)}, u32[]{:S(2)}) collective-permute-start(bf16[2,128,1152]{2,1,0:T(8,128)(2,1)} %get-tuple-element.32), channel_id=1, source_target_pairs={{0,6},{2,0},{4,2},{6,4},{1,7},{3,1},{5,3},{7,5},{8,14},{10,8},{12,... | collective-permute-start | bytes 1769480 | tf_op jit(solution)/shard_map/ppermute | solution.py:371
  143.2 12.2 %copy-start.4 = (bf16[2,128,1152]{2,1,0:T(8,128)(2,1)S(1)}, bf16[2,128,1152]{2,1,0:T(8,128)(2,1)}, u32[]{:S(2)}) copy-start(bf16[2,128,1152]{2,1,0:T(8,128)(2,1)} %copy-done.3) | copy-start | bytes 1769476
  143.2 65.1 %copy-start.8 = (bf16[128,1]{0,1:T(2,128)(2,1)S(1)}, bf16[128,1]{0,1:T(2,128)(2,1)}, u32[]{:S(2)}) copy-start(bf16[128,1]{0,1:T(2,128)(2,1)} %param.17) | copy-start | bytes 772
  143.2 65.1 %all-to-all-start.2 = ((bf16[64,4,2176]{2,1,0:T(4,128)(2,1)}), bf16[64,4,2176]{2,1,0:T(4,128)(2,1)S(1)}, u32[]{:S(2)}, u32[]{:S(2)}) async-start(bf16[64,4,2176]{2,1,0:T(4,128)(2,1)} %forward.1), calls=%async_computation.2 | async-start | bytes 2228224 | tf_op jit(solution)/shard_map/all_to_all | solution.py:462
  157.2 21.8 %collective-permute-start.4 = (bf16[128,1152]{1,0:T(8,128)(2,1)S(1)}, bf16[128,1152]{1,0:T(8,128)(2,1)S(1)}, u32[]{:S(2)}, u32[]{:S(2)}) collective-permute-start(bf16[128,1152]{1,0:T(8,128)(2,1)S(1)} %get-tuple-element.39), channel_id=1, source_target_pairs={{0,8},{8,0},{1,9},{9,1},{2,10},{10,2},{3,11},{11,3},{4,12},{12,4},... | collective-permute-start | bytes 884744 | tf_op jit(solution)/shard_map/ppermute | solution.py:371
